TPU v7x, 32 devices: a whole 2x2x4 slice. The times are simulated.
32 devices in a mesh: groups: 2 (over y), mp: 4 (over x, core), hidden: 4 (over z).
Axes of the slice: x: 2, y: 2, z: 4, core: 2. Of those that a mesh axis runs over, the one named last changes fastest.
Arguments:
- inputs: bfloat16 [2048, 8192], P(('groups', 'hidden'), 'mp'), parts along dimension 0, as said below
- out_grad: bfloat16 [2048, 16384], P(('groups', 'mp'), 'hidden'), parts along dimension 0, as said below
- weight: float32 [8192, 16384], P('mp', 'hidden'), may hold values from -0.0625 to 0.0625
- noise: bfloat16 [2, 16384, 16384], P(None, ('groups', 'mp'), 'hidden'), parts along dimension 1, may hold values from -6 to 6
Outputs:
- outputs: bfloat16 [2048, 16384], P(('groups', 'mp'), 'hidden'), parts along dimension 0
- in_grad: bfloat16 [2048, 8192], P(('groups', 'hidden'), 'mp'), parts along dimension 0
- update: float32 [8192, 32768], P('mp', ('groups', 'hidden')), parts along dimension 1
There are 2 independent parts, one for each index of `groups`. A program takes and returns all parts, laid end to end along the dimension named above; an argument that names none is the same for every part. Nothing has to cross between parts.
Inputs may be any that keep to these rules, and one draw needn't show every extreme that they name: `inputs`: Real-valued activations whose rows and columns carry independent scales. `out_grad`: Real-valued gradients whose rows and columns carry independent scales; examples differ in overall size.
All inputs are finite; a program needn't handle non-finite values.
Results may differ from a plain program's by a relative error of at most 0.0049.
Values may be sent and summed in bfloat16 or wider, within the bound.
No kernel may reach another device: no remote copies, remote signals or barrier semaphores. Data moves between devices by JAX's collectives and lax.ppermute only.
A program may use at most 256 MiB of HBM per device.

v0:
```python
import math

import jax
import jax.numpy as jnp
from jax import lax
from jax.sharding import PartitionSpec as P

D = 8192
FF = 16384
SEQ = 64
EXAMPLES = 16


def shards(inputs, out_grad, weight, noise):
    weight_half = weight.astype(jnp.bfloat16)
    feature_rows = lax.all_gather(inputs, "hidden", axis=0, tiled=True)
    unit_rows = lax.all_gather(out_grad, "mp", axis=0, tiled=True)
    picked = feature_rows
    outputs = lax.psum_scatter(
        jnp.dot(picked, weight_half, preferred_element_type=jnp.float32),
        "mp",
        scatter_dimension=0,
        tiled=True,
    ).astype(jnp.bfloat16)
    picked = unit_rows
    in_grad = lax.psum_scatter(
        lax.dot_general(
            picked, weight_half, (((1,), (1,)), ((), ())), preferred_element_type=jnp.float32
        ),
        "hidden",
        scatter_dimension=0,
        tiled=True,
    ).astype(jnp.bfloat16)
    feature_blocks = feature_rows.reshape(EXAMPLES, SEQ, feature_rows.shape[1])
    unit_blocks = unit_rows.reshape(EXAMPLES, SEQ, unit_rows.shape[1])
    feature_gram = jnp.einsum(
        "bsd,btd->bst", feature_blocks, feature_blocks, preferred_element_type=jnp.float32
    )
    unit_gram = jnp.einsum(
        "bsd,btd->bst", unit_blocks, unit_blocks, preferred_element_type=jnp.float32
    )
    feature_gram = lax.psum(feature_gram.astype(jnp.bfloat16), "mp").astype(jnp.float32)
    unit_gram = lax.psum(unit_gram.astype(jnp.bfloat16), "hidden").astype(jnp.float32)
    squares = jnp.sum(feature_gram * unit_gram, axis=(1, 2))
    clip_norm = math.sqrt(SEQ * D * FF)
    factor = jnp.minimum(1.0, clip_norm / jnp.sqrt(squares + 1e-06))
    token_factor = jnp.repeat(factor, SEQ)[:, None]
    scaled_grad = (unit_rows.astype(jnp.float32) * token_factor).astype(jnp.bfloat16)
    weight_grad = lax.dot_general(
        feature_rows, scaled_grad, (((0,), (0,)), ((), ())), preferred_element_type=jnp.float32
    )
    band_noise = noise[0].astype(jnp.float32) - 0.6 * noise[1].astype(jnp.float32)
    update = (weight_grad * (math.sqrt(D * FF) / clip_norm) + 4.0 * band_noise) / EXAMPLES
    return (outputs, in_grad, update)


def solution(mesh):
    in_specs = (
        P(("groups", "hidden"), "mp"),
        P(("groups", "mp"), "hidden"),
        P("mp", "hidden"),
        P(None, ("groups", "mp"), "hidden"),
    )
    out_specs = (
        P(("groups", "mp"), "hidden"),
        P(("groups", "hidden"), "mp"),
        P("mp", ("groups", "hidden")),
    )
    return jax.shard_map(shards, mesh=mesh, in_specs=in_specs, out_specs=out_specs, check_vma=False)
```

profile of v0, /device:TPU:0, one launch (start us, length us, event | category | flops | bytes accessed | tf_op | source)
XLA Modules:
  0.0 511.0 jit_solution(1098056114129314794)
XLA Ops:
  7.2 0.0 all-gather.3.cloned.1.call-start
  7.2 0.7 all-gather.3.cloned.1.call-update
  7.9 0.0 all-gather.5.cloned.1.call-start
  7.9 0.7 all-gather.5.cloned.1.call-update
  8.6 0.0 all-reduce.3.cloned.1.call-start
  8.7 84.4 %all-gather.3.cloned.1.call-done = bf16[1024,2048]{1,0:T(8,128)(2,1)} async-done(((bf16[256,2048]{1,0:T(8,128)(2,1)}), bf16[1024,2048]{1,0:T(8,128)(2,1)}) %all-gather.3.cloned.1.call-update) | async-done | bytes 4194320 | tf_op jit(solution)/shard_map/all_gather | solution.py:16
  93.1 5.4 %convolution_convert_fusion.1 = bf16[16,64,64]{2,1,0:T(8,128)(2,1)} fusion(bf16[16,64,2048]{2,1,0:T(8,128)(2,1)} %bitcast.16), kind=kOutput, calls=%fused_computation.9 | convolution fusion | flops 268500992 | bytes 4325376 | tf_op jit(solution)/shard_map/bsd,btd->bst/dot_general | solution.py:36
  98.5 0.0 all-reduce.3.cloned.1.call-update
  98.5 0.0 all-reduce.5.cloned.1.call-start
  98.5 52.9 %all-gather.5.cloned.1.call-done = bf16[1024,4096]{1,0:T(8,128)(2,1)} async-done(((bf16[256,4096]{1,0:T(8,128)(2,1)}), bf16[1024,4096]{1,0:T(8,128)(2,1)}) %all-gather.5.cloned.1.call-update) | async-done | bytes 8388624 | tf_op jit(solution)/shard_map/all_gather | solution.py:17
  151.5 8.8 %convolution_convert_fusion = bf16[16,64,64]{2,1,0:T(8,128)(2,1)} fusion(bf16[16,64,4096]{2,1,0:T(8,128)(2,1)} %bitcast.15), kind=kOutput, calls=%fused_computation.8 | convolution fusion | flops 536936448 | bytes 8519680 | tf_op jit(solution)/shard_map/bsd,btd->bst/dot_general | solution.py:39
  160.3 0.0 all-reduce.5.cloned.1.call-update
  160.3 0.0 reduce-scatter.5.cloned.1.call-start
  160.3 25.4 %fusion.2 = f32[1024,2048]{1,0:T(8,128)} fusion(bf16[1024,4096]{1,0:T(8,128)(2,1)} %all-gather.5.cloned.1.call-done, f32[2048,4096]{1,0:T(8,128)} %param.6), kind=kOutput, calls=%fused_computation.4 | convolution fusion | flops 17188257792 | bytes 50331648 | tf_op jit(solution)/shard_map/dot_general | solution.py:27
  185.7 0.0 reduce-scatter.5.cloned.1.call-update
  185.7 0.0 reduce-scatter.3.cloned.1.call-start
  185.8 25.1 %fusion.4 = f32[1024,4096]{1,0:T(8,128)} fusion(bf16[1024,2048]{1,0:T(8,128)(2,1)} %all-gather.3.cloned.1.call-done, f32[2048,4096]{1,0:T(8,128)} %param.6), kind=kOutput, calls=%fused_computation.6 | convolution fusion | flops 17188257792 | bytes 54525952 | tf_op jit(solution)/shard_map/dot_general | solution.py:20
  210.8 0.0 reduce-scatter.3.cloned.1.call-update
  210.9 23.5 %fusion.6 = (bf16[1,2048,4096]{2,1,0:T(8,128)(2,1)}, bf16[1,2048,4096]{2,1,0:T(8,128)(2,1)}) fusion(bf16[2,2048,4096]{2,1,0:T(8,128)(2,1)} %param.7), kind=kLoop, calls=%fused_computation.12 | loop fusion | bytes 67108864 | tf_op jit(solution)/shard_map/slice | solution.py:52
  234.3 22.6 %copy.10 = bf16[1,2048,4096]{1,2,0:T(8,128)(2,1)} copy(bf16[1,2048,4096]{2,1,0:T(8,128)(2,1)} %get-tuple-element.6) | data formatting | bytes 33554432
  256.9 22.5 %copy.11 = bf16[1,2048,4096]{1,2,0:T(8,128)(2,1)} copy(bf16[1,2048,4096]{2,1,0:T(8,128)(2,1)} %get-tuple-element.7) | data formatting | bytes 33554432
  279.3 0.0 all-reduce.3.cloned.1.call-done
  279.3 0.0 all-reduce.5.cloned.1.call-done
  279.3 1.2 multiply_reduce_fusion
  280.6 0.1 broadcast_in_dim.3
  280.7 0.1 mul.39
  280.7 36.6 %fusion = f32[2048,4096]{0,1:T(8,128)} fusion(bf16[1,2048,4096]{1,2,0:T(8,128)(2,1)} %copy.11, bf16[1,2048,4096]{1,2,0:T(8,128)(2,1)} %copy.10, bf16[1024,2048]{1,0:T(8,128)(2,1)} %all-gather.3.cloned.1.call-done, bf16[1024,4096]{1,0:T(8,128)(2,1)} %all-gather.5.cloned.1.call-done, f32[1024]{0:T(1024)S(1)} %mul.39), kind=kOutput, calls=%fused_computation.1 | convolution fusion | flops 17259560960 | bytes 79695872 | tf_op jit(solution)/shard_map/dot_general | solution.py:49
  317.3 31.1 %copy.9 = f32[2048,4096]{1,0:T(8,128)} copy(f32[2048,4096]{0,1:T(8,128)} %fusion) | data formatting | bytes 67108864
  348.5 22.6 %reduce-scatter.5.cloned.1.call-done = f32[256,2048]{1,0:T(8,128)} async-done(((f32[1024,2048]{1,0:T(8,128)}), f32[256,2048]{1,0:T(8,128)}) %reduce-scatter.5.cloned.1.call-update) | async-done | bytes 2097168 | tf_op jit(solution)/shard_map/reduce_scatter | solution.py:26
  371.0 2.7 convert_element_type.37
  373.7 126.6 %reduce-scatter.3.cloned.1.call-done = f32[256,4096]{1,0:T(8,128)} async-done(((f32[1024,4096]{1,0:T(8,128)}), f32[256,4096]{1,0:T(8,128)}) %reduce-scatter.3.cloned.1.call-update) | async-done | bytes 4194320 | tf_op jit(solution)/shard_map/reduce_scatter | solution.py:19
  500.3 3.8 convert_element_type.36
  (1 shorter events, 0.0 us)
Async XLA Ops:
  7.2 85.9 %all-gather.3.cloned.1.call-start = ((), (), s32[]{:S(2)}) async-start(), calls=%async_computation.2 | async-start | bytes 5242880 | tf_op jit(solution)/shard_map/all_gather | solution.py:16
  7.9 143.6 %all-gather.5.cloned.1.call-start = ((), (), s32[]{:S(2)}) async-start(), calls=%async_computation.4 | async-start | bytes 10485760 | tf_op jit(solution)/shard_map/all_gather | solution.py:17
  8.6 270.7 %all-reduce.3.cloned.1.call-start = ((), (), s32[]{:S(2)}) async-start(), calls=%async_computation.6 | async-start | bytes 524288 | tf_op jit(solution)/shard_map/psum | solution.py:42
  98.5 180.8 %all-reduce.5.cloned.1.call-start = ((), (), s32[]{:S(2)}) async-start(), calls=%async_computation.7 | async-start | bytes 524288 | tf_op jit(solution)/shard_map/psum | solution.py:43
  160.3 210.7 %reduce-scatter.5.cloned.1.call-start = ((), (), s32[]{:S(2)}) async-start(), calls=%async_computation.5 | async-start | bytes 10485760 | tf_op jit(solution)/shard_map/reduce_scatter | solution.py:26
  185.7 314.6 %reduce-scatter.3.cloned.1.call-start = ((), (), s32[]{:S(2)}) async-start(), calls=%async_computation.3 | async-start | bytes 20971520 | tf_op jit(solution)/shard_map/reduce_scatter | solution.py:19
Sparse Core Ops, SparseCore 0:
  9.6 83.4 all-gather.2
  94.6 56.8 all-gather.4
  154.4 31.9 all-reduce.2
  189.3 35.2 all-reduce.4
  226.8 144.1 reduce-scatter.4
  373.5 126.8 reduce-scatter.2
where the time goes:
time: 513 us; the launch traced here: 511 us
  waiting for transfers between devices  288 us (56%)
  matrix products  101 us (20%)
  local copies, waits for them, and re-layouts  99.8 us (19%)
  between operations  14.1 us (3%)
  other arithmetic  7.75 us (2%)
    reduce_scatter x1, waiting for transfers between devices, shards(): lax.psum_scatter(jnp.dot(picked, weight_half, preferred_element_type=jnp....  127 us
    all_gather x1, waiting for transfers between devices, shards(): feature_rows = lax.all_gather(inputs, 'hidden', axis=0, tiled=True)  84.4 us
    unnamed x3, local copies, waits for them, and re-layouts  76.2 us
    all_gather x1, waiting for transfers between devices, shards(): unit_rows = lax.all_gather(out_grad, 'mp', axis=0, tiled=True)  52.9 us
    dot_general x1, matrix products, shards(): lax.dot_general(feature_rows, scaled_grad, (((0,), (0,)), ((), ())), pref...  36.6 us
    dot_general x1, matrix products, shards(): lax.dot_general(picked, weight_half, (((1,), (1,)), ((), ())), preferred_...  25.4 us
    dot_general x1, matrix products, shards(): jnp.dot(picked, weight_half, preferred_element_type=jnp.float32)  25.1 us
    slice x1, local copies, waits for them, and re-layouts, shards(): noise[0].astype(jnp.float32) - 0.6 * noise[1].astype(jnp.float32)  23.5 us
  transfers between devices with their start and end apart: 6, of which 4 were waited for; matrix products, arithmetic and copies ran while one was open for 40% of the time, Pallas kernels for 0%

commit v1 on v0

v1 whole, which is shorter than its diff:
```python
import math

import jax
import jax.numpy as jnp
from jax import lax
from jax.experimental import pallas as pl
from jax.experimental.pallas import tpu as pltpu
from jax.sharding import PartitionSpec as P

SEQ = 64
NOISE_BAND = 0.6
NOISE_SCALE = 4.0
VMEM = 60 * 1024 * 1024
F32 = jnp.float32
BF16 = jnp.bfloat16
ANY = pl.BlockSpec(memory_space=pl.ANY)


def params(dims):
    return pltpu.CompilerParams(
        vmem_limit_bytes=VMEM, dimension_semantics=("arbitrary",) * dims
    )


def whole(shape):
    return pl.BlockSpec(shape, lambda *_: (0,) * len(shape))


def pair_kernel(transposed, place, finish, count, merged, extra, at, *refs):
    pieces, w = refs[:count], refs[count]
    merges = refs[count + 1 : count + 1 + merged]
    *products, full, rows = refs[count + 1 + merged + extra :]
    r = rows.shape[0] // 2

    @pl.when(pl.program_id(0) == 0)
    def _():
        for cond, slot, spot, piece in place(at, pieces):

            def put(slot=slot, spot=spot, piece=piece):
                rows[pl.ds(pl.multiple_of(slot * r, r), r), :] = piece[...]
                full[spot] = piece[...]

            if cond is None:
                put()
            else:
                pl.when(cond)(put)

    tile = w[...]
    if tile.dtype != BF16:
        tile = tile.astype(BF16)
        products[-1][...] = tile
    dims = (((1,), (1 if transposed else 0,)), ((), ()))
    total = lax.dot_general(rows[...], tile, dims, preferred_element_type=F32)
    finish(at, total[:r], total[r:], merges, products)


def pair_matmul(at, pair, pieces, w, place, transposed, finish, outs, merges, before, after, name):
    r, depth = pieces[0].shape
    width = w.shape[0] if transposed else w.shape[1]
    cast = w.dtype != BF16
    tile = min(256 if cast else 512 if transposed else 1024, width)
    w_spec = (
        pl.BlockSpec((tile, depth), lambda i, at: (i, 0))
        if transposed
        else pl.BlockSpec((depth, tile), lambda i, at: (0, i))
    )
    extra = ([] if before is None else [before]) + list(after)
    count = len(pieces)
    product = pl.BlockSpec((r, tile), lambda i, at: (0, i))
    kernel = lambda *refs: pair_kernel(
        transposed, place, finish, count, len(merges), len(extra), *refs
    )
    return pl.pallas_call(
        kernel,
        grid_spec=pltpu.PrefetchScalarGridSpec(
            num_scalar_prefetch=1,
            grid=(width // tile,),
            in_specs=[whole((r, depth))] * count
            + [w_spec]
            + [product] * len(merges)
            + [ANY] * len(extra),
            out_specs=[product] * outs
            + [w_spec] * cast
            + [pl.BlockSpec((2, r, depth), lambda i, at: (at[pair], 0, 0))],
            scratch_shapes=[pltpu.VMEM((2 * r, depth), BF16)],
        ),
        out_shape=[jax.ShapeDtypeStruct((r, width), BF16)] * outs
        + [jax.ShapeDtypeStruct(w.shape, BF16)] * cast
        + [jax.ShapeDtypeStruct((4, r, depth), BF16)],
        input_output_aliases={}
        if before is None
        else {count + 2 + len(merges): outs + cast},
        compiler_params=params(1),
        cost_estimate=pl.CostEstimate(
            flops=4 * r * depth * width,
            bytes_accessed=(6 if cast else 2) * depth * width + 4 * r * (width + depth),
            transcendentals=0,
        ),
        name=name,
    )(at, *pieces, w, *merges, *extra)


def update_kernel(gain, count, factor, x, g, noise, out, scaled):
    @pl.when(pl.program_id(0) == 0)
    def _():
        for t in range(0, scaled.shape[0], SEQ):
            span = pl.ds(t, SEQ)
            scaled[span, :] = (g[span, :].astype(F32) * factor[span, :]).astype(BF16)

    step = min(1024, out.shape[1])
    for j in range(0, out.shape[1], step):
        span = pl.ds(j, step)
        grad = lax.dot_general(
            x[...], scaled[:, span], (((0,), (0,)), ((), ())), preferred_element_type=F32
        )
        band = noise[0, :, span].astype(F32) - NOISE_BAND * noise[1, :, span].astype(F32)
        out[:, span] = (grad * gain + NOISE_SCALE * band) * (1.0 / count)


def make_update(x, g, factor, noise, gain, count, part=0, parts=1, before=None, after=()):
    tokens, depth = x.shape
    whole_width = g.shape[1]
    width = whole_width // parts
    tile = min(256, depth)
    extra = ([] if before is None else [before]) + list(after)

    def kernel(factor, x, g, noise, *refs):
        update_kernel(gain, count, factor, x, g, noise, *refs[len(extra) :])

    return pl.pallas_call(
        kernel,
        grid=(depth // tile,),
        in_specs=[
            whole((tokens, 1)),
            pl.BlockSpec((tokens, tile), lambda i: (0, i)),
            pl.BlockSpec((tokens, width), lambda i: (0, part)),
            pl.BlockSpec((2, tile, width), lambda i: (0, i, part)),
        ]
        + [ANY] * len(extra),
        out_specs=pl.BlockSpec((tile, width), lambda i: (i, part)),
        out_shape=jax.ShapeDtypeStruct((depth, whole_width), F32),
        scratch_shapes=[pltpu.VMEM((tokens, width), BF16)],
        input_output_aliases={} if before is None else {4: 0},
        compiler_params=params(1),
        cost_estimate=pl.CostEstimate(
            flops=2 * tokens * depth * width,
            bytes_accessed=(8 * depth * width + 2 * tokens * (depth + width)),
            transcendentals=0,
        ),
        name="update",
    )(factor, x, g, noise, *extra)


OUTER = [(0, 1), (1, 0), (2, 3), (3, 2)]
MIDDLE = [(1, 2), (2, 1)]
INWARD = [(0, 1), (3, 2)]
OUTWARD = [(1, 0), (2, 3)]


def along(value, pairs):
    return lax.ppermute(value, "hidden", pairs)


def swap(value, bit):
    return lax.ppermute(value, "mp", [(i, i ^ bit) for i in range(4)])


def gram(rows):
    blocks = rows.reshape(-1, SEQ, rows.shape[1])
    return jnp.einsum("bsd,btd->bst", blocks, blocks, preferred_element_type=F32)


def gram_pairs(rows):
    blocks = gram(rows).astype(BF16)
    return jnp.concatenate([blocks[0::2], blocks[1::2]], axis=2)


def factor_kernel(clip, pairs, at, f, u, got, out):
    h, m = at[4], at[5]
    blocks = 2 * u.shape[0] // (2 * pairs)
    r = out.shape[0] // blocks
    half = f.shape[0]
    lane = lax.broadcasted_iota(jnp.int32, (1, 2 * SEQ), 1)

    def sums(block):
        j, i = block ^ h, block ^ m
        for p in range(pairs):
            unit = u[i * pairs + p].astype(F32) + got[half + i * pairs + p].astype(F32)
            spot = j * pairs + p
            mine = f[jnp.minimum(spot, half - 1)].astype(F32)
            feature = jnp.where(spot < half, mine, got[jnp.maximum(spot - half, 0)].astype(F32))
            yield p, jnp.sum(feature * unit, axis=0, keepdims=True)

    for block in range(blocks):
        for p, total in sums(block):
            for side in range(2):
                square = jnp.sum(
                    jnp.where(lane // SEQ == side, total, 0.0), axis=1, keepdims=True
                )
                factor = jnp.minimum(1.0, clip / jnp.sqrt(square + 1e-06))
                start = block * r + (2 * p + side) * SEQ
                out[start : start + SEQ, :] = jnp.broadcast_to(factor, (SEQ, 1))


def make_factor(at, f, u, got, clip, pairs, tokens):
    return pl.pallas_call(
        lambda *refs: factor_kernel(clip, pairs, *refs),
        in_specs=[pl.BlockSpec(memory_space=pltpu.SMEM)]
        + [pl.BlockSpec(memory_space=pltpu.VMEM)] * 3,
        out_specs=pl.BlockSpec(memory_space=pltpu.VMEM),
        out_shape=jax.ShapeDtypeStruct((tokens, 1), F32),
        name="clip_factor",
    )(at, f, u, got)


def plus(a, b):
    return (a.astype(F32) + b.astype(F32)).astype(BF16)


def pipelined(inputs, out_grad, weight, noise):
    n = 4
    m, h = lax.axis_index("mp"), lax.axis_index("hidden")
    at = jnp.stack([h // 2, 1 - h // 2, m // 2, 1 - m // 2, h, m]).astype(jnp.int32)
    d_all, ff_all = inputs.shape[1] * n, out_grad.shape[1] * n
    tokens = inputs.shape[0] * n
    examples = inputs.shape[0] // SEQ
    clip = math.sqrt(SEQ * d_all * ff_all)

    hold = lax.optimization_barrier
    g_side = swap(out_grad, 1)
    g_far = swap(out_grad, 2)
    x_side = along(inputs, OUTER)
    x_mid = along(inputs, MIDDLE)
    features, units = gram_pairs(inputs), gram_pairs(out_grad)
    pairs = features.shape[0]
    grams = swap(jnp.concatenate([features, units]), 1)
    weight, g_side, features, units = hold((weight, g_side, features, units))

    def out_grad_rows(at, pieces):
        h, core, half = at[4], at[5] & 1, at[2]

        def slot(block_core, near):
            return jnp.where(near, (block_core ^ h ^ 1) & 1, block_core ^ at[4] // 2 ^ 1)

        near = half == at[0]
        return [
            (None, slot(core, near), core, pieces[0]),
            (None, slot(1 - core, near), 1 - core, pieces[1]),
        ]

    def far_out_grad_rows(at, pieces):
        h, core, half = at[4], at[5] & 1, at[3]
        near = half == at[0]

        def slot(block_core):
            return jnp.where(near, (block_core ^ h ^ 1) & 1, block_core ^ at[4] // 2 ^ 1)

        return [
            (None, slot(core), core, pieces[0]),
            (None, slot(1 - core), 1 - core, pieces[1]),
        ]

    def near_rows(at, pieces):
        odd, core = at[4] & 1, at[5] & 1
        return [
            (None, odd ^ core, odd, pieces[0]),
            (None, 1 - (odd ^ core), 1 - odd, pieces[1]),
        ]

    def far_rows(at, pieces):
        up, core = at[0], at[5] & 1
        inner = (at[4] == 1) | (at[4] == 2)
        outer = jnp.logical_not(inner)
        return [
            (inner, up ^ core, up, pieces[0]),
            (outer, up ^ core, up, pieces[1]),
            (inner, 1 - (up ^ core), 1 - up, pieces[2]),
            (outer, 1 - (up ^ core), 1 - up, pieces[3]),
        ]

    def plainly(at, first, second, merges, products):
        products[0][...] = first.astype(BF16)
        products[1][...] = second.astype(BF16)

    def in_grad_order(at, first, second, merges, products):
        near_last = at[2] == at[0]

        @pl.when(near_last)
        def _():
            products[0][...], products[1][...] = first.astype(BF16), second.astype(BF16)
            products[2][...], products[3][...] = merges[0][...], merges[1][...]

        @pl.when(jnp.logical_not(near_last))
        def _():
            products[0][...], products[1][...] = merges[0][...], merges[1][...]
            products[2][...], products[3][...] = first.astype(BF16), second.astype(BF16)

    def outputs_order(at, first, second, merges, products):
        near = (merges[0][...].astype(F32) + merges[1][...].astype(F32)).astype(BF16)
        near_mine = at[2] == at[0]
        products[2][...] = second.astype(BF16)

        @pl.when(near_mine)
        def _():
            products[0][...], products[1][...] = first.astype(BF16), near

        @pl.when(jnp.logical_not(near_mine))
        def _():
            products[0][...], products[1][...] = near, first.astype(BF16)

    qa0, qa1, w, g_half = pair_matmul(
        at, 2, [out_grad, g_side], weight, out_grad_rows, True, plainly, 2, [], None, [], "in_grad_here"
    )
    x_side, x_mid, w, grams = hold((x_side, x_mid, w, grams))
    features = plus(features, grams[:pairs])
    units = jnp.concatenate([units, grams[pairs:]])
    grams = swap(jnp.concatenate([features, units]), 2)
    x_mid2 = along(x_side, MIDDLE)
    x_out = along(x_mid, OUTWARD)
    pa0, pa1, x_half = pair_matmul(
        at, 0, [inputs, x_side], w, near_rows, False, plainly, 2, [], None, [], "outputs_near"
    )
    g_far, pa1, x_mid2, x_out, grams = hold((g_far, pa1, x_mid2, x_out, grams))
    g_far_side = swap(g_far, 1)
    x_out2 = along(x_mid2, OUTWARD)
    pa1 = swap(pa1, 1)
    features = plus(features, grams[:pairs])
    units = jnp.concatenate([units, grams[pairs:]])
    grams = along(jnp.concatenate([features, units]), OUTER)
    first, second, beside, own, g_all = pair_matmul(
        at, 3, [g_far, g_far_side], w, far_out_grad_rows, True, in_grad_order, 4, [qa0, qa1], g_half, [pa0], "in_grad_there"
    )
    grams, first, x_out2 = hold((grams, first, x_out2))
    r1a = along(first, INWARD)
    features = jnp.concatenate([features, grams[:pairs]])
    units = plus(units, grams[pairs:])
    grams = along(jnp.concatenate([features, units]), [(i, i ^ 2) for i in range(n)])
    other, mine, pb1, x_all = pair_matmul(
        at, 1, [x_mid, x_out, x_mid2, x_out2], w, far_rows, False, outputs_order, 3, [pa0, pa1], x_half, [first], "outputs_far"
    )
    same = m // 2 == h // 2
    r1a, pb1 = hold((r1a, pb1))
    pb1 = swap(pb1, 1)
    r2a = along(plus(first, r1a), MIDDLE)
    r1b = along(second, INWARD)
    other = plus(other, jnp.where(same, pb1, 0))
    theirs = swap(other, 2)

    grams, other = hold((grams, other))
    factor = make_factor(at, features, units, grams, clip, pairs, tokens)
    x_all, g_all = x_all.reshape(tokens, -1), g_all.reshape(tokens, -1)
    gain = math.sqrt(d_all * ff_all) / clip
    update = make_update(x_all, g_all, factor, noise, gain, tokens // SEQ, 0, 2, None, [other])
    r2a, r1b, update = hold((r2a, r1b, update))
    r3 = along(plus(beside, r2a), OUTER)
    r2b = along(plus(second, r1b), MIDDLE)
    update = make_update(x_all, g_all, factor, noise, gain, tokens // SEQ, 1, 2, update)
    r3, r2b, theirs, update = hold((r3, r2b, theirs, update))
    in_grad = (own.astype(F32) + r3.astype(F32) + r2b.astype(F32)).astype(BF16)
    mine = mine.astype(F32) + jnp.where(same, 0, pb1).astype(F32)
    outputs = (mine + theirs.astype(F32)).astype(BF16)
    return outputs, in_grad, update


def plain(tokens, d_all, ff_all, inputs, out_grad, weight, noise):
    w = weight.astype(BF16)
    x = lax.all_gather(inputs, "hidden", axis=0, tiled=True)
    g = lax.all_gather(out_grad, "mp", axis=0, tiled=True)
    clip = math.sqrt(SEQ * d_all * ff_all)
    outputs = lax.psum_scatter(
        jnp.dot(x, w, preferred_element_type=F32), "mp", scatter_dimension=0, tiled=True
    )
    in_grad = lax.psum_scatter(
        lax.dot_general(g, w, (((1,), (1,)), ((), ())), preferred_element_type=F32),
        "hidden",
        scatter_dimension=0,
        tiled=True,
    )
    grams = lax.psum(gram(x), "mp") * lax.psum(gram(g), "hidden")
    factor = jnp.minimum(1.0, clip / jnp.sqrt(jnp.sum(grams, axis=(1, 2)) + 1e-06))
    update = make_update(
        x,
        g,
        jnp.repeat(factor, SEQ)[:, None],
        noise,
        math.sqrt(d_all * ff_all) / clip,
        tokens // SEQ,
    )
    return outputs.astype(BF16), in_grad.astype(BF16), update


def solution(mesh):
    mp, hidden = mesh.shape["mp"], mesh.shape["hidden"]

    def shards(inputs, out_grad, weight, noise):
        if mp == hidden == 4 and inputs.shape[0] % (2 * SEQ) == 0:
            return pipelined(inputs, out_grad, weight, noise)
        return plain(
            inputs.shape[0] * hidden,
            inputs.shape[1] * mp,
            out_grad.shape[1] * hidden,
            inputs,
            out_grad,
            weight,
            noise,
        )

    in_specs = (
        P(("groups", "hidden"), "mp"),
        P(("groups", "mp"), "hidden"),
        P("mp", "hidden"),
        P(None, ("groups", "mp"), "hidden"),
    )
    out_specs = (
        P(("groups", "mp"), "hidden"),
        P(("groups", "hidden"), "mp"),
        P("mp", ("groups", "hidden")),
    )
    return jax.shard_map(shards, mesh=mesh, in_specs=in_specs, out_specs=out_specs, check_vma=False)
```

time: 513 us -> 204 us (0.40)
  waiting for transfers between devices: 288 us -> 24.8 us
  Pallas kernels: 0 us -> 120 us
  matrix products: 101 us -> 3.41 us
  local copies, waits for them, and re-layouts: 99.8 us -> 4.27 us
  starting transfers between devices: 0.24 us -> 30.9 us
  between operations: 14.1 us -> 0.92 us
  other arithmetic: 7.75 us -> 19 us
    reduce_scatter x2 -> x0, waiting for transfers between devices: 149 us -> none  [the longest x1 127 us: shards(): lax.psum_scatter(jnp.dot(picked, weight_half, preferred_element_type=jnp....]
    all_gather x2 -> x0, waiting for transfers between devices: 137 us -> none  [the longest x1 84.4 us: shards(): feature_rows = lax.all_gather(inputs, 'hidden', axis=0, tiled=True)]
    pallas_call x0 -> x7, Pallas kernels: none -> 120 us  [the longest x4 75.6 us: pair_matmul(): pl.pallas_call(kernel, grid_spec=pltpu.PrefetchScalarGridSpec(num_scalar_...]
    dot_general x5 -> x2, matrix products: 101 us -> 3.41 us  [gram(): jnp.einsum('bsd,btd->bst', blocks, blocks, preferred_element_type=F32)]
    unnamed x3 -> x26, local copies, waits for them, and re-layouts: 76.2 us -> 2.69 us
    ppermute x0 -> x20, starting transfers between devices: none -> 30.9 us  [the longest x12 27.7 us: along(): return lax.ppermute(value, 'hidden', pairs)]
    ppermute x0 -> x20, waiting for transfers between devices: none -> 24.8 us  [the longest x12 24.3 us: along(): return lax.ppermute(value, 'hidden', pairs)]
    slice x1 -> x5, local copies, waits for them, and re-layouts: 23.5 us -> 0.93 us  [the longest x1 0.91 us: pipelined(): features = jnp.concatenate([features, grams[:pairs]])]
  transfers between devices with their start and end apart: 6 -> 20, of which waited for: 4 -> 5; matrix products, arithmetic and copies ran while one was open for 40% -> 8% of each run, Pallas kernels for 0% -> 59%
where the time goes in v1:
time: 204 us; the launch traced here: 203 us
  Pallas kernels  120 us (59%)
  starting transfers between devices  30.9 us (15%)
  waiting for transfers between devices  24.8 us (12%)
  other arithmetic  19 us (9%)
  local copies, waits for them, and re-layouts  4.27 us (2%)
  matrix products  3.41 us (2%)
    pallas_call x4, Pallas kernels, pair_matmul(): pl.pallas_call(kernel, grid_spec=pltpu.PrefetchScalarGridSpec(num_scalar_...  75.6 us
    pallas_call x2, Pallas kernels, make_update(): pl.pallas_call(kernel, grid=(depth // tile,), in_specs=[whole((tokens, 1)...  41.6 us
    ppermute x12, starting transfers between devices, along(): return lax.ppermute(value, 'hidden', pairs)  27.7 us
    ppermute x12, waiting for transfers between devices, along(): return lax.ppermute(value, 'hidden', pairs)  24.3 us
    convert_element_type x7, other arithmetic, plus(): return (a.astype(F32) + b.astype(F32)).astype(BF16)  10.5 us
  transfers between devices with their start and end apart: 20, of which 5 were waited for; matrix products, arithmetic and copies ran while one was open for 8% of the time, Pallas kernels for 59%

profile of v1, /device:TPU:0, one launch (start us, length us, event | category | flops | bytes accessed | tf_op | source)
XLA Modules:
  0.0 203.0 jit_solution(17123718707417187961)
XLA Ops:
  0.6 0.5 collective-permute-start.2
  1.1 1.6 collective-permute-start.1
  2.8 4.5 %collective-permute-start = (bf16[256,2048]{1,0:T(8,128)(2,1)}, bf16[256,2048]{1,0:T(8,128)(2,1)}, u32[]{:S(2)}, u32[]{:S(2)}) collective-permute-start(bf16[256,2048]{1,0:T(8,128)(2,1)} %refs_1_.3), channel_id=1, source_target_pairs={{0,1},{1,0},{2,3},{3,2},{4,5},{5,4},{6,7},{7,6},{8,9},{9,8},{10,11... | collective-permute-start | bytes 3145736 | tf_op jit(solution)/shard_map/ppermute | solution.py:161
  7.3 1.5 collective-permute-start.4
  8.8 3.0 %convolution_convert_fusion = bf16[4,64,64]{2,1,0:T(8,128)(2,1)S(1)} fusion(bf16[4,64,4096]{2,1,0:T(8,128)(2,1)} %bitcast.16), kind=kOutput, calls=%fused_computation.6 | convolution fusion | flops 134234112 | bytes 2129920 | tf_op jit(solution)/shard_map/bsd,btd->bst/dot_general | solution.py:170
  11.8 0.4 convolution_convert_fusion.1
  12.3 0.1 maximum_maximum_fusion
  12.4 0.1 collective-permute-start.3
  12.5 0.7 stack.27.refs_0_
  13.1 0.1 pad_maximum_fusion.4
  13.2 0.0 collective-permute-done.2.refs_2_
  13.2 25.7 %in_grad_here.1 = (bf16[256,2048]{1,0:T(8,128)(2,1)}, bf16[256,2048]{1,0:T(8,128)(2,1)}, bf16[2048,4096]{1,0:T(8,128)(2,1)}, bf16[4,256,4096]{2,1,0:T(8,128)(2,1)}) custom-call(s32[6]{0:T(128)} %stack.27.refs_0_, bf16[256,4096]{1,0:T(8,128)(2,1)} %refs_1_.2, bf16[256,4096]{1,0:T(8,128)(2,1)} %collective-permute-done.2.refs_2_, f32[2048,4096]{1,0:T(8,128)} %refs_3_), custom_call_target="tpu_custom_call" | custom-call | flops 8589934592 | bytes 56623104 | tf_op jit(solution)/shard_map/in_grad_here/pallas_call | solution.py:73
  38.9 0.0 collective-permute-done.3
  38.9 0.0 collective-permute-done.1.refs_1_
  38.9 0.0 collective-permute-done.refs_2_
  39.0 1.3 collective-permute-start.6
  40.3 1.7 collective-permute-start.5
  42.0 0.6 collective-permute-start.7
  42.6 14.7 %outputs_near.1 = (bf16[256,4096]{1,0:T(8,128)(2,1)}, bf16[256,4096]{1,0:T(8,128)(2,1)}, bf16[4,256,2048]{2,1,0:T(8,128)(2,1)}) custom-call(s32[6]{0:T(128)} %stack.27.refs_0_, bf16[256,2048]{1,0:T(8,128)(2,1)} %refs_1_.3, bf16[256,2048]{1,0:T(8,128)(2,1)} %collective-permute-done.refs_2_, bf16[2048,4096]{1,0:T(8,128)(2,1)} %get-tuple-element.51.refs_3_.refs_5_), custom_call_target="tpu_custom_call" | custom-call | flops 8589934592 | bytes 23068672 | tf_op jit(solution)/shard_map/outputs_near/pallas_call | solution.py:73
  57.2 0.0 collective-permute-done.4.refs_1_
  57.2 0.0 collective-permute-done.7
  57.2 9.5 %collective-permute-done.6.refs_2_ = bf16[256,2048]{1,0:T(8,128)(2,1)} collective-permute-done((bf16[256,2048]{1,0:T(8,128)(2,1)}, bf16[256,2048]{1,0:T(8,128)(2,1)}, u32[]{:S(2)}, u32[]{:S(2)}) %collective-permute-start.6) | collective-permute-done | bytes 1048608 | tf_op jit(solution)/shard_map/ppermute | solution.py:161
  66.7 0.0 collective-permute-done.5.refs_3_
  66.7 0.0 collective-permute-start.9
  66.7 0.5 collective-permute-start.11
  67.2 1.3 collective-permute-start.10
  68.6 4.8 %collective-permute-start.8 = (bf16[10,64,128]{2,1,0:T(8,128)(2,1)S(1)}, bf16[10,64,128]{2,1,0:T(8,128)(2,1)S(1)}, u32[]{:S(2)}, u32[]{:S(2)}) collective-permute-start(bf16[10,64,128]{2,1,0:T(8,128)(2,1)S(1)} %pad_maximum_fusion.1), channel_id=1, source_target_pairs={{0,1},{1,0},{2,3},{3,2},{4,5},{5,4},{6,7},{7,6},{8,9},{9,8},{10,11... | collective-permute-start | bytes 491528 | tf_op jit(solution)/shard_map/ppermute | solution.py:161
  73.3 0.5 collective-permute-done.9.refs_2_
  73.8 1.3 copy-done.6
  75.2 17.4 %in_grad_there.1 = (bf16[256,2048]{1,0:T(8,128)(2,1)}, bf16[256,2048]{1,0:T(8,128)(2,1)}, bf16[256,2048]{1,0:T(8,128)(2,1)}, bf16[256,2048]{1,0:T(8,128)(2,1)}, bf16[4,256,4096]{2,1,0:T(8,128)(2,1)}) custom-call(s32[6]{0:T(128)} %stack.27.refs_0_, bf16[256,4096]{1,0:T(8,128)(2,1)} %copy-done.4, ...), custom_call_target="tpu_custom_call", output_to_operand_aliasing={{4}: (6, {})} | custom-call | flops 8589934592 | bytes 23068672 | tf_op jit(solution)/shard_map/in_grad_there/pallas_call | solution.py:73
  92.6 7.6 %collective-permute-done.8 = bf16[10,64,128]{2,1,0:T(8,128)(2,1)S(1)} collective-permute-done((bf16[10,64,128]{2,1,0:T(8,128)(2,1)S(1)}, bf16[10,64,128]{2,1,0:T(8,128)(2,1)S(1)}, u32[]{:S(2)}, u32[]{:S(2)}) %collective-permute-start.8) | collective-permute-done | bytes 163872 | tf_op jit(solution)/shard_map/ppermute | solution.py:161
  100.2 0.0 collective-permute-done.10.refs_4_
  100.2 2.5 %collective-permute-start.12 = (bf16[256,2048]{1,0:T(8,128)(2,1)}, bf16[256,2048]{1,0:T(8,128)(2,1)}, u32[]{:S(2)}, u32[]{:S(2)}) collective-permute-start(bf16[256,2048]{1,0:T(8,128)(2,1)} %get-tuple-element.68.refs_9_), channel_id=1, source_target_pairs={{0,1},{3,2},{4,5},{7,6},{8,9},{11,10},{12,13},{15,14},{16,17},{19,... | collective-permute-start | bytes 3145736 | tf_op jit(solution)/shard_map/ppermute | solution.py:161
  102.7 0.0 collective-permute-done.11.refs_7_
  102.7 17.8 %outputs_far.1 = (bf16[256,4096]{1,0:T(8,128)(2,1)}, bf16[256,4096]{1,0:T(8,128)(2,1)}, bf16[256,4096]{1,0:T(8,128)(2,1)}, bf16[4,256,2048]{2,1,0:T(8,128)(2,1)}) custom-call(s32[6]{0:T(128)} %stack.27.refs_0_, bf16[256,2048]{1,0:T(8,128)(2,1)} %collective-permute-done.1.refs_1_, ...), custom_call_target="tpu_custom_call", output_to_operand_aliasing={{3}: (8, {})} | custom-call | flops 8589934592 | bytes 23068672 | tf_op jit(solution)/shard_map/outputs_far/pallas_call | solution.py:73
  120.5 3.7 %collective-permute-done.12 = bf16[256,2048]{1,0:T(8,128)(2,1)} collective-permute-done((bf16[256,2048]{1,0:T(8,128)(2,1)}, bf16[256,2048]{1,0:T(8,128)(2,1)}, u32[]{:S(2)}, u32[]{:S(2)}) %collective-permute-start.12) | collective-permute-done | bytes 1048608 | tf_op jit(solution)/shard_map/ppermute | solution.py:161
  124.1 0.0 collective-permute-start.13
  124.1 0.9 slice.38
  125.1 0.9 add_convert_fusion.6.refs_2_
  126.0 0.0 copy-start.8
  126.0 2.4 %collective-permute-start.16 = (bf16[12,64,128]{2,1,0:T(8,128)(2,1)S(1)}, bf16[12,64,128]{2,1,0:T(8,128)(2,1)}, u32[]{:S(2)}, u32[]{:S(2)}) collective-permute-start(bf16[12,64,128]{2,1,0:T(8,128)(2,1)S(1)} %pad_maximum_fusion), channel_id=1, source_target_pairs={{0,2},{1,3},{2,0},{3,1},{4,6},{5,7},{6,4},{7,5},{8,10},{9,11},{10,... | collective-permute-start | bytes 589832 | tf_op jit(solution)/shard_map/ppermute | solution.py:161
  128.5 3.0 %collective-permute-start.15 = (bf16[256,2048]{1,0:T(8,128)(2,1)S(1)}, bf16[256,2048]{1,0:T(8,128)(2,1)}, u32[]{:S(2)}, u32[]{:S(2)}) collective-permute-start(bf16[256,2048]{1,0:T(8,128)(2,1)S(1)} %copy-done.10), channel_id=1, source_target_pairs={{0,1},{3,2},{4,5},{7,6},{8,9},{11,10},{12,13},{15,14},{16,17},{19,... | collective-permute-start | bytes 3145736 | tf_op jit(solution)/shard_map/ppermute | solution.py:161
  131.5 0.6 pad_maximum_fusion.3.refs_1_
  132.1 2.9 %add_convert_fusion.5 = bf16[256,2048]{1,0:T(8,128)(2,1)} fusion(bf16[256,2048]{1,0:T(8,128)(2,1)} %collective-permute-done.12, bf16[256,2048]{1,0:T(8,128)(2,1)} %get-tuple-element.68.refs_9_), kind=kLoop, calls=%fused_computation.5 | loop fusion | flops 2097152 | bytes 3145728 | tf_op jit(solution)/shard_map/convert_element_type | solution.py:217
  135.0 1.7 collective-permute-start.14
  136.8 0.0 collective-permute-done.13
  136.8 1.3 copy-done.1
  138.1 2.4 %add_convert_fusion.1.refs_0_ = bf16[256,4096]{1,0:T(8,128)(2,1)S(1)} fusion(bf16[256,4096]{1,0:T(8,128)(2,1)S(1)} %copy-done.5, bf16[256,4096]{1,0:T(8,128)(2,1)} %copy-done.1, pred[]{:T(512)S(6)} %eq.3), kind=kLoop, calls=%fused_computation.1 | loop fusion | flops 5242880 | bytes 6291457 | tf_op jit(solution)/shard_map/convert_element_type | solution.py:217
  140.5 0.1 collective-permute-start.19
  140.6 0.0 collective-permute-done.16.refs_3_
  140.6 2.5 %clip_factor.1.factor = f32[1024,1]{1,0:T(8,128)} custom-call(s32[6]{0:T(128)} %stack.27.refs_0_, bf16[4,64,128]{2,1,0:T(8,128)(2,1)} %pad_maximum_fusion.3.refs_1_, bf16[8,64,128]{2,1,0:T(8,128)(2,1)} %copy-done.8, bf16[12,64,128]{2,1,0:T(8,128)(2,1)} %collective-permute-done.16.refs_3_), custom_call_target="tpu_custom_call" | custom-call | tf_op jit(solution)/shard_map/clip_factor/pallas_call | solution.py:206
  143.1 20.9 %update.2.refs_0_ = f32[2048,4096]{1,0:T(8,128)} custom-call(f32[1024,1]{1,0:T(8,128)} %clip_factor.1.factor, bf16[1024,2048]{1,0:T(8,128)(2,1)} %bitcast.17, bf16[1024,4096]{1,0:T(8,128)(2,1)} %bitcast.14, bf16[2,2048,4096]{2,1,0:T(8,128)(2,1)} %noise.3, bf16[256,4096]{1,0:T(8,128)(2,1)} %copy-done), custom_call_target="tpu_custom_call" | custom-call | flops 8589934592 | bytes 41943040 | tf_op jit(solution)/shard_map/update/pallas_call | solution.py:130
  163.9 0.0 collective-permute-done.15
  163.9 0.0 collective-permute-done.14
  163.9 2.7 %add_convert_fusion.3 = bf16[256,2048]{1,0:T(8,128)(2,1)} fusion(bf16[256,2048]{1,0:T(8,128)(2,1)} %collective-permute-done.15, bf16[256,2048]{1,0:T(8,128)(2,1)S(1)} %copy-done.10), kind=kLoop, calls=%fused_computation.3 | loop fusion | flops 2097152 | bytes 3145728 | tf_op jit(solution)/shard_map/convert_element_type | solution.py:217
  166.6 1.6 collective-permute-start.18
  168.2 1.6 add_convert_fusion.4
  169.9 1.2 collective-permute-start.17
  171.1 20.8 %update.3 = f32[2048,4096]{1,0:T(8,128)} custom-call(f32[1024,1]{1,0:T(8,128)} %clip_factor.1.factor, bf16[1024,2048]{1,0:T(8,128)(2,1)} %bitcast.18, bf16[1024,4096]{1,0:T(8,128)(2,1)} %bitcast.15, bf16[2,2048,4096]{2,1,0:T(8,128)(2,1)} %noise.3, f32[2048,4096]{1,0:T(8,128)} %update.2.refs_0_), custom_call_target="tpu_custom_call", output_to_operand_aliasing={{}: (4, {})} | custom-call | flops 8589934592 | bytes 41943040 | tf_op jit(solution)/shard_map/update/pallas_call | solution.py:130
  191.9 0.0 collective-permute-done.18
  191.9 3.5 %collective-permute-done.17 = bf16[256,2048]{1,0:T(8,128)(2,1)} collective-permute-done((bf16[256,2048]{1,0:T(8,128)(2,1)S(1)}, bf16[256,2048]{1,0:T(8,128)(2,1)}, u32[]{:S(2)}, u32[]{:S(2)}) %collective-permute-start.17) | collective-permute-done | bytes 1048608 | tf_op jit(solution)/shard_map/ppermute | solution.py:161
  195.4 0.0 collective-permute-done.19
  195.4 3.6 %add_convert_fusion.2 = bf16[256,2048]{1,0:T(8,128)(2,1)} fusion(bf16[256,2048]{1,0:T(8,128)(2,1)} %collective-permute-done.18, bf16[256,2048]{1,0:T(8,128)(2,1)} %collective-permute-done.17, bf16[256,2048]{1,0:T(8,128)(2,1)} %get-tuple-element.85), kind=kLoop, calls=%fused_computation.2 | loop fusion | flops 3145728 | bytes 4194304 | tf_op jit(solution)/shard_map/convert_element_type | solution.py:359
  199.0 4.0 %add_convert_fusion = bf16[256,4096]{1,0:T(8,128)(2,1)} fusion(bf16[256,4096]{1,0:T(8,128)(2,1)} %collective-permute-done.19, bf16[256,4096]{1,0:T(8,128)(2,1)S(1)} %copy-done.7, bf16[256,4096]{1,0:T(8,128)(2,1)S(1)} %copy-done.2, pred[]{:T(512)S(6)} %eq.3), kind=kLoop, calls=%fused_computation | loop fusion | flops 7340032 | bytes 8388609 | tf_op jit(solution)/shard_map/convert_element_type | solution.py:361
  (32 shorter events, 0.1 us)
Async XLA Ops:
  0.6 12.6 %collective-permute-start.2 = (bf16[256,4096]{1,0:T(8,128)(2,1)}, bf16[256,4096]{1,0:T(8,128)(2,1)}, u32[]{:S(2)}, u32[]{:S(2)}) collective-permute-start(bf16[256,4096]{1,0:T(8,128)(2,1)} %refs_1_.2), channel_id=1, source_target_pairs={{0,4},{4,0},{8,12},{12,8},{1,5},{5,1},{9,13},{13,9},{2,6},{6,2},{1... | collective-permute-start | bytes 6291464 | tf_op jit(solution)/shard_map/ppermute | solution.py:165
  1.1 37.8 %collective-permute-start.1 = (bf16[256,2048]{1,0:T(8,128)(2,1)}, bf16[256,2048]{1,0:T(8,128)(2,1)}, u32[]{:S(2)}, u32[]{:S(2)}) collective-permute-start(bf16[256,2048]{1,0:T(8,128)(2,1)} %refs_1_.3), channel_id=1, source_target_pairs={{1,2},{2,1},{5,6},{6,5},{9,10},{10,9},{13,14},{14,13},{17,18},{18,... | collective-permute-start | bytes 3145736 | tf_op jit(solution)/shard_map/ppermute | solution.py:161
  2.8 36.2 %collective-permute-start = (bf16[256,2048]{1,0:T(8,128)(2,1)}, bf16[256,2048]{1,0:T(8,128)(2,1)}, u32[]{:S(2)}, u32[]{:S(2)}) collective-permute-start(bf16[256,2048]{1,0:T(8,128)(2,1)} %refs_1_.3), channel_id=1, source_target_pairs={{0,1},{1,0},{2,3},{3,2},{4,5},{5,4},{6,7},{7,6},{8,9},{9,8},{10,11... | collective-permute-start | bytes 3145736 | tf_op jit(solution)/shard_map/ppermute | solution.py:161
  7.3 49.9 %collective-permute-start.4 = (bf16[256,4096]{1,0:T(8,128)(2,1)}, bf16[256,4096]{1,0:T(8,128)(2,1)S(1)}, u32[]{:S(2)}, u32[]{:S(2)}) collective-permute-start(bf16[256,4096]{1,0:T(8,128)(2,1)} %refs_1_.2), channel_id=1, source_target_pairs={{0,8},{4,12},{8,0},{12,4},{1,9},{5,13},{9,1},{13,5},{2,10},{6,14},... | collective-permute-start | bytes 6291464 | tf_op jit(solution)/shard_map/ppermute | solution.py:165
  8.8 3.0 %copy-start.3 = (bf16[256,2048]{1,0:T(8,128)(2,1)S(1)}, bf16[256,2048]{1,0:T(8,128)(2,1)}, u32[]{:S(2)}) copy-start(bf16[256,2048]{1,0:T(8,128)(2,1)} %refs_1_.3) | copy-start | bytes 3145732
  12.4 26.6 %collective-permute-start.3 = (bf16[4,64,128]{2,1,0:T(8,128)(2,1)S(1)}, bf16[4,64,128]{2,1,0:T(8,128)(2,1)S(1)}, u32[]{:S(2)}, u32[]{:S(2)}) collective-permute-start(bf16[4,64,128]{2,1,0:T(8,128)(2,1)S(1)} %maximum_maximum_fusion), channel_id=1, source_target_pairs={{0,4},{4,0},{8,12},{12,8},{1,5},{5,1},{9,13},{13,9},{2,6},{6,2},{1... | collective-permute-start | bytes 196616 | tf_op jit(solution)/shard_map/ppermute | solution.py:165
  39.0 27.7 %collective-permute-start.6 = (bf16[256,2048]{1,0:T(8,128)(2,1)}, bf16[256,2048]{1,0:T(8,128)(2,1)}, u32[]{:S(2)}, u32[]{:S(2)}) collective-permute-start(bf16[256,2048]{1,0:T(8,128)(2,1)} %collective-permute-done.1.refs_1_), channel_id=1, source_target_pairs={{1,0},{2,3},{5,4},{6,7},{9,8},{10,11},{13,12},{14,15},{17,16},{18,... | collective-permute-start | bytes 3145736 | tf_op jit(solution)/shard_map/ppermute | solution.py:161
  40.3 26.4 %collective-permute-start.5 = (bf16[256,2048]{1,0:T(8,128)(2,1)}, bf16[256,2048]{1,0:T(8,128)(2,1)}, u32[]{:S(2)}, u32[]{:S(2)}) collective-permute-start(bf16[256,2048]{1,0:T(8,128)(2,1)} %collective-permute-done.refs_2_), channel_id=1, source_target_pairs={{1,2},{2,1},{5,6},{6,5},{9,10},{10,9},{13,14},{14,13},{17,18},{18,... | collective-permute-start | bytes 3145736 | tf_op jit(solution)/shard_map/ppermute | solution.py:161
  42.0 15.3 %collective-permute-start.7 = (bf16[6,64,128]{2,1,0:T(8,128)(2,1)S(1)}, bf16[6,64,128]{2,1,0:T(8,128)(2,1)S(1)}, u32[]{:S(2)}, u32[]{:S(2)}) collective-permute-start(bf16[6,64,128]{2,1,0:T(8,128)(2,1)S(1)} %pad_maximum_fusion.2), channel_id=1, source_target_pairs={{0,8},{4,12},{8,0},{12,4},{1,9},{5,13},{9,1},{13,5},{2,10},{6,14},... | collective-permute-start | bytes 294920 | tf_op jit(solution)/shard_map/ppermute | solution.py:165
  57.2 17.9 %copy-start.4 = (bf16[256,4096]{1,0:T(8,128)(2,1)}, bf16[256,4096]{1,0:T(8,128)(2,1)S(1)}, u32[]{:S(2)}) copy-start(bf16[256,4096]{1,0:T(8,128)(2,1)S(1)} %collective-permute-done.4.refs_1_) | copy-start | bytes 6291460
  66.7 7.1 %collective-permute-start.9 = (bf16[256,4096]{1,0:T(8,128)(2,1)S(1)}, bf16[256,4096]{1,0:T(8,128)(2,1)S(1)}, u32[]{:S(2)}, u32[]{:S(2)}) collective-permute-start(bf16[256,4096]{1,0:T(8,128)(2,1)S(1)} %collective-permute-done.4.refs_1_), channel_id=1, source_target_pairs={{0,4},{4,0},{8,12},{12,8},{1,5},{5,1},{9,13},{13,9},{2,6},{6,2},{1... | collective-permute-start | bytes 6291464 | tf_op jit(solution)/shard_map/ppermute | solution.py:165
  66.7 36.0 %collective-permute-start.11 = (bf16[256,4096]{1,0:T(8,128)(2,1)}, bf16[256,4096]{1,0:T(8,128)(2,1)}, u32[]{:S(2)}, u32[]{:S(2)}) collective-permute-start(bf16[256,4096]{1,0:T(8,128)(2,1)} %get-tuple-element.66), channel_id=1, source_target_pairs={{0,4},{4,0},{8,12},{12,8},{1,5},{5,1},{9,13},{13,9},{2,6},{6,2},{1... | collective-permute-start | bytes 6291464 | tf_op jit(solution)/shard_map/ppermute | solution.py:165
  67.2 33.0 %collective-permute-start.10 = (bf16[256,2048]{1,0:T(8,128)(2,1)}, bf16[256,2048]{1,0:T(8,128)(2,1)S(1)}, u32[]{:S(2)}, u32[]{:S(2)}) collective-permute-start(bf16[256,2048]{1,0:T(8,128)(2,1)} %collective-permute-done.5.refs_3_), channel_id=1, source_target_pairs={{1,0},{2,3},{5,4},{6,7},{9,8},{10,11},{13,12},{14,15},{17,16},{18,... | collective-permute-start | bytes 3145736 | tf_op jit(solution)/shard_map/ppermute | solution.py:161
  68.6 31.6 %collective-permute-start.8 = (bf16[10,64,128]{2,1,0:T(8,128)(2,1)S(1)}, bf16[10,64,128]{2,1,0:T(8,128)(2,1)S(1)}, u32[]{:S(2)}, u32[]{:S(2)}) collective-permute-start(bf16[10,64,128]{2,1,0:T(8,128)(2,1)S(1)} %pad_maximum_fusion.1), channel_id=1, source_target_pairs={{0,1},{1,0},{2,3},{3,2},{4,5},{5,4},{6,7},{7,6},{8,9},{9,8},{10,11... | collective-permute-start | bytes 491528 | tf_op jit(solution)/shard_map/ppermute | solution.py:161
  73.8 1.3 copy-start.6
  100.2 20.3 %copy-start.11 = (bf16[10,64,128]{2,1,0:T(8,128)(2,1)}, bf16[10,64,128]{2,1,0:T(8,128)(2,1)S(1)}, u32[]{:S(2)}) copy-start(bf16[10,64,128]{2,1,0:T(8,128)(2,1)S(1)} %collective-permute-done.8) | copy-start | bytes 491524
  100.2 2.5 %copy-start.12 = (bf16[256,2048]{1,0:T(8,128)(2,1)}, bf16[256,2048]{1,0:T(8,128)(2,1)S(1)}, u32[]{:S(2)}) copy-start(bf16[256,2048]{1,0:T(8,128)(2,1)S(1)} %collective-permute-done.10.refs_4_) | copy-start | bytes 3145732
  100.2 23.9 %collective-permute-start.12 = (bf16[256,2048]{1,0:T(8,128)(2,1)}, bf16[256,2048]{1,0:T(8,128)(2,1)}, u32[]{:S(2)}, u32[]{:S(2)}) collective-permute-start(bf16[256,2048]{1,0:T(8,128)(2,1)} %get-tuple-element.68.refs_9_), channel_id=1, source_target_pairs={{0,1},{3,2},{4,5},{7,6},{8,9},{11,10},{12,13},{15,14},{16,17},{19,... | collective-permute-start | bytes 3145736 | tf_op jit(solution)/shard_map/ppermute | solution.py:161
  102.7 25.8 %copy-start.10 = (bf16[256,2048]{1,0:T(8,128)(2,1)S(1)}, bf16[256,2048]{1,0:T(8,128)(2,1)}, u32[]{:S(2)}) copy-start(bf16[256,2048]{1,0:T(8,128)(2,1)} %get-tuple-element.74) | copy-start | bytes 3145732
  124.1 12.6 %collective-permute-start.13 = (bf16[256,4096]{1,0:T(8,128)(2,1)}, bf16[256,4096]{1,0:T(8,128)(2,1)S(1)}, u32[]{:S(2)}, u32[]{:S(2)}) collective-permute-start(bf16[256,4096]{1,0:T(8,128)(2,1)} %get-tuple-element.71), channel_id=1, source_target_pairs={{0,4},{4,0},{8,12},{12,8},{1,5},{5,1},{9,13},{13,9},{2,6},{6,2},{1... | collective-permute-start | bytes 6291464 | tf_op jit(solution)/shard_map/ppermute | solution.py:165
  124.1 13.9 %copy-start.5 = (bf16[256,4096]{1,0:T(8,128)(2,1)S(1)}, bf16[256,4096]{1,0:T(8,128)(2,1)}, u32[]{:S(2)}) copy-start(bf16[256,4096]{1,0:T(8,128)(2,1)} %get-tuple-element.76) | copy-start | bytes 6291460
  126.0 14.5 %copy-start.8 = (bf16[8,64,128]{2,1,0:T(8,128)(2,1)}, bf16[8,64,128]{2,1,0:T(8,128)(2,1)S(1)}, u32[]{:S(2)}) copy-start(bf16[8,64,128]{2,1,0:T(8,128)(2,1)S(1)} %add_convert_fusion.6.refs_2_) | copy-start | bytes 393220
  126.0 14.5 %collective-permute-start.16 = (bf16[12,64,128]{2,1,0:T(8,128)(2,1)S(1)}, bf16[12,64,128]{2,1,0:T(8,128)(2,1)}, u32[]{:S(2)}, u32[]{:S(2)}) collective-permute-start(bf16[12,64,128]{2,1,0:T(8,128)(2,1)S(1)} %pad_maximum_fusion), channel_id=1, source_target_pairs={{0,2},{1,3},{2,0},{3,1},{4,6},{5,7},{6,4},{7,5},{8,10},{9,11},{10,... | collective-permute-start | bytes 589832 | tf_op jit(solution)/shard_map/ppermute | solution.py:161
  128.5 35.5 %collective-permute-start.15 = (bf16[256,2048]{1,0:T(8,128)(2,1)S(1)}, bf16[256,2048]{1,0:T(8,128)(2,1)}, u32[]{:S(2)}, u32[]{:S(2)}) collective-permute-start(bf16[256,2048]{1,0:T(8,128)(2,1)S(1)} %copy-done.10), channel_id=1, source_target_pairs={{0,1},{3,2},{4,5},{7,6},{8,9},{11,10},{12,13},{15,14},{16,17},{19,... | collective-permute-start | bytes 3145736 | tf_op jit(solution)/shard_map/ppermute | solution.py:161
  135.0 28.9 %collective-permute-start.14 = (bf16[256,2048]{1,0:T(8,128)(2,1)}, bf16[256,2048]{1,0:T(8,128)(2,1)}, u32[]{:S(2)}, u32[]{:S(2)}) collective-permute-start(bf16[256,2048]{1,0:T(8,128)(2,1)} %add_convert_fusion.5), channel_id=1, source_target_pairs={{1,2},{2,1},{5,6},{6,5},{9,10},{10,9},{13,14},{14,13},{17,18},{18,... | collective-permute-start | bytes 3145736 | tf_op jit(solution)/shard_map/ppermute | solution.py:161
  136.8 1.3 copy-start.1
  140.5 2.6 %copy-start = (bf16[256,4096]{1,0:T(8,128)(2,1)}, bf16[256,4096]{1,0:T(8,128)(2,1)S(1)}, u32[]{:S(2)}) copy-start(bf16[256,4096]{1,0:T(8,128)(2,1)S(1)} %add_convert_fusion.1.refs_0_) | copy-start | bytes 6291460
  140.5 54.9 %collective-permute-start.19 = (bf16[256,4096]{1,0:T(8,128)(2,1)S(1)}, bf16[256,4096]{1,0:T(8,128)(2,1)}, u32[]{:S(2)}, u32[]{:S(2)}) collective-permute-start(bf16[256,4096]{1,0:T(8,128)(2,1)S(1)} %add_convert_fusion.1.refs_0_), channel_id=1, source_target_pairs={{0,8},{4,12},{8,0},{12,4},{1,9},{5,13},{9,1},{13,5},{2,10},{6,14},... | collective-permute-start | bytes 6291464 | tf_op jit(solution)/shard_map/ppermute | solution.py:165
  163.9 4.3 %copy-start.9 = (bf16[256,2048]{1,0:T(8,128)(2,1)S(1)}, bf16[256,2048]{1,0:T(8,128)(2,1)}, u32[]{:S(2)}) copy-start(bf16[256,2048]{1,0:T(8,128)(2,1)} %get-tuple-element.72) | copy-start | bytes 3145732
  166.6 25.2 %collective-permute-start.18 = (bf16[256,2048]{1,0:T(8,128)(2,1)}, bf16[256,2048]{1,0:T(8,128)(2,1)}, u32[]{:S(2)}, u32[]{:S(2)}) collective-permute-start(bf16[256,2048]{1,0:T(8,128)(2,1)} %add_convert_fusion.3), channel_id=1, source_target_pairs={{1,2},{2,1},{5,6},{6,5},{9,10},{10,9},{13,14},{14,13},{17,18},{18,... | collective-permute-start | bytes 3145736 | tf_op jit(solution)/shard_map/ppermute | solution.py:161
  169.9 25.5 %collective-permute-start.17 = (bf16[256,2048]{1,0:T(8,128)(2,1)S(1)}, bf16[256,2048]{1,0:T(8,128)(2,1)}, u32[]{:S(2)}, u32[]{:S(2)}) collective-permute-start(bf16[256,2048]{1,0:T(8,128)(2,1)S(1)} %add_convert_fusion.4), channel_id=1, source_target_pairs={{0,1},{1,0},{2,3},{3,2},{4,5},{5,4},{6,7},{7,6},{8,9},{9,8},{10,11... | collective-permute-start | bytes 3145736 | tf_op jit(solution)/shard_map/ppermute | solution.py:161
  195.4 3.6 %copy-start.2 = (bf16[256,4096]{1,0:T(8,128)(2,1)S(1)}, bf16[256,4096]{1,0:T(8,128)(2,1)}, u32[]{:S(2)}) copy-start(bf16[256,4096]{1,0:T(8,128)(2,1)} %copy-done.1) | copy-start | bytes 6291460
  195.4 3.6 %copy-start.7 = (bf16[256,4096]{1,0:T(8,128)(2,1)S(1)}, bf16[256,4096]{1,0:T(8,128)(2,1)}, u32[]{:S(2)}) copy-start(bf16[256,4096]{1,0:T(8,128)(2,1)} %get-tuple-element.69) | copy-start | bytes 6291460

commit v2 on v1

v2 whole, which is shorter than its diff:
```python
import math

import jax
import jax.numpy as jnp
from jax import lax
from jax.experimental import pallas as pl
from jax.experimental.pallas import tpu as pltpu
from jax.sharding import PartitionSpec as P

SEQ = 64
NOISE_BAND = 0.6
NOISE_SCALE = 4.0
VMEM = 60 * 1024 * 1024
F32 = jnp.float32
BF16 = jnp.bfloat16
ANY = pl.BlockSpec(memory_space=pl.ANY)
BRIEF = pl.CostEstimate(flops=1, bytes_accessed=1, transcendentals=0)


def params(dims):
    return pltpu.CompilerParams(
        vmem_limit_bytes=VMEM, dimension_semantics=("arbitrary",) * dims
    )


def whole(shape):
    return pl.BlockSpec(shape, lambda *_: (0,) * len(shape))


def pair_kernel(transposed, place, finish, count, merged, extra, keep, at, *refs):
    pieces, w = refs[:count], refs[count]
    merges = refs[count + 1 : count + 1 + merged]
    *products, rows = refs[count + 1 + merged + extra :]
    kept = products.pop() if keep else None
    r = rows.shape[0] // 2

    @pl.when(pl.program_id(0) == 0)
    def _():
        for cond, slot, spot, piece in place(at, pieces):

            def put(slot=slot, spot=spot, piece=piece):
                rows[pl.ds(pl.multiple_of(slot * r, r), r), :] = piece[...]
                if keep:
                    kept[spot] = piece[...]

            if cond is None:
                put()
            else:
                pl.when(cond)(put)

    tile = w[...]
    if tile.dtype != BF16:
        tile = tile.astype(BF16)
        products[-1][...] = tile
    dims = (((1,), (1 if transposed else 0,)), ((), ()))
    total = lax.dot_general(rows[...], tile, dims, preferred_element_type=F32)
    finish(at, total[:r], total[r:], merges, products)


def pair_matmul(
    at, pieces, w, place, transposed, finish, outs, merges, after, name, keep=False, share=(0, 8), before=()
):
    r, depth = pieces[0].shape
    width = w.shape[0] if transposed else w.shape[1]
    cast = w.dtype != BF16
    tile = min(256 if cast else 512 if transposed else 1024, width)
    skip = width // tile * share[0] // 8
    steps = width // tile * share[1] // 8 - skip
    w_spec = (
        pl.BlockSpec((tile, depth), lambda i: (i + skip, 0))
        if transposed
        else pl.BlockSpec((depth, tile), lambda i: (0, i + skip))
    )
    extra = [*before, *after]
    count = len(pieces)
    first_extra = count + 2 + len(merges)
    product = pl.BlockSpec((r, tile), lambda i: (0, i + skip))
    kernel = lambda *refs: pair_kernel(
        transposed, place, finish, count, len(merges), len(extra), keep, *refs
    )
    return pl.pallas_call(
        kernel,
        grid=(steps,),
        in_specs=[pl.BlockSpec(memory_space=pltpu.SMEM)]
        + [whole((r, depth))] * count
        + [w_spec]
        + [product] * len(merges)
        + [ANY] * len(extra),
        out_specs=[product] * outs + [w_spec] * cast + [whole((2, r, depth))] * keep,
        scratch_shapes=[pltpu.VMEM((2 * r, depth), BF16)],
        out_shape=[jax.ShapeDtypeStruct((r, width), BF16)] * outs
        + [jax.ShapeDtypeStruct(w.shape, BF16)] * cast
        + [jax.ShapeDtypeStruct((2, r, depth), BF16)] * keep,
        input_output_aliases={first_extra + i: i for i in range(len(before))},
        compiler_params=params(1),
        cost_estimate=BRIEF,
        name=name,
    )(at, *pieces, w, *merges, *extra)


def update_kernel(gain, count, nx, ng, extra, slot_of, block_of, at, factor, *refs):
    xs, gs, noise = refs[:nx], refs[nx : nx + ng], refs[nx + ng]
    out, scaled, rows = refs[nx + ng + 1 + extra :]
    rx, rg = rows.shape[0] // nx, scaled.shape[0] // ng

    @pl.when(pl.program_id(0) == 0)
    def _():
        for j, g in enumerate(gs):
            block = block_of(at, j)
            source, target = block * rg, slot_of(at, block) * rg
            for t in range(0, rg, SEQ):
                scale = factor[pl.ds(pl.multiple_of(source + t, SEQ), SEQ), :]
                scaled[pl.ds(pl.multiple_of(target + t, SEQ), SEQ), :] = (
                    g[t : t + SEQ, :].astype(F32) * scale
                ).astype(BF16)

    for j, x in enumerate(xs):
        rows[j * rx : (j + 1) * rx, :] = x[...].reshape(rx, -1)
    step = min(1024, out.shape[1])
    for j in range(0, out.shape[1], step):
        span = pl.ds(j, step)
        grad = lax.dot_general(
            rows[...], scaled[:, span], (((0,), (0,)), ((), ())), preferred_element_type=F32
        )
        band = noise[0, :, span].astype(F32) - NOISE_BAND * noise[1, :, span].astype(F32)
        out[:, span] = (grad * gain + NOISE_SCALE * band) * (1.0 / count)


def make_update(
    at, xs, gs, slot_of, block_of, factor, noise, gain, count, part=0, parts=1, before=None, after=()
):
    tokens = factor.shape[0]
    depth, whole_width = noise.shape[1:]
    width = whole_width // parts
    tile = min(512, depth)
    rx, rg = tokens // len(xs), tokens // len(gs)
    extra = ([] if before is None else [before]) + list(after)

    def x_spec(lead):
        if lead is None:
            return pl.BlockSpec((rx, tile), lambda i: (0, i))
        return pl.BlockSpec((1, rx, tile), lambda i: (lead, 0, i))

    def kernel(*refs):
        update_kernel(gain, count, len(xs), len(gs), len(extra), slot_of, block_of, *refs)

    return pl.pallas_call(
        kernel,
        grid=(depth // tile,),
        in_specs=[pl.BlockSpec(memory_space=pltpu.SMEM), whole((tokens, 1))]
        + [x_spec(lead) for _, lead in xs]
        + [pl.BlockSpec((rg, width), lambda i: (0, part))] * len(gs)
        + [pl.BlockSpec((2, tile, width), lambda i: (0, i, part))]
        + [ANY] * len(extra),
        out_specs=pl.BlockSpec((tile, width), lambda i: (i, part)),
        out_shape=jax.ShapeDtypeStruct((depth, whole_width), F32),
        scratch_shapes=[pltpu.VMEM((tokens, width), BF16), pltpu.VMEM((tokens, tile), BF16)],
        input_output_aliases={} if before is None else {3 + len(xs) + len(gs): 0},
        compiler_params=params(1),
        cost_estimate=BRIEF,
        name="update",
    )(at, factor, *[x for x, _ in xs], *gs, noise, *extra)


def add_kernel(sums, ins, at, *refs):
    sums(at, refs[:ins], refs[ins:])


def add_up(at, sums, arrays, outs, steps, name):
    def band(shape):
        return pl.BlockSpec((shape[0] // steps, shape[1]), lambda i: (i, 0))

    return pl.pallas_call(
        lambda *refs: add_kernel(sums, len(arrays), *refs),
        grid=(steps,),
        in_specs=[pl.BlockSpec(memory_space=pltpu.SMEM)] + [band(x.shape) for x in arrays],
        out_specs=[band(shape) for shape in outs],
        out_shape=[jax.ShapeDtypeStruct(shape, BF16) for shape in outs],
        compiler_params=params(1),
        cost_estimate=BRIEF,
        name=name,
    )(at, *arrays)


def total(*refs):
    return sum(ref[...].astype(F32) for ref in refs)


OUTER = [(0, 1), (1, 0), (2, 3), (3, 2)]
MIDDLE = [(1, 2), (2, 1)]
INWARD = [(0, 1), (3, 2)]
OUTWARD = [(1, 0), (2, 3)]


def along(value, pairs):
    return lax.ppermute(value, "hidden", pairs)


def swap(value, bit):
    return lax.ppermute(value, "mp", [(i, i ^ bit) for i in range(4)])


def gram(rows):
    blocks = rows.reshape(-1, SEQ, rows.shape[1])
    return jnp.einsum("bsd,btd->bst", blocks, blocks, preferred_element_type=F32)


def gram_pairs(rows):
    blocks = gram(rows).astype(BF16)
    return jnp.concatenate([blocks[0::2], blocks[1::2]], axis=2)


def factor_kernel(clip, pairs, n, at, *refs):
    *grams, out = refs
    h, m = at[2], at[3]
    r = out.shape[0] // n
    lane = lax.broadcasted_iota(jnp.int32, (1, 2 * SEQ), 1)
    for i, gram in enumerate(grams):
        block = m ^ i
        for p in range(pairs):
            spot = (block ^ h) * pairs + p
            feature = sum(g[spot].astype(F32) for g in grams)
            products = feature * gram[n * pairs + p].astype(F32)
            sums = jnp.sum(products, axis=0, keepdims=True)
            for side in range(2):
                square = jnp.sum(
                    jnp.where(lane // SEQ == side, sums, 0.0), axis=1, keepdims=True
                )
                factor = jnp.minimum(1.0, clip / jnp.sqrt(square + 1e-06))
                start = pl.multiple_of(block * r + (2 * p + side) * SEQ, SEQ)
                out[pl.ds(start, SEQ), :] = jnp.broadcast_to(factor, (SEQ, 1))


def make_factor(at, grams, clip, pairs, tokens):
    return pl.pallas_call(
        lambda *refs: factor_kernel(clip, pairs, len(grams), *refs),
        in_specs=[pl.BlockSpec(memory_space=pltpu.SMEM)]
        + [pl.BlockSpec(memory_space=pltpu.VMEM)] * len(grams),
        out_specs=pl.BlockSpec(memory_space=pltpu.VMEM),
        out_shape=jax.ShapeDtypeStruct((tokens, 1), F32),
        cost_estimate=BRIEF,
        name="clip_factor",
    )(at, *grams)


def plus(a, b):
    return (a.astype(F32) + b.astype(F32)).astype(BF16)


def pipelined(inputs, out_grad, weight, noise):
    n = 4
    m, h = lax.axis_index("mp"), lax.axis_index("hidden")
    at = jnp.stack([h // 2, m // 2, h, m]).astype(jnp.int32)
    d_all, ff_all = inputs.shape[1] * n, out_grad.shape[1] * n
    tokens = inputs.shape[0] * n
    clip = math.sqrt(SEQ * d_all * ff_all)
    hold = lax.optimization_barrier

    g_side = swap(out_grad, 1)
    g_far = swap(out_grad, 2)
    x_side = along(inputs, OUTER)
    x_mid = along(inputs, MIDDLE)
    features, units = gram_pairs(inputs), gram_pairs(out_grad)
    pairs = features.shape[0]
    grams = along(jnp.concatenate([features, units]), OUTER)
    weight, g_side, features, units = hold((weight, g_side, features, units))


    def out_grad_rows(half):
        def place(at, pieces):
            core, near = at[3] & 1, half(at) == at[0]

            def slot(block_core):
                return jnp.where(near, (block_core ^ at[2] ^ 1) & 1, block_core ^ at[0] ^ 1)

            return [(None, slot(core), 0, pieces[0]), (None, slot(1 - core), 0, pieces[1])]

        return place

    def near_rows(at, pieces):
        slot = (at[2] ^ at[3]) & 1
        return [(None, slot, 0, pieces[0]), (None, 1 - slot, 0, pieces[1])]

    def far_rows(at, pieces):
        slot = (at[0] ^ at[3]) & 1
        inner = (at[2] == 1) | (at[2] == 2)
        outer = jnp.logical_not(inner)
        return [
            (inner, slot, 0, pieces[0]),
            (outer, slot, 0, pieces[1]),
            (inner, 1 - slot, 1, pieces[2]),
            (outer, 1 - slot, 1, pieces[3]),
        ]

    def plainly(at, first, second, merges, products):
        products[0][...] = first.astype(BF16)
        products[1][...] = second.astype(BF16)

    def in_grad_order(at, first, second, merges, products):
        near_first = at[0] == at[1]

        @pl.when(near_first)
        def _():
            products[0][...], products[1][...] = first.astype(BF16), second.astype(BF16)
            products[2][...], products[3][...] = merges[0][...], merges[1][...]

        @pl.when(jnp.logical_not(near_first))
        def _():
            products[0][...], products[1][...] = merges[0][...], merges[1][...]
            products[2][...], products[3][...] = first.astype(BF16), second.astype(BF16)

    def outputs_order(at, first, second, merges, products):
        near = total(*merges).astype(BF16)
        near_mine = at[0] == at[1]
        products[2][...] = second.astype(BF16)

        @pl.when(near_mine)
        def _():
            products[0][...], products[1][...] = first.astype(BF16), near

        @pl.when(jnp.logical_not(near_mine))
        def _():
            products[0][...], products[1][...] = near, first.astype(BF16)

    def rows_here(share, before):
        return pair_matmul(
            at, [out_grad, g_side], weight, out_grad_rows(lambda at: at[1]), True, plainly, 2, [], [units],
            "in_grad_here", share=share, before=before,
        )

    x_side, x_mid, grams, *qa = hold((x_side, x_mid, grams, *rows_here((0, 5), ())))
    x_mid2 = along(x_side, MIDDLE)
    x_out = along(x_mid, OUTWARD)
    qa0, qa1, w = rows_here((5, 8), qa)
    pa0, pa1 = pair_matmul(
        at, [inputs, x_side], w, near_rows, False, plainly, 2, [], [], "outputs_near"
    )
    g_far, pa1, x_mid2, x_out, grams = hold((g_far, pa1, x_mid2, x_out, grams))
    features = jnp.concatenate([features, grams[:pairs]])
    units = plus(units, grams[pairs:])
    grams = along(jnp.concatenate([features, units]), [(i, i ^ 2) for i in range(n)])
    g_far_side = swap(g_far, 1)
    x_out2 = along(x_mid2, OUTWARD)
    pa1 = swap(pa1, 1)
    first, second, beside, own = pair_matmul(
        at, [g_far, g_far_side], w, out_grad_rows(lambda at: 1 - at[1]), True, in_grad_order, 4,
        [qa0, qa1], [pa0], "in_grad_there",
    )
    grams, first = hold((grams, first))
    grams = jnp.concatenate(
        [features, grams[: 2 * pairs], plus(units, grams[2 * pairs :])]
    )
    others = [swap(grams, j) for j in range(1, n)]
    r1a = along(first, INWARD)
    other, mine, pb1, x_far = pair_matmul(
        at, [x_mid, x_out, x_mid2, x_out2], w, far_rows, False, outputs_order, 3,
        [pa0, pa1], [first], "outputs_far", keep=True,
    )
    r1a, pb1, others = hold((r1a, pb1, others))
    pb1 = swap(pb1, 1)

    def now(at, refs, outs):
        outs[0][...] = total(refs[0], refs[1]).astype(BF16)
        side = jnp.where(at[0] == at[1], refs[3][...].astype(F32), 0.0)
        outs[1][...] = (refs[2][...].astype(F32) + side).astype(BF16)

    def later(at, refs, outs):
        outs[0][...] = total(refs[0], refs[1]).astype(BF16)
        outs[1][...] = total(refs[2], refs[3]).astype(BF16)

    def last(at, refs, outs):
        outs[0][...] = total(refs[0], refs[1], refs[2]).astype(BF16)
        side = jnp.where(at[0] == at[1], 0.0, refs[4][...].astype(F32))
        outs[1][...] = (total(refs[3], refs[5]) + side).astype(BF16)

    narrow, wide = first.shape, other.shape
    r2a, other = add_up(at, now, [first, r1a, other, pb1], [narrow, wide], 2, "sums_now")
    r2a = along(r2a, MIDDLE)
    r1b = along(second, INWARD)
    theirs = swap(other, 2)
    factor = make_factor(at, [grams, *others], clip, pairs, tokens)

    def block_of(at, j):
        return at[3] ^ j

    def slot_of(at, block):
        far = jnp.where(at[0] == 0, block, 3 - block)
        return jnp.where(block // 2 == at[0], (block ^ at[2]) & 1, far)

    xs = [(inputs, None), (x_side, None), (x_far, 0), (x_far, 1)]
    gs = [out_grad, g_side, g_far, g_far_side]
    gain = math.sqrt(d_all * ff_all) / clip
    facts = (slot_of, block_of, factor, noise, gain, tokens // SEQ)
    update = make_update(at, xs, gs, *facts, 0, 2, None, [other])
    r2a, r1b, update = hold((r2a, r1b, update))
    r3, r2b = add_up(at, later, [beside, r2a, second, r1b], [narrow, narrow], 2, "sums_later")
    r3 = along(r3, OUTER)
    r2b = along(r2b, MIDDLE)
    update = make_update(at, xs, gs, *facts, 1, 2, update)
    r3, r2b, theirs, update = hold((r3, r2b, theirs, update))
    in_grad, outputs = add_up(
        at, last, [own, r3, r2b, mine, pb1, theirs], [narrow, wide], 4, "sums_last"
    )
    return outputs, in_grad, update


def plain(tokens, d_all, ff_all, inputs, out_grad, weight, noise):
    w = weight.astype(BF16)
    x = lax.all_gather(inputs, "hidden", axis=0, tiled=True)
    g = lax.all_gather(out_grad, "mp", axis=0, tiled=True)
    clip = math.sqrt(SEQ * d_all * ff_all)
    outputs = lax.psum_scatter(
        jnp.dot(x, w, preferred_element_type=F32), "mp", scatter_dimension=0, tiled=True
    )
    in_grad = lax.psum_scatter(
        lax.dot_general(g, w, (((1,), (1,)), ((), ())), preferred_element_type=F32),
        "hidden",
        scatter_dimension=0,
        tiled=True,
    )
    grams = lax.psum(gram(x), "mp") * lax.psum(gram(g), "hidden")
    factor = jnp.minimum(1.0, clip / jnp.sqrt(jnp.sum(grams, axis=(1, 2)) + 1e-06))
    none = lambda at, j: 0
    update = make_update(
        jnp.zeros((1,), jnp.int32),
        [(x, None)],
        [g],
        none,
        none,
        jnp.repeat(factor, SEQ)[:, None],
        noise,
        math.sqrt(d_all * ff_all) / clip,
        tokens // SEQ,
    )
    return outputs.astype(BF16), in_grad.astype(BF16), update


def solution(mesh):
    mp, hidden = mesh.shape["mp"], mesh.shape["hidden"]

    def shards(inputs, out_grad, weight, noise):
        if mp == hidden == 4 and inputs.shape[0] % (2 * SEQ) == 0:
            return pipelined(inputs, out_grad, weight, noise)
        return plain(
            inputs.shape[0] * hidden,
            inputs.shape[1] * mp,
            out_grad.shape[1] * hidden,
            inputs,
            out_grad,
            weight,
            noise,
        )

    in_specs = (
        P(("groups", "hidden"), "mp"),
        P(("groups", "mp"), "hidden"),
        P("mp", "hidden"),
        P(None, ("groups", "mp"), "hidden"),
    )
    out_specs = (
        P(("groups", "mp"), "hidden"),
        P(("groups", "hidden"), "mp"),
        P("mp", ("groups", "hidden")),
    )
    return jax.shard_map(shards, mesh=mesh, in_specs=in_specs, out_specs=out_specs, check_vma=False)
```

time: 204 us -> 189 us (0.926)
  other arithmetic: 19 us -> 1.6 us
  waiting for transfers between devices: 24.8 us -> 7.91 us
  Pallas kernels: 120 us -> 129 us
  starting transfers between devices: 30.9 us -> 39.7 us
    ppermute x12, waiting for transfers between devices: 24.3 us -> 7.89 us  [along(): return lax.ppermute(value, 'hidden', pairs)]
    convert_element_type x7 -> x2, other arithmetic: 10.5 us -> 0.03 us  [plus(): return (a.astype(F32) + b.astype(F32)).astype(BF16)]
    pallas_call x7 -> x11, Pallas kernels: 120 us -> 129 us  [the longest x5 74.2 us: pair_matmul(): pl.pallas_call(kernel, grid=(steps,), in_specs=[pl.BlockSpec(memory_space...]
    convert_element_type x2 -> x0, other arithmetic: 7.55 us -> none  [the longest x1 3.98 us: pipelined(): outputs = (mine + theirs.astype(F32)).astype(BF16)]
    ppermute x12, starting transfers between devices: 27.7 us -> 34 us  [along(): return lax.ppermute(value, 'hidden', pairs)]
    unnamed x26 -> x28, local copies, waits for them, and re-layouts: 2.69 us -> 5.39 us
    ppermute x8 -> x9, starting transfers between devices: 3.26 us -> 5.71 us  [swap(): return lax.ppermute(value, 'mp', [(i, i ^ bit) for i in range(4)])]
  transfers between devices with their start and end apart: 20 -> 21, of which waited for: 5 -> 4; matrix products, arithmetic and copies ran while one was open for 8% -> 2% of each run, Pallas kernels for 59% -> 66%
where the time goes in v2:
time: 189 us; the launch traced here: 188 us
  Pallas kernels  129 us (68%)
  starting transfers between devices  39.7 us (21%)
  waiting for transfers between devices  7.91 us (4%)
  local copies, waits for them, and re-layouts  5.41 us (3%)
  matrix products  2.64 us (1%)
    pallas_call x5, Pallas kernels, pair_matmul(): pl.pallas_call(kernel, grid=(steps,), in_specs=[pl.BlockSpec(memory_space...  74.2 us
    pallas_call x2, Pallas kernels, make_update(): pl.pallas_call(kernel, grid=(depth // tile,), in_specs=[pl.BlockSpec(memo...  39.5 us
    ppermute x12, starting transfers between devices, along(): return lax.ppermute(value, 'hidden', pairs)  34 us
    pallas_call x3, Pallas kernels, add_up(): pl.pallas_call(lambda *refs: add_kernel(sums, len(arrays), *refs), grid=(...  13.5 us
    ppermute x12, waiting for transfers between devices, along(): return lax.ppermute(value, 'hidden', pairs)  7.89 us
    ppermute x9, starting transfers between devices, swap(): return lax.ppermute(value, 'mp', [(i, i ^ bit) for i in range(4)])  5.71 us
    unnamed x28, local copies, waits for them, and re-layouts  5.39 us
  transfers between devices with their start and end apart: 21, of which 4 were waited for; matrix products, arithmetic and copies ran while one was open for 2% of the time, Pallas kernels for 66%

profile of v2, /device:TPU:0, one launch (start us, length us, event | category | flops | bytes accessed | tf_op | source)
XLA Modules:
  0.0 187.6 jit_solution(14418221081173957931)
XLA Ops:
  0.6 0.0 copy-start
  0.6 0.5 collective-permute-start.4
  1.2 0.8 collective-permute-start.2
  2.0 5.4 %collective-permute-start.1 = (bf16[256,2048]{1,0:T(8,128)(2,1)}, bf16[256,2048]{1,0:T(8,128)(2,1)S(1)}, u32[]{:S(2)}, u32[]{:S(2)}) collective-permute-start(bf16[256,2048]{1,0:T(8,128)(2,1)} %refs_2_.3), channel_id=1, source_target_pairs={{0,1},{1,0},{2,3},{3,2},{4,5},{5,4},{6,7},{7,6},{8,9},{9,8},{10,11... | collective-permute-start | bytes 3145736 | tf_op jit(solution)/shard_map/ppermute | solution.py:196
  7.4 1.5 collective-permute-start
  8.9 2.0 %convolution_convert_fusion.1 = bf16[4,64,64]{2,1,0:T(8,128)(2,1)S(1)} fusion(bf16[4,64,2048]{2,1,0:T(8,128)(2,1)} %bitcast.11), kind=kOutput, calls=%fused_computation.1 | convolution fusion | flops 67125248 | bytes 1081344 | tf_op jit(solution)/shard_map/bsd,btd->bst/dot_general | solution.py:205
  10.9 0.7 convolution_convert_fusion
  11.6 0.1 maximum_maximum_fusion
  11.7 0.1 collective-permute-start.3
  11.9 0.1 pad_maximum_fusion.2
  12.0 0.7 pad_maximum_fusion.3.refs_4_.refs_7_
  12.7 0.7 pad_add_fusion.refs_0_
  13.3 0.0 collective-permute-done.4.refs_2_.refs_7_
  13.3 16.9 %in_grad_here.2 = (bf16[256,2048]{1,0:T(8,128)(2,1)}, bf16[256,2048]{1,0:T(8,128)(2,1)}, bf16[2048,4096]{1,0:T(8,128)(2,1)}) custom-call(s32[4]{0:T(128)} %pad_add_fusion.refs_0_, bf16[256,4096]{1,0:T(8,128)(2,1)} %refs_6_.3, bf16[256,4096]{1,0:T(8,128)(2,1)} %collective-permute-done.4.refs_2_.refs_7_, f32[2048,4096]{1,0:T(8,128)} %refs_3_.1, ...), custom_call_target="tpu_custom_call" | custom-call | flops 1 | bytes 1 | tf_op jit(solution)/shard_map/in_grad_here/pallas_call | solution.py:81
  30.2 2.2 %collective-permute-done.3 = bf16[4,64,128]{2,1,0:T(8,128)(2,1)S(1)} collective-permute-done((bf16[4,64,128]{2,1,0:T(8,128)(2,1)S(1)}, bf16[4,64,128]{2,1,0:T(8,128)(2,1)S(1)}, u32[]{:S(2)}, u32[]{:S(2)}) %collective-permute-start.3) | collective-permute-done | bytes 65568 | tf_op jit(solution)/shard_map/ppermute | solution.py:196
  32.5 0.0 collective-permute-done.2.refs_1_
  32.5 0.0 collective-permute-done.1.refs_2_.refs_3_
  32.5 1.3 collective-permute-start.6
  33.8 1.7 collective-permute-start.5
  35.5 11.7 %in_grad_here.3 = (bf16[256,2048]{1,0:T(8,128)(2,1)}, bf16[256,2048]{1,0:T(8,128)(2,1)}, bf16[2048,4096]{1,0:T(8,128)(2,1)}) custom-call(s32[4]{0:T(128)} %pad_add_fusion.refs_0_, bf16[256,4096]{1,0:T(8,128)(2,1)} %refs_6_.3, bf16[256,4096]{1,0:T(8,128)(2,1)} %collective-permute-done.4.refs_2_.refs_7_, ...), custom_call_target="tpu_custom_call", output_to_operand_aliasing={{0}: (4, {}), {1}: (5, {}), {2}: (6, {})} | custom-call | flops 1 | bytes 1 | tf_op jit(solution)/shard_map/in_grad_here/pallas_call | solution.py:81
  47.2 0.0 copy-start.10
  47.2 13.5 %outputs_near.1 = (bf16[256,4096]{1,0:T(8,128)(2,1)}, bf16[256,4096]{1,0:T(8,128)(2,1)}) custom-call(s32[4]{0:T(128)} %pad_add_fusion.refs_0_, bf16[256,2048]{1,0:T(8,128)(2,1)} %refs_2_.3, bf16[256,2048]{1,0:T(8,128)(2,1)} %copy-done.2, bf16[2048,4096]{1,0:T(8,128)(2,1)} %get-tuple-element.64.refs_3_.refs_5_), custom_call_target="tpu_custom_call" | custom-call | flops 1 | bytes 1 | tf_op jit(solution)/shard_map/outputs_near/pallas_call | solution.py:81
  60.7 0.0 collective-permute-done.refs_1_.refs_8_
  60.7 0.0 collective-permute-done.6.refs_2_
  60.7 0.0 collective-permute-done.5.refs_3_
  60.7 0.1 collective-permute-start.7
  60.8 0.5 collective-permute-start.11
  61.3 1.3 collective-permute-start.10
  62.6 6.3 %collective-permute-start.8 = (bf16[6,64,128]{2,1,0:T(8,128)(2,1)S(1)}, bf16[6,64,128]{2,1,0:T(8,128)(2,1)S(1)}, u32[]{:S(2)}, u32[]{:S(2)}) collective-permute-start(bf16[6,64,128]{2,1,0:T(8,128)(2,1)S(1)} %pad_maximum_fusion.1), channel_id=1, source_target_pairs={{0,2},{1,3},{2,0},{3,1},{4,6},{5,7},{6,4},{7,5},{8,10},{9,11},{10,... | collective-permute-start | bytes 294920 | tf_op jit(solution)/shard_map/ppermute | solution.py:196
  68.9 0.0 collective-permute-done.7.refs_2_.refs_9_
  69.0 1.3 copy-done.1
  70.3 15.2 %in_grad_there.1 = (bf16[256,2048]{1,0:T(8,128)(2,1)}, bf16[256,2048]{1,0:T(8,128)(2,1)}, bf16[256,2048]{1,0:T(8,128)(2,1)}, bf16[256,2048]{1,0:T(8,128)(2,1)}) custom-call(s32[4]{0:T(128)} %pad_add_fusion.refs_0_, bf16[256,4096]{1,0:T(8,128)(2,1)} %collective-permute-done.refs_1_.refs_8_, bf16[256,4096]{1,0:T(8,128)(2,1)} %copy-done.1, ...), custom_call_target="tpu_custom_call" | custom-call | flops 1 | bytes 1 | tf_op jit(solution)/shard_map/in_grad_there/pallas_call | solution.py:81
  85.4 0.0 collective-permute-done.8
  85.4 4.7 %collective-permute-start.9 = (bf16[256,2048]{1,0:T(8,128)(2,1)}, bf16[256,2048]{1,0:T(8,128)(2,1)S(1)}, u32[]{:S(2)}, u32[]{:S(2)}) collective-permute-start(bf16[256,2048]{1,0:T(8,128)(2,1)} %get-tuple-element.77.refs_8_.refs_1_), channel_id=1, source_target_pairs={{0,1},{3,2},{4,5},{7,6},{8,9},{11,10},{12,13},{15,14},{16,17},{19,... | collective-permute-start | bytes 3145736 | tf_op jit(solution)/shard_map/ppermute | solution.py:196
  90.2 1.0 collective-permute-start.14
  91.2 0.6 collective-permute-start.13
  91.8 0.8 collective-permute-done.10.refs_4_
  92.7 0.0 collective-permute-start.12
  92.7 0.0 collective-permute-done.11.refs_7_
  92.7 17.0 %outputs_far.1 = (bf16[256,4096]{1,0:T(8,128)(2,1)}, bf16[256,4096]{1,0:T(8,128)(2,1)}, bf16[256,4096]{1,0:T(8,128)(2,1)}, bf16[2,256,2048]{2,1,0:T(8,128)(2,1)}) custom-call(s32[4]{0:T(128)} %pad_add_fusion.refs_0_, bf16[256,2048]{1,0:T(8,128)(2,1)} %copy-done.5, bf16[256,2048]{1,0:T(8,128)(2,1)} %collective-permute-done.6.refs_2_, ...), custom_call_target="tpu_custom_call" | custom-call | flops 1 | bytes 1 | tf_op jit(solution)/shard_map/outputs_far/pallas_call | solution.py:81
  109.7 0.0 collective-permute-done.14.refs_4_
  109.7 0.0 collective-permute-done.13.refs_3_
  109.7 0.0 collective-permute-done.12.refs_2_
  109.7 0.0 copy-start.13
  109.7 3.3 %collective-permute-done.9.refs_2_ = bf16[256,2048]{1,0:T(8,128)(2,1)S(1)} collective-permute-done((bf16[256,2048]{1,0:T(8,128)(2,1)}, bf16[256,2048]{1,0:T(8,128)(2,1)S(1)}, u32[]{:S(2)}, u32[]{:S(2)}) %collective-permute-start.9) | collective-permute-done | bytes 1048608 | tf_op jit(solution)/shard_map/ppermute | solution.py:196
  113.1 1.0 copy-done.7
  114.0 0.0 collective-permute-start.15
  114.0 5.3 %collective-permute-start.17 = (bf16[256,2048]{1,0:T(8,128)(2,1)S(1)}, bf16[256,2048]{1,0:T(8,128)(2,1)}, u32[]{:S(2)}, u32[]{:S(2)}) collective-permute-start(bf16[256,2048]{1,0:T(8,128)(2,1)S(1)} %copy-done.6), channel_id=1, source_target_pairs={{0,1},{3,2},{4,5},{7,6},{8,9},{11,10},{12,13},{15,14},{16,17},{19,... | collective-permute-start | bytes 3145736 | tf_op jit(solution)/shard_map/ppermute | solution.py:196
  119.3 0.0 collective-permute-done.15.refs_4_.refs_5_
  119.3 1.4 copy-done.3
  120.7 4.3 %sums_now.1 = (bf16[256,2048]{1,0:T(8,128)(2,1)}, bf16[256,4096]{1,0:T(8,128)(2,1)}) custom-call(s32[4]{0:T(128)} %pad_add_fusion.refs_0_, bf16[256,2048]{1,0:T(8,128)(2,1)} %get-tuple-element.77.refs_8_.refs_1_, bf16[256,2048]{1,0:T(8,128)(2,1)} %copy-done.7, bf16[256,4096]{1,0:T(8,128)(2,1)} %get-tuple-element.84.refs_3_, bf16[256,4096]{1,0:T(8,128)(2,1)} %copy-done.3), custom_call_target="tpu_custom_call" | custom-call | flops 1 | bytes 1 | tf_op jit(solution)/shard_map/sums_now/pallas_call | solution.py:173
  124.9 1.6 collective-permute-start.16
  126.6 1.5 collective-permute-start.20
  128.0 2.2 %clip_factor.1.refs_1_ = f32[1024,1]{1,0:T(8,128)} custom-call(s32[4]{0:T(128)} %pad_add_fusion.refs_0_, bf16[10,64,128]{2,1,0:T(8,128)(2,1)} %copy-done.9, bf16[10,64,128]{2,1,0:T(8,128)(2,1)} %copy-done.13, bf16[10,64,128]{2,1,0:T(8,128)(2,1)} %copy-done.12, bf16[10,64,128]{2,1,0:T(8,128)(2,1)} %copy-done.11), custom_call_target="tpu_custom_call" | custom-call | flops 1 | bytes 1 | tf_op jit(solution)/shard_map/clip_factor/pallas_call | solution.py:235
  130.2 19.8 %update.2.refs_11_ = f32[2048,4096]{1,0:T(8,128)} custom-call(s32[4]{0:T(128)} %pad_add_fusion.refs_0_, f32[1024,1]{1,0:T(8,128)} %clip_factor.1.refs_1_, bf16[256,2048]{1,0:T(8,128)(2,1)} %refs_2_.3, bf16[256,2048]{1,0:T(8,128)(2,1)} %copy-done.2, bf16[2,256,2048]{2,1,0:T(8,128)(2,1)} %get-tuple-element.91.refs_4_.refs_5_, ...), custom_call_target="tpu_custom_call" | custom-call | flops 1 | bytes 1 | tf_op jit(solution)/shard_map/update/pallas_call | solution.py:147
  150.0 0.0 collective-permute-done.17.refs_4_
  150.0 3.3 %sums_later.1 = (bf16[256,2048]{1,0:T(8,128)(2,1)}, bf16[256,2048]{1,0:T(8,128)(2,1)}) custom-call(s32[4]{0:T(128)} %pad_add_fusion.refs_0_, bf16[256,2048]{1,0:T(8,128)(2,1)} %get-tuple-element.73.refs_1_, bf16[256,2048]{1,0:T(8,128)(2,1)} %collective-permute-done.16.refs_2_, bf16[256,2048]{1,0:T(8,128)(2,1)} %get-tuple-element.87.refs_3_, ...), custom_call_target="tpu_custom_call" | custom-call | flops 1 | bytes 1 | tf_op jit(solution)/shard_map/sums_later/pallas_call | solution.py:173
  153.3 3.8 %collective-permute-start.18 = (bf16[256,2048]{1,0:T(8,128)(2,1)}, bf16[256,2048]{1,0:T(8,128)(2,1)S(1)}, u32[]{:S(2)}, u32[]{:S(2)}) collective-permute-start(bf16[256,2048]{1,0:T(8,128)(2,1)} %get-tuple-element.95), channel_id=1, source_target_pairs={{0,1},{1,0},{2,3},{3,2},{4,5},{5,4},{6,7},{7,6},{8,9},{9,8},{10,11... | collective-permute-start | bytes 3145736 | tf_op jit(solution)/shard_map/ppermute | solution.py:196
  157.1 1.6 collective-permute-start.19
  158.8 19.7 %update.3 = f32[2048,4096]{1,0:T(8,128)} custom-call(s32[4]{0:T(128)} %pad_add_fusion.refs_0_, f32[1024,1]{1,0:T(8,128)} %clip_factor.1.refs_1_, bf16[256,2048]{1,0:T(8,128)(2,1)} %refs_2_.3, bf16[256,2048]{1,0:T(8,128)(2,1)} %copy-done.2, bf16[2,256,2048]{2,1,0:T(8,128)(2,1)} %get-tuple-element.91.refs_4_.refs_5_, ...), custom_call_target="tpu_custom_call", output_to_operand_aliasing={{}: (11, {})} | custom-call | flops 1 | bytes 1 | tf_op jit(solution)/shard_map/update/pallas_call | solution.py:147
  178.5 1.5 collective-permute-done.18.refs_2_
  180.0 1.0 copy-done.8
  181.0 0.7 copy-done.4
  181.7 5.9 %sums_last.1 = (bf16[256,2048]{1,0:T(8,128)(2,1)}, bf16[256,4096]{1,0:T(8,128)(2,1)}) custom-call(s32[4]{0:T(128)} %pad_add_fusion.refs_0_, bf16[256,2048]{1,0:T(8,128)(2,1)} %get-tuple-element.72.refs_1_, bf16[256,2048]{1,0:T(8,128)(2,1)} %copy-done.8, bf16[256,2048]{1,0:T(8,128)(2,1)} %collective-permute-done.19.refs_3_, ...), custom_call_target="tpu_custom_call" | custom-call | flops 1 | bytes 1 | tf_op jit(solution)/shard_map/sums_last/pallas_call | solution.py:173
  (30 shorter events, 0.1 us)
Async XLA Ops:
  0.6 10.3 %copy-start = (bf16[256,4096]{1,0:T(8,128)(2,1)S(1)}, bf16[256,4096]{1,0:T(8,128)(2,1)}, u32[]{:S(2)}) copy-start(bf16[256,4096]{1,0:T(8,128)(2,1)} %refs_6_.3) | copy-start | bytes 6291460
  0.6 12.7 %collective-permute-start.4 = (bf16[256,4096]{1,0:T(8,128)(2,1)}, bf16[256,4096]{1,0:T(8,128)(2,1)}, u32[]{:S(2)}, u32[]{:S(2)}) collective-permute-start(bf16[256,4096]{1,0:T(8,128)(2,1)} %refs_6_.3), channel_id=1, source_target_pairs={{0,4},{4,0},{8,12},{12,8},{1,5},{5,1},{9,13},{13,9},{2,6},{6,2},{1... | collective-permute-start | bytes 6291464 | tf_op jit(solution)/shard_map/ppermute | solution.py:200
  1.2 31.3 %collective-permute-start.2 = (bf16[256,2048]{1,0:T(8,128)(2,1)}, bf16[256,2048]{1,0:T(8,128)(2,1)S(1)}, u32[]{:S(2)}, u32[]{:S(2)}) collective-permute-start(bf16[256,2048]{1,0:T(8,128)(2,1)} %refs_2_.3), channel_id=1, source_target_pairs={{1,2},{2,1},{5,6},{6,5},{9,10},{10,9},{13,14},{14,13},{17,18},{18,... | collective-permute-start | bytes 3145736 | tf_op jit(solution)/shard_map/ppermute | solution.py:196
  2.0 30.4 %collective-permute-start.1 = (bf16[256,2048]{1,0:T(8,128)(2,1)}, bf16[256,2048]{1,0:T(8,128)(2,1)S(1)}, u32[]{:S(2)}, u32[]{:S(2)}) collective-permute-start(bf16[256,2048]{1,0:T(8,128)(2,1)} %refs_2_.3), channel_id=1, source_target_pairs={{0,1},{1,0},{2,3},{3,2},{4,5},{5,4},{6,7},{7,6},{8,9},{9,8},{10,11... | collective-permute-start | bytes 3145736 | tf_op jit(solution)/shard_map/ppermute | solution.py:196
  7.4 53.3 %collective-permute-start = (bf16[256,4096]{1,0:T(8,128)(2,1)}, bf16[256,4096]{1,0:T(8,128)(2,1)}, u32[]{:S(2)}, u32[]{:S(2)}) collective-permute-start(bf16[256,4096]{1,0:T(8,128)(2,1)} %refs_6_.3), channel_id=1, source_target_pairs={{0,8},{4,12},{8,0},{12,4},{1,9},{5,13},{9,1},{13,5},{2,10},{6,14},... | collective-permute-start | bytes 6291464 | tf_op jit(solution)/shard_map/ppermute | solution.py:200
  11.7 20.7 %collective-permute-start.3 = (bf16[4,64,128]{2,1,0:T(8,128)(2,1)S(1)}, bf16[4,64,128]{2,1,0:T(8,128)(2,1)S(1)}, u32[]{:S(2)}, u32[]{:S(2)}) collective-permute-start(bf16[4,64,128]{2,1,0:T(8,128)(2,1)S(1)} %maximum_maximum_fusion), channel_id=1, source_target_pairs={{0,1},{1,0},{2,3},{3,2},{4,5},{5,4},{6,7},{7,6},{8,9},{9,8},{10,11... | collective-permute-start | bytes 196616 | tf_op jit(solution)/shard_map/ppermute | solution.py:196
  32.5 14.7 %copy-start.5 = (bf16[256,2048]{1,0:T(8,128)(2,1)}, bf16[256,2048]{1,0:T(8,128)(2,1)S(1)}, u32[]{:S(2)}) copy-start(bf16[256,2048]{1,0:T(8,128)(2,1)S(1)} %collective-permute-done.2.refs_1_) | copy-start | bytes 3145732
  32.5 14.7 %copy-start.2 = (bf16[256,2048]{1,0:T(8,128)(2,1)}, bf16[256,2048]{1,0:T(8,128)(2,1)S(1)}, u32[]{:S(2)}) copy-start(bf16[256,2048]{1,0:T(8,128)(2,1)S(1)} %collective-permute-done.1.refs_2_.refs_3_) | copy-start | bytes 3145732
  32.5 28.2 %collective-permute-start.6 = (bf16[256,2048]{1,0:T(8,128)(2,1)S(1)}, bf16[256,2048]{1,0:T(8,128)(2,1)}, u32[]{:S(2)}, u32[]{:S(2)}) collective-permute-start(bf16[256,2048]{1,0:T(8,128)(2,1)S(1)} %collective-permute-done.2.refs_1_), channel_id=1, source_target_pairs={{1,0},{2,3},{5,4},{6,7},{9,8},{10,11},{13,12},{14,15},{17,16},{18,... | collective-permute-start | bytes 3145736 | tf_op jit(solution)/shard_map/ppermute | solution.py:196
  33.8 26.9 %collective-permute-start.5 = (bf16[256,2048]{1,0:T(8,128)(2,1)S(1)}, bf16[256,2048]{1,0:T(8,128)(2,1)}, u32[]{:S(2)}, u32[]{:S(2)}) collective-permute-start(bf16[256,2048]{1,0:T(8,128)(2,1)S(1)} %collective-permute-done.1.refs_2_.refs_3_), channel_id=1, source_target_pairs={{1,2},{2,1},{5,6},{6,5},{9,10},{10,9},{13,14},{14,13},{17,18},{18,... | collective-permute-start | bytes 3145736 | tf_op jit(solution)/shard_map/ppermute | solution.py:196
  47.2 15.4 %copy-start.10 = (bf16[2,64,128]{2,1,0:T(8,128)(2,1)S(1)}, bf16[2,64,128]{2,1,0:T(8,128)(2,1)}, u32[]{:S(2)}) copy-start(bf16[2,64,128]{2,1,0:T(8,128)(2,1)} %pad_maximum_fusion.3.refs_4_.refs_7_) | copy-start | bytes 98308
  60.7 8.2 %collective-permute-start.7 = (bf16[256,4096]{1,0:T(8,128)(2,1)}, bf16[256,4096]{1,0:T(8,128)(2,1)S(1)}, u32[]{:S(2)}, u32[]{:S(2)}) collective-permute-start(bf16[256,4096]{1,0:T(8,128)(2,1)} %collective-permute-done.refs_1_.refs_8_), channel_id=1, source_target_pairs={{0,4},{4,0},{8,12},{12,8},{1,5},{5,1},{9,13},{13,9},{2,6},{6,2},{1... | collective-permute-start | bytes 6291464 | tf_op jit(solution)/shard_map/ppermute | solution.py:200
  60.8 31.9 %collective-permute-start.11 = (bf16[256,4096]{1,0:T(8,128)(2,1)}, bf16[256,4096]{1,0:T(8,128)(2,1)}, u32[]{:S(2)}, u32[]{:S(2)}) collective-permute-start(bf16[256,4096]{1,0:T(8,128)(2,1)} %get-tuple-element.80), channel_id=1, source_target_pairs={{0,4},{4,0},{8,12},{12,8},{1,5},{5,1},{9,13},{13,9},{2,6},{6,2},{1... | collective-permute-start | bytes 6291464 | tf_op jit(solution)/shard_map/ppermute | solution.py:200
  61.3 31.4 %collective-permute-start.10 = (bf16[256,2048]{1,0:T(8,128)(2,1)}, bf16[256,2048]{1,0:T(8,128)(2,1)}, u32[]{:S(2)}, u32[]{:S(2)}) collective-permute-start(bf16[256,2048]{1,0:T(8,128)(2,1)} %collective-permute-done.5.refs_3_), channel_id=1, source_target_pairs={{1,0},{2,3},{5,4},{6,7},{9,8},{10,11},{13,12},{14,15},{17,16},{18,... | collective-permute-start | bytes 3145736 | tf_op jit(solution)/shard_map/ppermute | solution.py:196
  62.6 22.8 %collective-permute-start.8 = (bf16[6,64,128]{2,1,0:T(8,128)(2,1)S(1)}, bf16[6,64,128]{2,1,0:T(8,128)(2,1)S(1)}, u32[]{:S(2)}, u32[]{:S(2)}) collective-permute-start(bf16[6,64,128]{2,1,0:T(8,128)(2,1)S(1)} %pad_maximum_fusion.1), channel_id=1, source_target_pairs={{0,2},{1,3},{2,0},{3,1},{4,6},{5,7},{6,4},{7,5},{8,10},{9,11},{10,... | collective-permute-start | bytes 294920 | tf_op jit(solution)/shard_map/ppermute | solution.py:196
  69.0 1.3 copy-start.1
  85.4 27.6 %collective-permute-start.9 = (bf16[256,2048]{1,0:T(8,128)(2,1)}, bf16[256,2048]{1,0:T(8,128)(2,1)S(1)}, u32[]{:S(2)}, u32[]{:S(2)}) collective-permute-start(bf16[256,2048]{1,0:T(8,128)(2,1)} %get-tuple-element.77.refs_8_.refs_1_), channel_id=1, source_target_pairs={{0,1},{3,2},{4,5},{7,6},{8,9},{11,10},{12,13},{15,14},{16,17},{19,... | collective-permute-start | bytes 3145736 | tf_op jit(solution)/shard_map/ppermute | solution.py:196
  90.2 19.5 %copy-start.9 = (bf16[10,64,128]{2,1,0:T(8,128)(2,1)}, bf16[10,64,128]{2,1,0:T(8,128)(2,1)S(1)}, u32[]{:S(2)}) copy-start(bf16[10,64,128]{2,1,0:T(8,128)(2,1)S(1)} %pad_maximum_fusion.refs_1_) | copy-start | bytes 491524
  90.2 23.9 %copy-start.6 = (bf16[256,2048]{1,0:T(8,128)(2,1)S(1)}, bf16[256,2048]{1,0:T(8,128)(2,1)}, u32[]{:S(2)}) copy-start(bf16[256,2048]{1,0:T(8,128)(2,1)} %get-tuple-element.87.refs_3_) | copy-start | bytes 3145732
  90.2 19.5 %collective-permute-start.14 = (bf16[10,64,128]{2,1,0:T(8,128)(2,1)S(1)}, bf16[10,64,128]{2,1,0:T(8,128)(2,1)S(1)}, u32[]{:S(2)}, u32[]{:S(2)}) collective-permute-start(bf16[10,64,128]{2,1,0:T(8,128)(2,1)S(1)} %pad_maximum_fusion.refs_1_), channel_id=1, source_target_pairs={{0,12},{4,8},{8,4},{12,0},{1,13},{5,9},{9,5},{13,1},{2,14},{6,10},... | collective-permute-start | bytes 491528 | tf_op jit(solution)/shard_map/ppermute | solution.py:200
  91.2 18.5 %collective-permute-start.13 = (bf16[10,64,128]{2,1,0:T(8,128)(2,1)S(1)}, bf16[10,64,128]{2,1,0:T(8,128)(2,1)S(1)}, u32[]{:S(2)}, u32[]{:S(2)}) collective-permute-start(bf16[10,64,128]{2,1,0:T(8,128)(2,1)S(1)} %pad_maximum_fusion.refs_1_), channel_id=1, source_target_pairs={{0,8},{4,12},{8,0},{12,4},{1,9},{5,13},{9,1},{13,5},{2,10},{6,14},... | collective-permute-start | bytes 491528 | tf_op jit(solution)/shard_map/ppermute | solution.py:200
  92.7 17.1 %collective-permute-start.12 = (bf16[10,64,128]{2,1,0:T(8,128)(2,1)S(1)}, bf16[10,64,128]{2,1,0:T(8,128)(2,1)S(1)}, u32[]{:S(2)}, u32[]{:S(2)}) collective-permute-start(bf16[10,64,128]{2,1,0:T(8,128)(2,1)S(1)} %pad_maximum_fusion.refs_1_), channel_id=1, source_target_pairs={{0,4},{4,0},{8,12},{12,8},{1,5},{5,1},{9,13},{13,9},{2,6},{6,2},{1... | collective-permute-start | bytes 491528 | tf_op jit(solution)/shard_map/ppermute | solution.py:200
  109.7 18.4 %copy-start.11 = (bf16[10,64,128]{2,1,0:T(8,128)(2,1)}, bf16[10,64,128]{2,1,0:T(8,128)(2,1)S(1)}, u32[]{:S(2)}) copy-start(bf16[10,64,128]{2,1,0:T(8,128)(2,1)S(1)} %collective-permute-done.14.refs_4_) | copy-start | bytes 491524
  109.7 3.3 %copy-start.12 = (bf16[10,64,128]{2,1,0:T(8,128)(2,1)}, bf16[10,64,128]{2,1,0:T(8,128)(2,1)S(1)}, u32[]{:S(2)}) copy-start(bf16[10,64,128]{2,1,0:T(8,128)(2,1)S(1)} %collective-permute-done.13.refs_3_) | copy-start | bytes 491524
  109.7 3.3 %copy-start.13 = (bf16[10,64,128]{2,1,0:T(8,128)(2,1)}, bf16[10,64,128]{2,1,0:T(8,128)(2,1)S(1)}, u32[]{:S(2)}) copy-start(bf16[10,64,128]{2,1,0:T(8,128)(2,1)S(1)} %collective-permute-done.12.refs_2_) | copy-start | bytes 491524
  113.1 1.0 copy-start.7
  114.0 5.3 %collective-permute-start.15 = (bf16[256,4096]{1,0:T(8,128)(2,1)}, bf16[256,4096]{1,0:T(8,128)(2,1)S(1)}, u32[]{:S(2)}, u32[]{:S(2)}) collective-permute-start(bf16[256,4096]{1,0:T(8,128)(2,1)} %get-tuple-element.85), channel_id=1, source_target_pairs={{0,4},{4,0},{8,12},{12,8},{1,5},{5,1},{9,13},{13,9},{2,6},{6,2},{1... | collective-permute-start | bytes 6291464 | tf_op jit(solution)/shard_map/ppermute | solution.py:200
  114.0 35.9 %collective-permute-start.17 = (bf16[256,2048]{1,0:T(8,128)(2,1)S(1)}, bf16[256,2048]{1,0:T(8,128)(2,1)}, u32[]{:S(2)}, u32[]{:S(2)}) collective-permute-start(bf16[256,2048]{1,0:T(8,128)(2,1)S(1)} %copy-done.6), channel_id=1, source_target_pairs={{0,1},{3,2},{4,5},{7,6},{8,9},{11,10},{12,13},{15,14},{16,17},{19,... | collective-permute-start | bytes 3145736 | tf_op jit(solution)/shard_map/ppermute | solution.py:196
  119.3 1.4 copy-start.3
  124.9 25.1 %collective-permute-start.16 = (bf16[256,2048]{1,0:T(8,128)(2,1)}, bf16[256,2048]{1,0:T(8,128)(2,1)}, u32[]{:S(2)}, u32[]{:S(2)}) collective-permute-start(bf16[256,2048]{1,0:T(8,128)(2,1)} %get-tuple-element.86), channel_id=1, source_target_pairs={{1,2},{2,1},{5,6},{6,5},{9,10},{10,9},{13,14},{14,13},{17,18},{18,... | collective-permute-start | bytes 3145736 | tf_op jit(solution)/shard_map/ppermute | solution.py:196
  126.6 53.4 %collective-permute-start.20 = (bf16[256,4096]{1,0:T(8,128)(2,1)}, bf16[256,4096]{1,0:T(8,128)(2,1)S(1)}, u32[]{:S(2)}, u32[]{:S(2)}) collective-permute-start(bf16[256,4096]{1,0:T(8,128)(2,1)} %get-tuple-element.92.refs_11_), channel_id=1, source_target_pairs={{0,8},{4,12},{8,0},{12,4},{1,9},{5,13},{9,1},{13,5},{2,10},{6,14},... | collective-permute-start | bytes 6291464 | tf_op jit(solution)/shard_map/ppermute | solution.py:200
  153.3 26.6 %collective-permute-start.18 = (bf16[256,2048]{1,0:T(8,128)(2,1)}, bf16[256,2048]{1,0:T(8,128)(2,1)S(1)}, u32[]{:S(2)}, u32[]{:S(2)}) collective-permute-start(bf16[256,2048]{1,0:T(8,128)(2,1)} %get-tuple-element.95), channel_id=1, source_target_pairs={{0,1},{1,0},{2,3},{3,2},{4,5},{5,4},{6,7},{7,6},{8,9},{9,8},{10,11... | collective-permute-start | bytes 3145736 | tf_op jit(solution)/shard_map/ppermute | solution.py:196
  157.1 22.8 %collective-permute-start.19 = (bf16[256,2048]{1,0:T(8,128)(2,1)}, bf16[256,2048]{1,0:T(8,128)(2,1)}, u32[]{:S(2)}, u32[]{:S(2)}) collective-permute-start(bf16[256,2048]{1,0:T(8,128)(2,1)} %get-tuple-element.96), channel_id=1, source_target_pairs={{1,2},{2,1},{5,6},{6,5},{9,10},{10,9},{13,14},{14,13},{17,18},{18,... | collective-permute-start | bytes 3145736 | tf_op jit(solution)/shard_map/ppermute | solution.py:196
  180.0 1.0 copy-start.8
  180.0 1.7 copy-start.4

commit v3 on v2

--- a/solution.py
+++ b/solution.py
@@ -10,7 +10,7 @@
 SEQ = 64
 NOISE_BAND = 0.6
 NOISE_SCALE = 4.0
-VMEM = 60 * 1024 * 1024
+VMEM = 63 * 1024 * 1024
 F32 = jnp.float32
 BF16 = jnp.bfloat16
 ANY = pl.BlockSpec(memory_space=pl.ANY)
@@ -166,20 +166,27 @@
     sums(at, refs[:ins], refs[ins:])
 
 
-def add_up(at, sums, arrays, outs, steps, name):
-    def band(shape):
-        return pl.BlockSpec((shape[0] // steps, shape[1]), lambda i: (i, 0))
-
+def add_up(at, sums, arrays, choices, outs, steps, name):
+    def band(shape, cond=None):
+        def index(i, at):
+            return (i if cond is None else jnp.where(cond(at), i, 0), 0)
+
+        return pl.BlockSpec((shape[0] // steps, shape[1]), index)
+
+    arrays, chosen = list(arrays), [x for _, x in choices]
     return pl.pallas_call(
-        lambda *refs: add_kernel(sums, len(arrays), *refs),
-        grid=(steps,),
-        in_specs=[pl.BlockSpec(memory_space=pltpu.SMEM)] + [band(x.shape) for x in arrays],
-        out_specs=[band(shape) for shape in outs],
+        lambda *refs: add_kernel(sums, len(arrays) + len(chosen), *refs),
+        grid_spec=pltpu.PrefetchScalarGridSpec(
+            num_scalar_prefetch=1,
+            grid=(steps,),
+            in_specs=[band(x.shape) for x in arrays] + [band(x.shape, c) for c, x in choices],
+            out_specs=[band(shape) for shape in outs],
+        ),
         out_shape=[jax.ShapeDtypeStruct(shape, BF16) for shape in outs],
         compiler_params=params(1),
         cost_estimate=BRIEF,
         name=name,
-    )(at, *arrays)
+    )(at, *arrays, *chosen)
 
 
 def total(*refs):
@@ -187,13 +194,20 @@
 
 
 OUTER = [(0, 1), (1, 0), (2, 3), (3, 2)]
-MIDDLE = [(1, 2), (2, 1)]
-INWARD = [(0, 1), (3, 2)]
 OUTWARD = [(1, 0), (2, 3)]
 
 
 def along(value, pairs):
     return lax.ppermute(value, "hidden", pairs)
+
+
+def middle(value):
+    pairs = [
+        (m * 4 + h, m * 4 + 3 - h if h in (1, 2) else (m ^ 1) * 4 + h)
+        for m in range(4)
+        for h in range(4)
+    ]
+    return lax.ppermute(value, ("mp", "hidden"), pairs)
 
 
 def swap(value, bit):
@@ -259,7 +273,7 @@
     g_side = swap(out_grad, 1)
     g_far = swap(out_grad, 2)
     x_side = along(inputs, OUTER)
-    x_mid = along(inputs, MIDDLE)
+    x_mid = middle(inputs)
     features, units = gram_pairs(inputs), gram_pairs(out_grad)
     pairs = features.shape[0]
     grams = along(jnp.concatenate([features, units]), OUTER)
@@ -309,19 +323,6 @@
             products[0][...], products[1][...] = merges[0][...], merges[1][...]
             products[2][...], products[3][...] = first.astype(BF16), second.astype(BF16)
 
-    def outputs_order(at, first, second, merges, products):
-        near = total(*merges).astype(BF16)
-        near_mine = at[0] == at[1]
-        products[2][...] = second.astype(BF16)
-
-        @pl.when(near_mine)
-        def _():
-            products[0][...], products[1][...] = first.astype(BF16), near
-
-        @pl.when(jnp.logical_not(near_mine))
-        def _():
-            products[0][...], products[1][...] = near, first.astype(BF16)
-
     def rows_here(share, before):
         return pair_matmul(
             at, [out_grad, g_side], weight, out_grad_rows(lambda at: at[1]), True, plainly, 2, [], [units],
@@ -329,8 +330,8 @@
         )
 
     x_side, x_mid, grams, *qa = hold((x_side, x_mid, grams, *rows_here((0, 5), ())))
-    x_mid2 = along(x_side, MIDDLE)
-    x_out = along(x_mid, OUTWARD)
+    x_mid2 = middle(x_side)
+    x_out = along(x_mid, OUTER)
     qa0, qa1, w = rows_here((5, 8), qa)
     pa0, pa1 = pair_matmul(
         at, [inputs, x_side], w, near_rows, False, plainly, 2, [], [], "outputs_near"
@@ -346,39 +347,60 @@
         at, [g_far, g_far_side], w, out_grad_rows(lambda at: 1 - at[1]), True, in_grad_order, 4,
         [qa0, qa1], [pa0], "in_grad_there",
     )
-    grams, first = hold((grams, first))
+    grams, first, pa1 = hold((grams, first, pa1))
     grams = jnp.concatenate(
         [features, grams[: 2 * pairs], plus(units, grams[2 * pairs :])]
     )
     others = [swap(grams, j) for j in range(1, n)]
-    r1a = along(first, INWARD)
-    other, mine, pb1, x_far = pair_matmul(
-        at, [x_mid, x_out, x_mid2, x_out2], w, far_rows, False, outputs_order, 3,
-        [pa0, pa1], [first], "outputs_far", keep=True,
-    )
-    r1a, pb1, others = hold((r1a, pb1, others))
+    r1a = along(first, OUTER)
+
+    def two(at, refs, outs):
+        outs[0][...] = total(*refs).astype(BF16)
+
+    narrow, wide = first.shape, pa0.shape
+    (near_sum,) = add_up(at, two, [pa0, pa1], [], [wide], 2, "sums_near")
+    pb0, pb1, x_far = pair_matmul(
+        at, [x_mid, x_out, x_mid2, x_out2], w, far_rows, False, plainly, 2,
+        [], [first, near_sum], "outputs_far", keep=True,
+    )
+    factor = make_factor(at, [grams, *others], clip, pairs, tokens)
+    r1a, pb1, factor = hold((r1a, pb1, factor))
     pb1 = swap(pb1, 1)
 
-    def now(at, refs, outs):
-        outs[0][...] = total(refs[0], refs[1]).astype(BF16)
-        side = jnp.where(at[0] == at[1], refs[3][...].astype(F32), 0.0)
-        outs[1][...] = (refs[2][...].astype(F32) + side).astype(BF16)
+    (r2a,) = add_up(at, two, [first, r1a], [], [narrow], 2, "sums_now")
+    pb1, r2a = hold((pb1, r2a))
+    r2a = middle(r2a)
+    r1b = along(second, OUTER)
+
+    def for_others(at, refs, outs):
+        far = total(refs[1], refs[2])
+        outs[0][...] = jnp.where(at[0] == at[1], far, refs[0][...].astype(F32)).astype(BF16)
+
+    def if_same(at):
+        return at[0] == at[1]
+
+    def if_other(at):
+        return at[0] != at[1]
+
+    (other,) = add_up(
+        at, for_others, [], [(if_other, near_sum), (if_same, pb0), (if_same, pb1)],
+        [wide], 2, "sums_others",
+    )
+    theirs = swap(other, 2)
+
+    def inner_only(at, ref):
+        return jnp.where((at[2] == 1) | (at[2] == 2), ref[...].astype(F32), 0.0)
 
     def later(at, refs, outs):
-        outs[0][...] = total(refs[0], refs[1]).astype(BF16)
+        outs[0][...] = (refs[0][...].astype(F32) + inner_only(at, refs[1])).astype(BF16)
         outs[1][...] = total(refs[2], refs[3]).astype(BF16)
 
-    def last(at, refs, outs):
-        outs[0][...] = total(refs[0], refs[1], refs[2]).astype(BF16)
-        side = jnp.where(at[0] == at[1], 0.0, refs[4][...].astype(F32))
-        outs[1][...] = (total(refs[3], refs[5]) + side).astype(BF16)
-
-    narrow, wide = first.shape, other.shape
-    r2a, other = add_up(at, now, [first, r1a, other, pb1], [narrow, wide], 2, "sums_now")
-    r2a = along(r2a, MIDDLE)
-    r1b = along(second, INWARD)
-    theirs = swap(other, 2)
-    factor = make_factor(at, [grams, *others], clip, pairs, tokens)
+    def last_outputs(at, refs, outs):
+        mine = jnp.where(at[0] == at[1], refs[1][...].astype(F32), total(*refs[2:]))
+        outs[0][...] = (mine + refs[0][...].astype(F32)).astype(BF16)
+
+    def last_in_grad(at, refs, outs):
+        outs[0][...] = (total(*refs[:2]) + inner_only(at, refs[2])).astype(BF16)
 
     def block_of(at, j):
         return at[3] ^ j
@@ -393,14 +415,17 @@
     facts = (slot_of, block_of, factor, noise, gain, tokens // SEQ)
     update = make_update(at, xs, gs, *facts, 0, 2, None, [other])
     r2a, r1b, update = hold((r2a, r1b, update))
-    r3, r2b = add_up(at, later, [beside, r2a, second, r1b], [narrow, narrow], 2, "sums_later")
+    r3, r2b = add_up(at, later, [beside, r2a, second, r1b], [], [narrow, narrow], 2, "sums_later")
     r3 = along(r3, OUTER)
-    r2b = along(r2b, MIDDLE)
+    r2b = middle(r2b)
     update = make_update(at, xs, gs, *facts, 1, 2, update)
-    r3, r2b, theirs, update = hold((r3, r2b, theirs, update))
-    in_grad, outputs = add_up(
-        at, last, [own, r3, r2b, mine, pb1, theirs], [narrow, wide], 4, "sums_last"
-    )
+    theirs, update = hold((theirs, update))
+    (outputs,) = add_up(
+        at, last_outputs, [theirs], [(if_same, near_sum), (if_other, pb0), (if_other, pb1)],
+        [wide], 2, "sums_outputs",
+    )
+    r3, r2b, outputs = hold((r3, r2b, outputs))
+    (in_grad,) = add_up(at, last_in_grad, [own, r3, r2b], [], [narrow], 2, "sums_in_grad")
     return outputs, in_grad, update
 
 

time: 189 us -> 177 us (0.937)
  starting transfers between devices: 39.7 us -> 19.8 us
  Pallas kernels: 129 us -> 138 us
  waiting for transfers between devices: 7.91 us -> 12.6 us
  local copies, waits for them, and re-layouts: 5.41 us -> 1.38 us
    ppermute x12 -> x8, starting transfers between devices: 34 us -> 13.7 us  [along(): return lax.ppermute(value, 'hidden', pairs)]
    pallas_call x3 -> x6, Pallas kernels: 13.5 us -> 24.3 us  [add_up(): pl.pallas_call(lambda *refs: add_kernel(sums, len(arrays) + len(chosen),...]
    unnamed x28 -> x12, local copies, waits for them, and re-layouts: 5.39 us -> 1.36 us
    ppermute x9, waiting for transfers between devices: 0.02 us -> 3.62 us  [swap(): return lax.ppermute(value, 'mp', [(i, i ^ bit) for i in range(4)])]
    pallas_call x5, Pallas kernels: 74.2 us -> 71.4 us  [pair_matmul(): pl.pallas_call(kernel, grid=(steps,), in_specs=[pl.BlockSpec(memory_space...]
    ppermute x12 -> x8, waiting for transfers between devices: 7.89 us -> 9.01 us  [along(): return lax.ppermute(value, 'hidden', pairs)]
  transfers between devices with their start and end apart: 21 -> 21, of which waited for: 4 -> 6; matrix products, arithmetic and copies ran while one was open for 2% -> 2% of each run, Pallas kernels for 66% -> 76%
where the time goes in v3:
time: 177 us; the launch traced here: 176 us
  Pallas kernels  138 us (78%)
  starting transfers between devices  19.8 us (11%)
  waiting for transfers between devices  12.6 us (7%)
  matrix products  2.64 us (1%)
    pallas_call x5, Pallas kernels, pair_matmul(): pl.pallas_call(kernel, grid=(steps,), in_specs=[pl.BlockSpec(memory_space...  71.4 us
    pallas_call x2, Pallas kernels, make_update(): pl.pallas_call(kernel, grid=(depth // tile,), in_specs=[pl.BlockSpec(memo...  39.6 us
    pallas_call x6, Pallas kernels, add_up(): pl.pallas_call(lambda *refs: add_kernel(sums, len(arrays) + len(chosen),...  24.3 us
    ppermute x8, starting transfers between devices, along(): return lax.ppermute(value, 'hidden', pairs)  13.7 us
    ppermute x8, waiting for transfers between devices, along(): return lax.ppermute(value, 'hidden', pairs)  9.01 us
    ppermute x9, starting transfers between devices, swap(): return lax.ppermute(value, 'mp', [(i, i ^ bit) for i in range(4)])  5.84 us
    ppermute x9, waiting for transfers between devices, swap(): return lax.ppermute(value, 'mp', [(i, i ^ bit) for i in range(4)])  3.62 us
  transfers between devices with their start and end apart: 21, of which 6 were waited for; matrix products, arithmetic and copies ran while one was open for 2% of the time, Pallas kernels for 76%

profile of v3, /device:TPU:0, one launch (start us, length us, event | category | flops | bytes accessed | tf_op | source)
XLA Modules:
  0.0 176.4 jit_solution(4506070153514179188)
XLA Ops:
  0.6 0.0 copy-start
  0.6 0.5 collective-permute-start.4
  1.2 0.1 collective-permute-start.2
  1.2 4.1 %collective-permute-start.1 = (bf16[256,2048]{1,0:T(8,128)(2,1)}, bf16[256,2048]{1,0:T(8,128)(2,1)}, u32[]{:S(2)}, u32[]{:S(2)}) collective-permute-start(bf16[256,2048]{1,0:T(8,128)(2,1)} %refs_2_.3), channel_id=1, source_target_pairs={{0,1},{1,0},{2,3},{3,2},{4,5},{5,4},{6,7},{7,6},{8,9},{9,8},{10,11... | collective-permute-start | bytes 3145736 | tf_op jit(solution)/shard_map/ppermute | solution.py:201
  5.4 1.5 collective-permute-start
  6.9 2.0 %convolution_convert_fusion.1 = bf16[4,64,64]{2,1,0:T(8,128)(2,1)S(1)} fusion(bf16[4,64,2048]{2,1,0:T(8,128)(2,1)} %bitcast.11), kind=kOutput, calls=%fused_computation.1 | convolution fusion | flops 67125248 | bytes 1081344 | tf_op jit(solution)/shard_map/bsd,btd->bst/dot_general | solution.py:219
  8.9 0.7 convolution_convert_fusion
  9.6 0.1 maximum_maximum_fusion
  9.7 0.1 collective-permute-start.3
  9.8 0.1 pad_maximum_fusion.2
  9.9 0.7 pad_maximum_fusion.3.refs_4_.refs_7_
  10.5 0.6 pad_add_fusion.refs_0_
  11.2 0.0 collective-permute-done.4.refs_2_.refs_7_
  11.2 16.9 %in_grad_here.2 = (bf16[256,2048]{1,0:T(8,128)(2,1)}, bf16[256,2048]{1,0:T(8,128)(2,1)}, bf16[2048,4096]{1,0:T(8,128)(2,1)}) custom-call(s32[4]{0:T(128)} %pad_add_fusion.refs_0_, bf16[256,4096]{1,0:T(8,128)(2,1)} %refs_6_.3, bf16[256,4096]{1,0:T(8,128)(2,1)} %collective-permute-done.4.refs_2_.refs_7_, f32[2048,4096]{1,0:T(8,128)} %refs_3_.1, ...), custom_call_target="tpu_custom_call" | custom-call | flops 1 | bytes 1 | tf_op jit(solution)/shard_map/in_grad_here/pallas_call | solution.py:81
  28.1 2.5 %collective-permute-done.3 = bf16[4,64,128]{2,1,0:T(8,128)(2,1)S(1)} collective-permute-done((bf16[4,64,128]{2,1,0:T(8,128)(2,1)S(1)}, bf16[4,64,128]{2,1,0:T(8,128)(2,1)S(1)}, u32[]{:S(2)}, u32[]{:S(2)}) %collective-permute-start.3) | collective-permute-done | bytes 65568 | tf_op jit(solution)/shard_map/ppermute | solution.py:201
  30.5 0.0 collective-permute-done.2.refs_1_
  30.5 0.0 collective-permute-done.1.refs_2_.refs_3_
  30.5 1.7 collective-permute-start.6
  32.2 0.0 collective-permute-start.5
  32.2 11.7 %in_grad_here.3 = (bf16[256,2048]{1,0:T(8,128)(2,1)}, bf16[256,2048]{1,0:T(8,128)(2,1)}, bf16[2048,4096]{1,0:T(8,128)(2,1)}) custom-call(s32[4]{0:T(128)} %pad_add_fusion.refs_0_, bf16[256,4096]{1,0:T(8,128)(2,1)} %refs_6_.3, bf16[256,4096]{1,0:T(8,128)(2,1)} %collective-permute-done.4.refs_2_.refs_7_, ...), custom_call_target="tpu_custom_call", output_to_operand_aliasing={{0}: (4, {}), {1}: (5, {}), {2}: (6, {})} | custom-call | flops 1 | bytes 1 | tf_op jit(solution)/shard_map/in_grad_here/pallas_call | solution.py:81
  43.9 13.5 %outputs_near.1 = (bf16[256,4096]{1,0:T(8,128)(2,1)}, bf16[256,4096]{1,0:T(8,128)(2,1)}) custom-call(s32[4]{0:T(128)} %pad_add_fusion.refs_0_, bf16[256,2048]{1,0:T(8,128)(2,1)} %refs_2_.3, bf16[256,2048]{1,0:T(8,128)(2,1)} %collective-permute-done.1.refs_2_.refs_3_, bf16[2048,4096]{1,0:T(8,128)(2,1)} %get-tuple-element.61.refs_3_.refs_5_), custom_call_target="tpu_custom_call" | custom-call | flops 1 | bytes 1 | tf_op jit(solution)/shard_map/outputs_near/pallas_call | solution.py:81
  57.4 0.0 collective-permute-done.refs_1_.refs_8_
  57.4 0.0 collective-permute-done.6.refs_2_
  57.4 0.0 collective-permute-done.5.refs_3_
  57.5 0.6 collective-permute-start.7
  58.0 0.1 collective-permute-start.9
  58.1 1.8 %collective-permute-start.8 = (bf16[6,64,128]{2,1,0:T(8,128)(2,1)S(1)}, bf16[6,64,128]{2,1,0:T(8,128)(2,1)S(1)}, u32[]{:S(2)}, u32[]{:S(2)}) collective-permute-start(bf16[6,64,128]{2,1,0:T(8,128)(2,1)S(1)} %pad_maximum_fusion.1), channel_id=1, source_target_pairs={{0,2},{1,3},{2,0},{3,1},{4,6},{5,7},{6,4},{7,5},{8,10},{9,11},{10,... | collective-permute-start | bytes 294920 | tf_op jit(solution)/shard_map/ppermute | solution.py:201
  59.9 1.5 collective-permute-start.11
  61.4 0.8 collective-permute-done.7.refs_2_.refs_9_
  62.1 15.1 %in_grad_there.1 = (bf16[256,2048]{1,0:T(8,128)(2,1)}, bf16[256,2048]{1,0:T(8,128)(2,1)}, bf16[256,2048]{1,0:T(8,128)(2,1)}, bf16[256,2048]{1,0:T(8,128)(2,1)}) custom-call(s32[4]{0:T(128)} %pad_add_fusion.refs_0_, bf16[256,4096]{1,0:T(8,128)(2,1)} %collective-permute-done.refs_1_.refs_8_, bf16[256,4096]{1,0:T(8,128)(2,1)} %collective-permute-done.7.refs_2_.refs_9_, ...), custom_call_target="tpu_custom_call" | custom-call | flops 1 | bytes 1 | tf_op jit(solution)/shard_map/in_grad_there/pallas_call | solution.py:81
  77.3 0.0 collective-permute-done.8
  77.3 0.0 collective-permute-done.9.refs_2_
  77.3 2.8 %collective-permute-start.10 = (bf16[256,2048]{1,0:T(8,128)(2,1)}, bf16[256,2048]{1,0:T(8,128)(2,1)}, u32[]{:S(2)}, u32[]{:S(2)}) collective-permute-start(bf16[256,2048]{1,0:T(8,128)(2,1)} %get-tuple-element.74.refs_6_.refs_1_), channel_id=1, source_target_pairs={{0,1},{1,0},{2,3},{3,2},{4,5},{5,4},{6,7},{7,6},{8,9},{9,8},{10,11... | collective-permute-start | bytes 3145736 | tf_op jit(solution)/shard_map/ppermute | solution.py:201
  80.1 0.0 copy-start.1
  80.1 0.4 collective-permute-start.14
  80.5 1.2 collective-permute-start.13
  81.8 0.3 collective-permute-start.12
  82.1 4.2 %sums_near.1.refs_7_.refs_1_.refs_2_ = bf16[256,4096]{1,0:T(8,128)(2,1)} custom-call(s32[4]{0:T(128)} %pad_add_fusion.refs_0_, bf16[256,4096]{1,0:T(8,128)(2,1)} %get-tuple-element.68.refs_6_.refs_1_, bf16[256,4096]{1,0:T(8,128)(2,1)} %collective-permute-done.9.refs_2_), custom_call_target="tpu_custom_call" | custom-call | flops 1 | bytes 1 | tf_op jit(solution)/shard_map/sums_near/pallas_call | solution.py:177
  86.2 2.8 %collective-permute-done.11.refs_4_ = bf16[256,2048]{1,0:T(8,128)(2,1)} collective-permute-done((bf16[256,2048]{1,0:T(8,128)(2,1)}, bf16[256,2048]{1,0:T(8,128)(2,1)}, u32[]{:S(2)}, u32[]{:S(2)}) %collective-permute-start.11) | collective-permute-done | bytes 1048608 | tf_op jit(solution)/shard_map/ppermute | solution.py:201
  89.0 14.2 %outputs_far.1 = (bf16[256,4096]{1,0:T(8,128)(2,1)}, bf16[256,4096]{1,0:T(8,128)(2,1)}, bf16[2,256,2048]{2,1,0:T(8,128)(2,1)}) custom-call(s32[4]{0:T(128)} %pad_add_fusion.refs_0_, bf16[256,2048]{1,0:T(8,128)(2,1)} %collective-permute-done.2.refs_1_, bf16[256,2048]{1,0:T(8,128)(2,1)} %collective-permute-done.6.refs_2_, ...), custom_call_target="tpu_custom_call" | custom-call | flops 1 | bytes 1 | tf_op jit(solution)/shard_map/outputs_far/pallas_call | solution.py:81
  103.2 0.0 collective-permute-done.14.refs_4_
  103.3 0.0 collective-permute-done.13.refs_3_
  103.3 0.0 collective-permute-done.12.refs_2_
  103.3 0.6 copy-done.3
  103.9 0.1 copy-done.4
  104.0 0.7 copy-done.5
  104.6 2.2 %clip_factor.1.refs_1_ = f32[1024,1]{1,0:T(8,128)} custom-call(s32[4]{0:T(128)} %pad_add_fusion.refs_0_, bf16[10,64,128]{2,1,0:T(8,128)(2,1)} %copy-done.1, bf16[10,64,128]{2,1,0:T(8,128)(2,1)} %copy-done.5, bf16[10,64,128]{2,1,0:T(8,128)(2,1)} %copy-done.4, bf16[10,64,128]{2,1,0:T(8,128)(2,1)} %copy-done.3), custom_call_target="tpu_custom_call" | custom-call | flops 1 | bytes 1 | tf_op jit(solution)/shard_map/clip_factor/pallas_call | solution.py:249
  106.8 3.7 %collective-permute-done.10.refs_2_ = bf16[256,2048]{1,0:T(8,128)(2,1)} collective-permute-done((bf16[256,2048]{1,0:T(8,128)(2,1)}, bf16[256,2048]{1,0:T(8,128)(2,1)}, u32[]{:S(2)}, u32[]{:S(2)}) %collective-permute-start.10) | collective-permute-done | bytes 1048608 | tf_op jit(solution)/shard_map/ppermute | solution.py:201
  110.5 0.0 collective-permute-start.15
  110.5 0.0 collective-permute-start.17
  110.5 3.1 %sums_now.1 = bf16[256,2048]{1,0:T(8,128)(2,1)} custom-call(s32[4]{0:T(128)} %pad_add_fusion.refs_0_, bf16[256,2048]{1,0:T(8,128)(2,1)} %get-tuple-element.74.refs_6_.refs_1_, bf16[256,2048]{1,0:T(8,128)(2,1)} %collective-permute-done.10.refs_2_), custom_call_target="tpu_custom_call" | custom-call | flops 1 | bytes 1 | tf_op jit(solution)/shard_map/sums_now/pallas_call | solution.py:177
  113.6 1.4 collective-permute-done.15.refs_3_.refs_4_
  115.0 0.1 collective-permute-start.16
  115.2 4.5 %sums_others.1.refs_11_ = bf16[256,4096]{1,0:T(8,128)(2,1)} custom-call(s32[4]{0:T(128)} %pad_add_fusion.refs_0_, bf16[256,4096]{1,0:T(8,128)(2,1)} %sums_near.1.refs_7_.refs_1_.refs_2_, bf16[256,4096]{1,0:T(8,128)(2,1)} %get-tuple-element.86.refs_2_.refs_3_, bf16[256,4096]{1,0:T(8,128)(2,1)} %collective-permute-done.15.refs_3_.refs_4_), custom_call_target="tpu_custom_call" | custom-call | flops 1 | bytes 1 | tf_op jit(solution)/shard_map/sums_others/pallas_call | solution.py:177
  119.7 1.3 collective-permute-start.20
  121.0 19.7 %update.2.refs_11_ = f32[2048,4096]{1,0:T(8,128)} custom-call(s32[4]{0:T(128)} %pad_add_fusion.refs_0_, f32[1024,1]{1,0:T(8,128)} %clip_factor.1.refs_1_, bf16[256,2048]{1,0:T(8,128)(2,1)} %refs_2_.3, bf16[256,2048]{1,0:T(8,128)(2,1)} %collective-permute-done.1.refs_2_.refs_3_, bf16[2,256,2048]{2,1,0:T(8,128)(2,1)} %get-tuple-element.85.refs_4_.refs_5_, ...), custom_call_target="tpu_custom_call" | custom-call | flops 1 | bytes 1 | tf_op jit(solution)/shard_map/update/pallas_call | solution.py:147
  140.7 0.0 collective-permute-done.17.refs_4_
  140.7 0.0 collective-permute-done.16.refs_2_
  140.7 4.0 %sums_later.1 = (bf16[256,2048]{1,0:T(8,128)(2,1)}, bf16[256,2048]{1,0:T(8,128)(2,1)}) custom-call(s32[4]{0:T(128)} %pad_add_fusion.refs_0_, bf16[256,2048]{1,0:T(8,128)(2,1)} %get-tuple-element.69.refs_1_, bf16[256,2048]{1,0:T(8,128)(2,1)} %collective-permute-done.16.refs_2_, bf16[256,2048]{1,0:T(8,128)(2,1)} %get-tuple-element.83.refs_3_, ...), custom_call_target="tpu_custom_call" | custom-call | flops 1 | bytes 1 | tf_op jit(solution)/shard_map/sums_later/pallas_call | solution.py:177
  144.7 1.8 %collective-permute-start.18 = (bf16[256,2048]{1,0:T(8,128)(2,1)}, bf16[256,2048]{1,0:T(8,128)(2,1)}, u32[]{:S(2)}, u32[]{:S(2)}) collective-permute-start(bf16[256,2048]{1,0:T(8,128)(2,1)} %get-tuple-element.90), channel_id=1, source_target_pairs={{0,1},{1,0},{2,3},{3,2},{4,5},{5,4},{6,7},{7,6},{8,9},{9,8},{10,11... | collective-permute-start | bytes 3145736 | tf_op jit(solution)/shard_map/ppermute | solution.py:201
  146.5 19.9 %update.3 = f32[2048,4096]{1,0:T(8,128)} custom-call(s32[4]{0:T(128)} %pad_add_fusion.refs_0_, f32[1024,1]{1,0:T(8,128)} %clip_factor.1.refs_1_, bf16[256,2048]{1,0:T(8,128)(2,1)} %refs_2_.3, bf16[256,2048]{1,0:T(8,128)(2,1)} %collective-permute-done.1.refs_2_.refs_3_, ...), custom_call_target="tpu_custom_call", output_to_operand_aliasing={{}: (11, {})} | custom-call | flops 1 | bytes 1 | tf_op jit(solution)/shard_map/update/pallas_call | solution.py:147
  166.5 1.5 collective-permute-done.20.refs_1_
  167.9 5.0 %sums_outputs.1 = bf16[256,4096]{1,0:T(8,128)(2,1)} custom-call(s32[4]{0:T(128)} %pad_add_fusion.refs_0_, bf16[256,4096]{1,0:T(8,128)(2,1)} %collective-permute-done.20.refs_1_, bf16[256,4096]{1,0:T(8,128)(2,1)} %sums_near.1.refs_7_.refs_1_.refs_2_, bf16[256,4096]{1,0:T(8,128)(2,1)} %get-tuple-element.86.refs_2_.refs_3_, ...), custom_call_target="tpu_custom_call" | custom-call | flops 1 | bytes 1 | tf_op jit(solution)/shard_map/sums_outputs/pallas_call | solution.py:177
  172.9 3.5 %sums_in_grad.1 = bf16[256,2048]{1,0:T(8,128)(2,1)} custom-call(s32[4]{0:T(128)} %pad_add_fusion.refs_0_, bf16[256,2048]{1,0:T(8,128)(2,1)} %get-tuple-element.95.refs_1_, bf16[256,2048]{1,0:T(8,128)(2,1)} %collective-permute-done.18.refs_2_, bf16[256,2048]{1,0:T(8,128)(2,1)} %collective-permute-done.19.refs_3_), custom_call_target="tpu_custom_call" | custom-call | flops 1 | bytes 1 | tf_op jit(solution)/shard_map/sums_in_grad/pallas_call | solution.py:177
  (17 shorter events, 0.1 us)
Async XLA Ops:
  0.6 8.2 %copy-start = (bf16[256,4096]{1,0:T(8,128)(2,1)S(1)}, bf16[256,4096]{1,0:T(8,128)(2,1)}, u32[]{:S(2)}) copy-start(bf16[256,4096]{1,0:T(8,128)(2,1)} %refs_6_.3) | copy-start | bytes 6291460
  0.6 10.5 %collective-permute-start.4 = (bf16[256,4096]{1,0:T(8,128)(2,1)}, bf16[256,4096]{1,0:T(8,128)(2,1)}, u32[]{:S(2)}, u32[]{:S(2)}) collective-permute-start(bf16[256,4096]{1,0:T(8,128)(2,1)} %refs_6_.3), channel_id=1, source_target_pairs={{0,4},{4,0},{8,12},{12,8},{1,5},{5,1},{9,13},{13,9},{2,6},{6,2},{1... | collective-permute-start | bytes 6291464 | tf_op jit(solution)/shard_map/ppermute | solution.py:214
  1.2 29.4 %collective-permute-start.2 = (bf16[256,2048]{1,0:T(8,128)(2,1)}, bf16[256,2048]{1,0:T(8,128)(2,1)}, u32[]{:S(2)}, u32[]{:S(2)}) collective-permute-start(bf16[256,2048]{1,0:T(8,128)(2,1)} %refs_2_.3), channel_id=1, source_target_pairs={{0,4},{1,2},{2,1},{3,7},{4,0},{5,6},{6,5},{7,3},{8,12},{9,10},{10,... | collective-permute-start | bytes 3145736 | tf_op jit(solution)/shard_map/ppermute | solution.py:210
  1.2 29.3 %collective-permute-start.1 = (bf16[256,2048]{1,0:T(8,128)(2,1)}, bf16[256,2048]{1,0:T(8,128)(2,1)}, u32[]{:S(2)}, u32[]{:S(2)}) collective-permute-start(bf16[256,2048]{1,0:T(8,128)(2,1)} %refs_2_.3), channel_id=1, source_target_pairs={{0,1},{1,0},{2,3},{3,2},{4,5},{5,4},{6,7},{7,6},{8,9},{9,8},{10,11... | collective-permute-start | bytes 3145736 | tf_op jit(solution)/shard_map/ppermute | solution.py:201
  5.4 52.1 %collective-permute-start = (bf16[256,4096]{1,0:T(8,128)(2,1)}, bf16[256,4096]{1,0:T(8,128)(2,1)}, u32[]{:S(2)}, u32[]{:S(2)}) collective-permute-start(bf16[256,4096]{1,0:T(8,128)(2,1)} %refs_6_.3), channel_id=1, source_target_pairs={{0,8},{4,12},{8,0},{12,4},{1,9},{5,13},{9,1},{13,5},{2,10},{6,14},... | collective-permute-start | bytes 6291464 | tf_op jit(solution)/shard_map/ppermute | solution.py:214
  9.7 20.9 %collective-permute-start.3 = (bf16[4,64,128]{2,1,0:T(8,128)(2,1)S(1)}, bf16[4,64,128]{2,1,0:T(8,128)(2,1)S(1)}, u32[]{:S(2)}, u32[]{:S(2)}) collective-permute-start(bf16[4,64,128]{2,1,0:T(8,128)(2,1)S(1)} %maximum_maximum_fusion), channel_id=1, source_target_pairs={{0,1},{1,0},{2,3},{3,2},{4,5},{5,4},{6,7},{7,6},{8,9},{9,8},{10,11... | collective-permute-start | bytes 196616 | tf_op jit(solution)/shard_map/ppermute | solution.py:201
  30.5 26.9 %collective-permute-start.6 = (bf16[256,2048]{1,0:T(8,128)(2,1)}, bf16[256,2048]{1,0:T(8,128)(2,1)}, u32[]{:S(2)}, u32[]{:S(2)}) collective-permute-start(bf16[256,2048]{1,0:T(8,128)(2,1)} %collective-permute-done.2.refs_1_), channel_id=1, source_target_pairs={{0,1},{1,0},{2,3},{3,2},{4,5},{5,4},{6,7},{7,6},{8,9},{9,8},{10,11... | collective-permute-start | bytes 3145736 | tf_op jit(solution)/shard_map/ppermute | solution.py:201
  32.2 25.2 %collective-permute-start.5 = (bf16[256,2048]{1,0:T(8,128)(2,1)}, bf16[256,2048]{1,0:T(8,128)(2,1)}, u32[]{:S(2)}, u32[]{:S(2)}) collective-permute-start(bf16[256,2048]{1,0:T(8,128)(2,1)} %collective-permute-done.1.refs_2_.refs_3_), channel_id=1, source_target_pairs={{0,4},{1,2},{2,1},{3,7},{4,0},{5,6},{6,5},{7,3},{8,12},{9,10},{10,... | collective-permute-start | bytes 3145736 | tf_op jit(solution)/shard_map/ppermute | solution.py:210
  43.9 14.2 %copy-start.2 = (bf16[2,64,128]{2,1,0:T(8,128)(2,1)S(1)}, bf16[2,64,128]{2,1,0:T(8,128)(2,1)}, u32[]{:S(2)}) copy-start(bf16[2,64,128]{2,1,0:T(8,128)(2,1)} %pad_maximum_fusion.3.refs_4_.refs_7_) | copy-start | bytes 98308
  57.5 4.7 %collective-permute-start.7 = (bf16[256,4096]{1,0:T(8,128)(2,1)}, bf16[256,4096]{1,0:T(8,128)(2,1)}, u32[]{:S(2)}, u32[]{:S(2)}) collective-permute-start(bf16[256,4096]{1,0:T(8,128)(2,1)} %collective-permute-done.refs_1_.refs_8_), channel_id=1, source_target_pairs={{0,4},{4,0},{8,12},{12,8},{1,5},{5,1},{9,13},{13,9},{2,6},{6,2},{1... | collective-permute-start | bytes 6291464 | tf_op jit(solution)/shard_map/ppermute | solution.py:214
  58.0 19.3 %collective-permute-start.9 = (bf16[256,4096]{1,0:T(8,128)(2,1)}, bf16[256,4096]{1,0:T(8,128)(2,1)}, u32[]{:S(2)}, u32[]{:S(2)}) collective-permute-start(bf16[256,4096]{1,0:T(8,128)(2,1)} %get-tuple-element.73), channel_id=1, source_target_pairs={{0,4},{4,0},{8,12},{12,8},{1,5},{5,1},{9,13},{13,9},{2,6},{6,2},{1... | collective-permute-start | bytes 6291464 | tf_op jit(solution)/shard_map/ppermute | solution.py:214
  58.1 19.2 %collective-permute-start.8 = (bf16[6,64,128]{2,1,0:T(8,128)(2,1)S(1)}, bf16[6,64,128]{2,1,0:T(8,128)(2,1)S(1)}, u32[]{:S(2)}, u32[]{:S(2)}) collective-permute-start(bf16[6,64,128]{2,1,0:T(8,128)(2,1)S(1)} %pad_maximum_fusion.1), channel_id=1, source_target_pairs={{0,2},{1,3},{2,0},{3,1},{4,6},{5,7},{6,4},{7,5},{8,10},{9,11},{10,... | collective-permute-start | bytes 294920 | tf_op jit(solution)/shard_map/ppermute | solution.py:201
  59.9 29.1 %collective-permute-start.11 = (bf16[256,2048]{1,0:T(8,128)(2,1)}, bf16[256,2048]{1,0:T(8,128)(2,1)}, u32[]{:S(2)}, u32[]{:S(2)}) collective-permute-start(bf16[256,2048]{1,0:T(8,128)(2,1)} %collective-permute-done.5.refs_3_), channel_id=1, source_target_pairs={{1,0},{2,3},{5,4},{6,7},{9,8},{10,11},{13,12},{14,15},{17,16},{18,... | collective-permute-start | bytes 3145736 | tf_op jit(solution)/shard_map/ppermute | solution.py:201
  77.3 33.2 %collective-permute-start.10 = (bf16[256,2048]{1,0:T(8,128)(2,1)}, bf16[256,2048]{1,0:T(8,128)(2,1)}, u32[]{:S(2)}, u32[]{:S(2)}) collective-permute-start(bf16[256,2048]{1,0:T(8,128)(2,1)} %get-tuple-element.74.refs_6_.refs_1_), channel_id=1, source_target_pairs={{0,1},{1,0},{2,3},{3,2},{4,5},{5,4},{6,7},{7,6},{8,9},{9,8},{10,11... | collective-permute-start | bytes 3145736 | tf_op jit(solution)/shard_map/ppermute | solution.py:201
  80.1 6.1 %copy-start.1 = (bf16[10,64,128]{2,1,0:T(8,128)(2,1)}, bf16[10,64,128]{2,1,0:T(8,128)(2,1)S(1)}, u32[]{:S(2)}) copy-start(bf16[10,64,128]{2,1,0:T(8,128)(2,1)S(1)} %pad_maximum_fusion.refs_1_) | copy-start | bytes 491524
  80.1 23.1 %collective-permute-start.14 = (bf16[10,64,128]{2,1,0:T(8,128)(2,1)S(1)}, bf16[10,64,128]{2,1,0:T(8,128)(2,1)S(1)}, u32[]{:S(2)}, u32[]{:S(2)}) collective-permute-start(bf16[10,64,128]{2,1,0:T(8,128)(2,1)S(1)} %pad_maximum_fusion.refs_1_), channel_id=1, source_target_pairs={{0,12},{4,8},{8,4},{12,0},{1,13},{5,9},{9,5},{13,1},{2,14},{6,10},... | collective-permute-start | bytes 491528 | tf_op jit(solution)/shard_map/ppermute | solution.py:214
  80.5 22.7 %collective-permute-start.13 = (bf16[10,64,128]{2,1,0:T(8,128)(2,1)S(1)}, bf16[10,64,128]{2,1,0:T(8,128)(2,1)S(1)}, u32[]{:S(2)}, u32[]{:S(2)}) collective-permute-start(bf16[10,64,128]{2,1,0:T(8,128)(2,1)S(1)} %pad_maximum_fusion.refs_1_), channel_id=1, source_target_pairs={{0,8},{4,12},{8,0},{12,4},{1,9},{5,13},{9,1},{13,5},{2,10},{6,14},... | collective-permute-start | bytes 491528 | tf_op jit(solution)/shard_map/ppermute | solution.py:214
  81.8 21.5 %collective-permute-start.12 = (bf16[10,64,128]{2,1,0:T(8,128)(2,1)S(1)}, bf16[10,64,128]{2,1,0:T(8,128)(2,1)S(1)}, u32[]{:S(2)}, u32[]{:S(2)}) collective-permute-start(bf16[10,64,128]{2,1,0:T(8,128)(2,1)S(1)} %pad_maximum_fusion.refs_1_), channel_id=1, source_target_pairs={{0,4},{4,0},{8,12},{12,8},{1,5},{5,1},{9,13},{13,9},{2,6},{6,2},{1... | collective-permute-start | bytes 491528 | tf_op jit(solution)/shard_map/ppermute | solution.py:214
  103.2 0.7 copy-start.3
  103.3 0.7 copy-start.4
  104.0 0.7 copy-start.5
  110.5 4.5 %collective-permute-start.15 = (bf16[256,4096]{1,0:T(8,128)(2,1)}, bf16[256,4096]{1,0:T(8,128)(2,1)}, u32[]{:S(2)}, u32[]{:S(2)}) collective-permute-start(bf16[256,4096]{1,0:T(8,128)(2,1)} %get-tuple-element.80), channel_id=1, source_target_pairs={{0,4},{4,0},{8,12},{12,8},{1,5},{5,1},{9,13},{13,9},{2,6},{6,2},{1... | collective-permute-start | bytes 6291464 | tf_op jit(solution)/shard_map/ppermute | solution.py:214
  110.5 30.1 %collective-permute-start.17 = (bf16[256,2048]{1,0:T(8,128)(2,1)}, bf16[256,2048]{1,0:T(8,128)(2,1)}, u32[]{:S(2)}, u32[]{:S(2)}) collective-permute-start(bf16[256,2048]{1,0:T(8,128)(2,1)} %get-tuple-element.83.refs_3_), channel_id=1, source_target_pairs={{0,1},{1,0},{2,3},{3,2},{4,5},{5,4},{6,7},{7,6},{8,9},{9,8},{10,11... | collective-permute-start | bytes 3145736 | tf_op jit(solution)/shard_map/ppermute | solution.py:201
  115.0 25.7 %collective-permute-start.16 = (bf16[256,2048]{1,0:T(8,128)(2,1)}, bf16[256,2048]{1,0:T(8,128)(2,1)}, u32[]{:S(2)}, u32[]{:S(2)}) collective-permute-start(bf16[256,2048]{1,0:T(8,128)(2,1)} %sums_now.1), channel_id=1, source_target_pairs={{0,4},{1,2},{2,1},{3,7},{4,0},{5,6},{6,5},{7,3},{8,12},{9,10},{10,... | collective-permute-start | bytes 3145736 | tf_op jit(solution)/shard_map/ppermute | solution.py:210
  119.7 48.2 %collective-permute-start.20 = (bf16[256,4096]{1,0:T(8,128)(2,1)}, bf16[256,4096]{1,0:T(8,128)(2,1)}, u32[]{:S(2)}, u32[]{:S(2)}) collective-permute-start(bf16[256,4096]{1,0:T(8,128)(2,1)} %sums_others.1.refs_11_), channel_id=1, source_target_pairs={{0,8},{4,12},{8,0},{12,4},{1,9},{5,13},{9,1},{13,5},{2,10},{6,14},... | collective-permute-start | bytes 6291464 | tf_op jit(solution)/shard_map/ppermute | solution.py:214
  144.7 28.2 %collective-permute-start.18 = (bf16[256,2048]{1,0:T(8,128)(2,1)}, bf16[256,2048]{1,0:T(8,128)(2,1)}, u32[]{:S(2)}, u32[]{:S(2)}) collective-permute-start(bf16[256,2048]{1,0:T(8,128)(2,1)} %get-tuple-element.90), channel_id=1, source_target_pairs={{0,1},{1,0},{2,3},{3,2},{4,5},{5,4},{6,7},{7,6},{8,9},{9,8},{10,11... | collective-permute-start | bytes 3145736 | tf_op jit(solution)/shard_map/ppermute | solution.py:201
  146.5 26.4 %collective-permute-start.19 = (bf16[256,2048]{1,0:T(8,128)(2,1)}, bf16[256,2048]{1,0:T(8,128)(2,1)}, u32[]{:S(2)}, u32[]{:S(2)}) collective-permute-start(bf16[256,2048]{1,0:T(8,128)(2,1)} %get-tuple-element.91), channel_id=1, source_target_pairs={{0,4},{1,2},{2,1},{3,7},{4,0},{5,6},{6,5},{7,3},{8,12},{9,10},{10,... | collective-permute-start | bytes 3145736 | tf_op jit(solution)/shard_map/ppermute | solution.py:210

commit v4 on v3

--- a/solution.py
+++ b/solution.py
@@ -194,6 +194,7 @@
 
 
 OUTER = [(0, 1), (1, 0), (2, 3), (3, 2)]
+INWARD = [(0, 1), (3, 2)]
 OUTWARD = [(1, 0), (2, 3)]
 
 
@@ -219,9 +220,30 @@
     return jnp.einsum("bsd,btd->bst", blocks, blocks, preferred_element_type=F32)
 
 
-def gram_pairs(rows):
-    blocks = gram(rows).astype(BF16)
-    return jnp.concatenate([blocks[0::2], blocks[1::2]], axis=2)
+def gram_kernel(*refs):
+    *arrays, out = refs
+    pairs = out.shape[0] // len(arrays)
+    for i, rows in enumerate(arrays):
+        for e in range(2 * pairs):
+            block = rows[e * SEQ : (e + 1) * SEQ, :]
+            square = lax.dot_general(
+                block, block, (((1,), (1,)), ((), ())), preferred_element_type=F32
+            )
+            side = e % 2 * SEQ
+            out[i * pairs + e // 2, :, side : side + SEQ] = square.astype(BF16)
+
+
+def gram_pairs(*arrays):
+    pairs = arrays[0].shape[0] // SEQ // 2
+    return pl.pallas_call(
+        gram_kernel,
+        in_specs=[pl.BlockSpec(memory_space=pltpu.VMEM)] * len(arrays),
+        out_specs=pl.BlockSpec(memory_space=pltpu.VMEM),
+        out_shape=jax.ShapeDtypeStruct((len(arrays) * pairs, SEQ, 2 * SEQ), BF16),
+        compiler_params=pltpu.CompilerParams(vmem_limit_bytes=VMEM),
+        cost_estimate=BRIEF,
+        name="gram",
+    )(*arrays)
 
 
 def factor_kernel(clip, pairs, n, at, *refs):
@@ -274,10 +296,11 @@
     g_far = swap(out_grad, 2)
     x_side = along(inputs, OUTER)
     x_mid = middle(inputs)
-    features, units = gram_pairs(inputs), gram_pairs(out_grad)
-    pairs = features.shape[0]
-    grams = along(jnp.concatenate([features, units]), OUTER)
-    weight, g_side, features, units = hold((weight, g_side, features, units))
+    grams = gram_pairs(inputs, out_grad)
+    pairs = grams.shape[0] // 2
+    features, units = grams[:pairs], grams[pairs:]
+    weight, g_side, first_grams = hold((weight, g_side, grams))
+    grams = along(grams, OUTER)
 
 
     def out_grad_rows(half):
@@ -325,14 +348,14 @@
 
     def rows_here(share, before):
         return pair_matmul(
-            at, [out_grad, g_side], weight, out_grad_rows(lambda at: at[1]), True, plainly, 2, [], [units],
+            at, [out_grad, g_side], weight, out_grad_rows(lambda at: at[1]), True, plainly, 2, [], [first_grams],
             "in_grad_here", share=share, before=before,
         )
 
-    x_side, x_mid, grams, *qa = hold((x_side, x_mid, grams, *rows_here((0, 5), ())))
+    x_side, x_mid, grams, *qa = hold((x_side, x_mid, grams, *rows_here((0, 6), ())))
     x_mid2 = middle(x_side)
     x_out = along(x_mid, OUTER)
-    qa0, qa1, w = rows_here((5, 8), qa)
+    qa0, qa1, w = rows_here((6, 8), qa)
     pa0, pa1 = pair_matmul(
         at, [inputs, x_side], w, near_rows, False, plainly, 2, [], [], "outputs_near"
     )
@@ -352,16 +375,15 @@
         [features, grams[: 2 * pairs], plus(units, grams[2 * pairs :])]
     )
     others = [swap(grams, j) for j in range(1, n)]
-    r1a = along(first, OUTER)
+    r1a = along(first, INWARD)
 
     def two(at, refs, outs):
         outs[0][...] = total(*refs).astype(BF16)
 
     narrow, wide = first.shape, pa0.shape
-    (near_sum,) = add_up(at, two, [pa0, pa1], [], [wide], 2, "sums_near")
     pb0, pb1, x_far = pair_matmul(
         at, [x_mid, x_out, x_mid2, x_out2], w, far_rows, False, plainly, 2,
-        [], [first, near_sum], "outputs_far", keep=True,
+        [], [first], "outputs_far", keep=True,
     )
     factor = make_factor(at, [grams, *others], clip, pairs, tokens)
     r1a, pb1, factor = hold((r1a, pb1, factor))
@@ -372,9 +394,11 @@
     r2a = middle(r2a)
     r1b = along(second, OUTER)
 
+    def either(cond, pair, other):
+        return jnp.where(cond, total(*pair), total(*other))
+
     def for_others(at, refs, outs):
-        far = total(refs[1], refs[2])
-        outs[0][...] = jnp.where(at[0] == at[1], far, refs[0][...].astype(F32)).astype(BF16)
+        outs[0][...] = either(at[0] == at[1], refs[2:], refs[:2]).astype(BF16)
 
     def if_same(at):
         return at[0] == at[1]
@@ -383,7 +407,7 @@
         return at[0] != at[1]
 
     (other,) = add_up(
-        at, for_others, [], [(if_other, near_sum), (if_same, pb0), (if_same, pb1)],
+        at, for_others, [], [(if_other, pa0), (if_other, pa1), (if_same, pb0), (if_same, pb1)],
         [wide], 2, "sums_others",
     )
     theirs = swap(other, 2)
@@ -396,7 +420,7 @@
         outs[1][...] = total(refs[2], refs[3]).astype(BF16)
 
     def last_outputs(at, refs, outs):
-        mine = jnp.where(at[0] == at[1], refs[1][...].astype(F32), total(*refs[2:]))
+        mine = either(at[0] == at[1], refs[1:3], refs[3:])
         outs[0][...] = (mine + refs[0][...].astype(F32)).astype(BF16)
 
     def last_in_grad(at, refs, outs):
@@ -421,8 +445,8 @@
     update = make_update(at, xs, gs, *facts, 1, 2, update)
     theirs, update = hold((theirs, update))
     (outputs,) = add_up(
-        at, last_outputs, [theirs], [(if_same, near_sum), (if_other, pb0), (if_other, pb1)],
-        [wide], 2, "sums_outputs",
+        at, last_outputs, [theirs],
+        [(if_same, pa0), (if_same, pa1), (if_other, pb0), (if_other, pb1)], [wide], 2, "sums_outputs",
     )
     r3, r2b, outputs = hold((r3, r2b, outputs))
     (in_grad,) = add_up(at, last_in_grad, [own, r3, r2b], [], [narrow], 2, "sums_in_grad")

time: 177 us -> 172 us (0.972)
  starting transfers between devices: 19.8 us -> 25.6 us
  waiting for transfers between devices: 12.6 us -> 7.49 us
  Pallas kernels: 138 us -> 135 us
  matrix products: 2.64 us -> 0 us
    ppermute x8, starting transfers between devices: 13.7 us -> 19.4 us  [along(): return lax.ppermute(value, 'hidden', pairs)]
    pallas_call x0 -> x1, Pallas kernels: none -> 3.57 us  [gram_pairs(): pl.pallas_call(gram_kernel, in_specs=[pl.BlockSpec(memory_space=pltpu.VME...]
    pallas_call x6 -> x5, Pallas kernels: 24.3 us -> 21.3 us  [add_up(): pl.pallas_call(lambda *refs: add_kernel(sums, len(arrays) + len(chosen),...]
    ppermute x8, waiting for transfers between devices: 9.01 us -> 6.04 us  [along(): return lax.ppermute(value, 'hidden', pairs)]
    dot_general x2 -> x0, matrix products: 2.64 us -> none  [gram(): jnp.einsum('bsd,btd->bst', blocks, blocks, preferred_element_type=F32)]
    pallas_call x5, Pallas kernels: 71.4 us -> 69 us  [pair_matmul(): pl.pallas_call(kernel, grid=(steps,), in_specs=[pl.BlockSpec(memory_space...]
    ppermute x9, waiting for transfers between devices: 3.62 us -> 1.44 us  [swap(): return lax.ppermute(value, 'mp', [(i, i ^ bit) for i in range(4)])]
  transfers between devices with their start and end apart: 21 -> 21, of which waited for: 6 -> 5; matrix products, arithmetic and copies ran while one was open for 2% -> 0% of each run, Pallas kernels for 76% -> 77%
where the time goes in v4:
time: 172 us; the launch traced here: 171 us
  Pallas kernels  135 us (78%)
  starting transfers between devices  25.6 us (15%)
  waiting for transfers between devices  7.49 us (4%)
    pallas_call x5, Pallas kernels, pair_matmul(): pl.pallas_call(kernel, grid=(steps,), in_specs=[pl.BlockSpec(memory_space...  69 us
    pallas_call x2, Pallas kernels, make_update(): pl.pallas_call(kernel, grid=(depth // tile,), in_specs=[pl.BlockSpec(memo...  39.4 us
    pallas_call x5, Pallas kernels, add_up(): pl.pallas_call(lambda *refs: add_kernel(sums, len(arrays) + len(chosen),...  21.3 us
    ppermute x8, starting transfers between devices, along(): return lax.ppermute(value, 'hidden', pairs)  19.4 us
    ppermute x8, waiting for transfers between devices, along(): return lax.ppermute(value, 'hidden', pairs)  6.04 us
    ppermute x9, starting transfers between devices, swap(): return lax.ppermute(value, 'mp', [(i, i ^ bit) for i in range(4)])  5.94 us
    pallas_call x1, Pallas kernels, gram_pairs(): pl.pallas_call(gram_kernel, in_specs=[pl.BlockSpec(memory_space=pltpu.VME...  3.57 us
  transfers between devices with their start and end apart: 21, of which 5 were waited for; matrix products, arithmetic and copies ran while one was open for 0% of the time, Pallas kernels for 77%

profile of v4, /device:TPU:0, one launch (start us, length us, event | category | flops | bytes accessed | tf_op | source)
XLA Modules:
  0.0 171.3 jit_solution(7067633005267649918)
XLA Ops:
  0.6 0.5 collective-permute-start.4
  1.1 0.1 collective-permute-start.2
  1.2 4.1 %collective-permute-start.1 = (bf16[256,2048]{1,0:T(8,128)(2,1)}, bf16[256,2048]{1,0:T(8,128)(2,1)}, u32[]{:S(2)}, u32[]{:S(2)}) collective-permute-start(bf16[256,2048]{1,0:T(8,128)(2,1)} %refs_2_.3), channel_id=1, source_target_pairs={{0,1},{1,0},{2,3},{3,2},{4,5},{5,4},{6,7},{7,6},{8,9},{9,8},{10,11... | collective-permute-start | bytes 3145736 | tf_op jit(solution)/shard_map/ppermute | solution.py:202
  5.4 1.5 collective-permute-start
  6.9 3.6 %gram.1.refs_4_.refs_7_ = bf16[4,64,128]{2,1,0:T(8,128)(2,1)} custom-call(bf16[256,2048]{1,0:T(8,128)(2,1)} %refs_2_.3, bf16[256,4096]{1,0:T(8,128)(2,1)} %refs_6_.3), custom_call_target="tpu_custom_call" | custom-call | flops 1 | bytes 1 | tf_op jit(solution)/shard_map/gram/pallas_call | solution.py:238
  10.4 0.0 collective-permute-start.3
  10.4 0.6 pad_add_fusion.refs_0_
  11.0 0.0 collective-permute-done.4.refs_2_.refs_7_
  11.0 18.3 %in_grad_here.2 = (bf16[256,2048]{1,0:T(8,128)(2,1)}, bf16[256,2048]{1,0:T(8,128)(2,1)}, bf16[2048,4096]{1,0:T(8,128)(2,1)}) custom-call(s32[4]{0:T(128)} %pad_add_fusion.refs_0_, bf16[256,4096]{1,0:T(8,128)(2,1)} %refs_6_.3, bf16[256,4096]{1,0:T(8,128)(2,1)} %collective-permute-done.4.refs_2_.refs_7_, f32[2048,4096]{1,0:T(8,128)} %refs_3_.1, ...), custom_call_target="tpu_custom_call" | custom-call | flops 1 | bytes 1 | tf_op jit(solution)/shard_map/in_grad_here/pallas_call | solution.py:81
  29.3 1.2 collective-permute-done.3
  30.5 0.0 collective-permute-done.2.refs_1_
  30.5 0.0 collective-permute-done.1.refs_2_.refs_3_
  30.5 1.7 collective-permute-start.6
  32.2 0.0 collective-permute-start.5
  32.2 7.9 %in_grad_here.3 = (bf16[256,2048]{1,0:T(8,128)(2,1)}, bf16[256,2048]{1,0:T(8,128)(2,1)}, bf16[2048,4096]{1,0:T(8,128)(2,1)}) custom-call(s32[4]{0:T(128)} %pad_add_fusion.refs_0_, bf16[256,4096]{1,0:T(8,128)(2,1)} %refs_6_.3, bf16[256,4096]{1,0:T(8,128)(2,1)} %collective-permute-done.4.refs_2_.refs_7_, ...), custom_call_target="tpu_custom_call", output_to_operand_aliasing={{0}: (4, {}), {1}: (5, {}), {2}: (6, {})} | custom-call | flops 1 | bytes 1 | tf_op jit(solution)/shard_map/in_grad_here/pallas_call | solution.py:81
  40.1 13.5 %outputs_near.1 = (bf16[256,4096]{1,0:T(8,128)(2,1)}, bf16[256,4096]{1,0:T(8,128)(2,1)}) custom-call(s32[4]{0:T(128)} %pad_add_fusion.refs_0_, bf16[256,2048]{1,0:T(8,128)(2,1)} %refs_2_.3, bf16[256,2048]{1,0:T(8,128)(2,1)} %collective-permute-done.1.refs_2_.refs_3_, bf16[2048,4096]{1,0:T(8,128)(2,1)} %get-tuple-element.60.refs_3_.refs_5_), custom_call_target="tpu_custom_call" | custom-call | flops 1 | bytes 1 | tf_op jit(solution)/shard_map/outputs_near/pallas_call | solution.py:81
  53.6 0.0 collective-permute-done.refs_1_.refs_8_
  53.6 2.1 %collective-permute-done.6.refs_2_ = bf16[256,2048]{1,0:T(8,128)(2,1)} collective-permute-done((bf16[256,2048]{1,0:T(8,128)(2,1)}, bf16[256,2048]{1,0:T(8,128)(2,1)}, u32[]{:S(2)}, u32[]{:S(2)}) %collective-permute-start.6) | collective-permute-done | bytes 1048608 | tf_op jit(solution)/shard_map/ppermute | solution.py:202
  55.7 0.0 collective-permute-done.5.refs_3_
  55.7 0.0 collective-permute-start.7
  55.7 0.5 collective-permute-start.9
  56.2 0.0 copy-done
  56.2 2.4 %collective-permute-start.8 = (bf16[6,64,128]{2,1,0:T(8,128)(2,1)S(1)}, bf16[6,64,128]{2,1,0:T(8,128)(2,1)S(1)}, u32[]{:S(2)}, u32[]{:S(2)}) collective-permute-start(bf16[6,64,128]{2,1,0:T(8,128)(2,1)S(1)} %pad_maximum_fusion.1), channel_id=1, source_target_pairs={{0,2},{1,3},{2,0},{3,1},{4,6},{5,7},{6,4},{7,5},{8,10},{9,11},{10,... | collective-permute-start | bytes 294920 | tf_op jit(solution)/shard_map/ppermute | solution.py:202
  58.7 1.3 collective-permute-start.11
  60.0 0.2 collective-permute-done.7.refs_2_.refs_9_
  60.2 15.2 %in_grad_there.1 = (bf16[256,2048]{1,0:T(8,128)(2,1)}, bf16[256,2048]{1,0:T(8,128)(2,1)}, bf16[256,2048]{1,0:T(8,128)(2,1)}, bf16[256,2048]{1,0:T(8,128)(2,1)}) custom-call(s32[4]{0:T(128)} %pad_add_fusion.refs_0_, bf16[256,4096]{1,0:T(8,128)(2,1)} %collective-permute-done.refs_1_.refs_8_, bf16[256,4096]{1,0:T(8,128)(2,1)} %collective-permute-done.7.refs_2_.refs_9_, ...), custom_call_target="tpu_custom_call" | custom-call | flops 1 | bytes 1 | tf_op jit(solution)/shard_map/in_grad_there/pallas_call | solution.py:81
  75.3 0.0 collective-permute-done.8
  75.4 0.0 collective-permute-done.9.refs_2_.refs_3_
  75.4 6.4 %collective-permute-start.10 = (bf16[256,2048]{1,0:T(8,128)(2,1)}, bf16[256,2048]{1,0:T(8,128)(2,1)}, u32[]{:S(2)}, u32[]{:S(2)}) collective-permute-start(bf16[256,2048]{1,0:T(8,128)(2,1)} %get-tuple-element.72.refs_6_.refs_1_), channel_id=1, source_target_pairs={{0,1},{3,2},{4,5},{7,6},{8,9},{11,10},{12,13},{15,14},{16,17},{19,... | collective-permute-start | bytes 3145736 | tf_op jit(solution)/shard_map/ppermute | solution.py:202
  81.8 0.0 copy-start.1
  81.8 0.3 collective-permute-start.14
  82.2 1.3 collective-permute-start.13
  83.5 0.3 collective-permute-start.12
  83.8 2.7 %collective-permute-done.11.refs_4_ = bf16[256,2048]{1,0:T(8,128)(2,1)} collective-permute-done((bf16[256,2048]{1,0:T(8,128)(2,1)}, bf16[256,2048]{1,0:T(8,128)(2,1)}, u32[]{:S(2)}, u32[]{:S(2)}) %collective-permute-start.11) | collective-permute-done | bytes 1048608 | tf_op jit(solution)/shard_map/ppermute | solution.py:202
  86.5 14.2 %outputs_far.1 = (bf16[256,4096]{1,0:T(8,128)(2,1)}, bf16[256,4096]{1,0:T(8,128)(2,1)}, bf16[2,256,2048]{2,1,0:T(8,128)(2,1)}) custom-call(s32[4]{0:T(128)} %pad_add_fusion.refs_0_, bf16[256,2048]{1,0:T(8,128)(2,1)} %collective-permute-done.2.refs_1_, bf16[256,2048]{1,0:T(8,128)(2,1)} %collective-permute-done.6.refs_2_, ...), custom_call_target="tpu_custom_call" | custom-call | flops 1 | bytes 1 | tf_op jit(solution)/shard_map/outputs_far/pallas_call | solution.py:81
  100.7 0.0 copy-done.1
  100.7 0.0 collective-permute-done.14.refs_4_
  100.7 0.0 collective-permute-done.13.refs_3_
  100.7 0.0 copy-start.3
  100.7 0.0 collective-permute-done.12.refs_2_
  100.7 0.6 copy-done.2
  101.4 0.1 copy-done.3
  101.4 0.7 copy-done.4
  102.1 2.1 %clip_factor.1.refs_1_ = f32[1024,1]{1,0:T(8,128)} custom-call(s32[4]{0:T(128)} %pad_add_fusion.refs_0_, bf16[10,64,128]{2,1,0:T(8,128)(2,1)} %copy-done.1, bf16[10,64,128]{2,1,0:T(8,128)(2,1)} %copy-done.4, bf16[10,64,128]{2,1,0:T(8,128)(2,1)} %copy-done.3, bf16[10,64,128]{2,1,0:T(8,128)(2,1)} %copy-done.2), custom_call_target="tpu_custom_call" | custom-call | flops 1 | bytes 1 | tf_op jit(solution)/shard_map/clip_factor/pallas_call | solution.py:271
  104.2 0.0 collective-permute-done.10.refs_2_
  104.2 0.0 collective-permute-start.15
  104.2 1.4 collective-permute-start.17
  105.6 3.1 %sums_now.1 = bf16[256,2048]{1,0:T(8,128)(2,1)} custom-call(s32[4]{0:T(128)} %pad_add_fusion.refs_0_, bf16[256,2048]{1,0:T(8,128)(2,1)} %get-tuple-element.72.refs_6_.refs_1_, bf16[256,2048]{1,0:T(8,128)(2,1)} %collective-permute-done.10.refs_2_), custom_call_target="tpu_custom_call" | custom-call | flops 1 | bytes 1 | tf_op jit(solution)/shard_map/sums_now/pallas_call | solution.py:177
  108.7 0.0 collective-permute-done.15.refs_4_.refs_5_
  108.7 0.2 collective-permute-start.16
  109.0 5.0 %sums_others.1.refs_11_ = bf16[256,4096]{1,0:T(8,128)(2,1)} custom-call(s32[4]{0:T(128)} %pad_add_fusion.refs_0_, bf16[256,4096]{1,0:T(8,128)(2,1)} %get-tuple-element.67.refs_6_.refs_1_.refs_2_, bf16[256,4096]{1,0:T(8,128)(2,1)} %collective-permute-done.9.refs_2_.refs_3_, bf16[256,4096]{1,0:T(8,128)(2,1)} %get-tuple-element.84.refs_3_.refs_4_, ...), custom_call_target="tpu_custom_call" | custom-call | flops 1 | bytes 1 | tf_op jit(solution)/shard_map/sums_others/pallas_call | solution.py:177
  113.9 1.5 collective-permute-start.20
  115.4 19.7 %update.2.refs_11_ = f32[2048,4096]{1,0:T(8,128)} custom-call(s32[4]{0:T(128)} %pad_add_fusion.refs_0_, f32[1024,1]{1,0:T(8,128)} %clip_factor.1.refs_1_, bf16[256,2048]{1,0:T(8,128)(2,1)} %refs_2_.3, bf16[256,2048]{1,0:T(8,128)(2,1)} %collective-permute-done.1.refs_2_.refs_3_, bf16[2,256,2048]{2,1,0:T(8,128)(2,1)} %get-tuple-element.82.refs_4_.refs_5_, ...), custom_call_target="tpu_custom_call" | custom-call | flops 1 | bytes 1 | tf_op jit(solution)/shard_map/update/pallas_call | solution.py:147
  135.1 0.0 collective-permute-done.17.refs_4_
  135.1 0.0 collective-permute-done.16.refs_2_
  135.2 4.0 %sums_later.1 = (bf16[256,2048]{1,0:T(8,128)(2,1)}, bf16[256,2048]{1,0:T(8,128)(2,1)}) custom-call(s32[4]{0:T(128)} %pad_add_fusion.refs_0_, bf16[256,2048]{1,0:T(8,128)(2,1)} %get-tuple-element.68.refs_1_, bf16[256,2048]{1,0:T(8,128)(2,1)} %collective-permute-done.16.refs_2_, bf16[256,2048]{1,0:T(8,128)(2,1)} %get-tuple-element.80.refs_3_, ...), custom_call_target="tpu_custom_call" | custom-call | flops 1 | bytes 1 | tf_op jit(solution)/shard_map/sums_later/pallas_call | solution.py:177
  139.1 2.0 %collective-permute-start.18 = (bf16[256,2048]{1,0:T(8,128)(2,1)}, bf16[256,2048]{1,0:T(8,128)(2,1)}, u32[]{:S(2)}, u32[]{:S(2)}) collective-permute-start(bf16[256,2048]{1,0:T(8,128)(2,1)} %get-tuple-element.88), channel_id=1, source_target_pairs={{0,1},{1,0},{2,3},{3,2},{4,5},{5,4},{6,7},{7,6},{8,9},{9,8},{10,11... | collective-permute-start | bytes 3145736 | tf_op jit(solution)/shard_map/ppermute | solution.py:202
  141.1 0.0 collective-permute-start.19
  141.1 19.7 %update.3 = f32[2048,4096]{1,0:T(8,128)} custom-call(s32[4]{0:T(128)} %pad_add_fusion.refs_0_, f32[1024,1]{1,0:T(8,128)} %clip_factor.1.refs_1_, bf16[256,2048]{1,0:T(8,128)(2,1)} %refs_2_.3, bf16[256,2048]{1,0:T(8,128)(2,1)} %collective-permute-done.1.refs_2_.refs_3_, ...), custom_call_target="tpu_custom_call", output_to_operand_aliasing={{}: (11, {})} | custom-call | flops 1 | bytes 1 | tf_op jit(solution)/shard_map/update/pallas_call | solution.py:147
  160.9 1.2 collective-permute-done.20.refs_1_
  162.1 5.7 %sums_outputs.1 = bf16[256,4096]{1,0:T(8,128)(2,1)} custom-call(s32[4]{0:T(128)} %pad_add_fusion.refs_0_, bf16[256,4096]{1,0:T(8,128)(2,1)} %collective-permute-done.20.refs_1_, bf16[256,4096]{1,0:T(8,128)(2,1)} %get-tuple-element.67.refs_6_.refs_1_.refs_2_, bf16[256,4096]{1,0:T(8,128)(2,1)} %collective-permute-done.9.refs_2_.refs_3_, ...), custom_call_target="tpu_custom_call" | custom-call | flops 1 | bytes 1 | tf_op jit(solution)/shard_map/sums_outputs/pallas_call | solution.py:177
  167.8 0.0 collective-permute-done.18.refs_2_
  167.8 0.0 collective-permute-done.19.refs_3_
  167.8 3.5 %sums_in_grad.1 = bf16[256,2048]{1,0:T(8,128)(2,1)} custom-call(s32[4]{0:T(128)} %pad_add_fusion.refs_0_, bf16[256,2048]{1,0:T(8,128)(2,1)} %get-tuple-element.93.refs_1_, bf16[256,2048]{1,0:T(8,128)(2,1)} %collective-permute-done.18.refs_2_, bf16[256,2048]{1,0:T(8,128)(2,1)} %collective-permute-done.19.refs_3_), custom_call_target="tpu_custom_call" | custom-call | flops 1 | bytes 1 | tf_op jit(solution)/shard_map/sums_in_grad/pallas_call | solution.py:177
  (10 shorter events, 0.1 us)
Async XLA Ops:
  0.6 10.4 %collective-permute-start.4 = (bf16[256,4096]{1,0:T(8,128)(2,1)}, bf16[256,4096]{1,0:T(8,128)(2,1)}, u32[]{:S(2)}, u32[]{:S(2)}) collective-permute-start(bf16[256,4096]{1,0:T(8,128)(2,1)} %refs_6_.3), channel_id=1, source_target_pairs={{0,4},{4,0},{8,12},{12,8},{1,5},{5,1},{9,13},{13,9},{2,6},{6,2},{1... | collective-permute-start | bytes 6291464 | tf_op jit(solution)/shard_map/ppermute | solution.py:215
  1.1 29.4 %collective-permute-start.2 = (bf16[256,2048]{1,0:T(8,128)(2,1)}, bf16[256,2048]{1,0:T(8,128)(2,1)}, u32[]{:S(2)}, u32[]{:S(2)}) collective-permute-start(bf16[256,2048]{1,0:T(8,128)(2,1)} %refs_2_.3), channel_id=1, source_target_pairs={{0,4},{1,2},{2,1},{3,7},{4,0},{5,6},{6,5},{7,3},{8,12},{9,10},{10,... | collective-permute-start | bytes 3145736 | tf_op jit(solution)/shard_map/ppermute | solution.py:211
  1.2 29.3 %collective-permute-start.1 = (bf16[256,2048]{1,0:T(8,128)(2,1)}, bf16[256,2048]{1,0:T(8,128)(2,1)}, u32[]{:S(2)}, u32[]{:S(2)}) collective-permute-start(bf16[256,2048]{1,0:T(8,128)(2,1)} %refs_2_.3), channel_id=1, source_target_pairs={{0,1},{1,0},{2,3},{3,2},{4,5},{5,4},{6,7},{7,6},{8,9},{9,8},{10,11... | collective-permute-start | bytes 3145736 | tf_op jit(solution)/shard_map/ppermute | solution.py:202
  5.4 48.2 %collective-permute-start = (bf16[256,4096]{1,0:T(8,128)(2,1)}, bf16[256,4096]{1,0:T(8,128)(2,1)}, u32[]{:S(2)}, u32[]{:S(2)}) collective-permute-start(bf16[256,4096]{1,0:T(8,128)(2,1)} %refs_6_.3), channel_id=1, source_target_pairs={{0,8},{4,12},{8,0},{12,4},{1,9},{5,13},{9,1},{13,5},{2,10},{6,14},... | collective-permute-start | bytes 6291464 | tf_op jit(solution)/shard_map/ppermute | solution.py:215
  10.4 20.1 %collective-permute-start.3 = (bf16[4,64,128]{2,1,0:T(8,128)(2,1)}, bf16[4,64,128]{2,1,0:T(8,128)(2,1)S(1)}, u32[]{:S(2)}, u32[]{:S(2)}) collective-permute-start(bf16[4,64,128]{2,1,0:T(8,128)(2,1)} %gram.1.refs_4_.refs_7_), channel_id=1, source_target_pairs={{0,1},{1,0},{2,3},{3,2},{4,5},{5,4},{6,7},{7,6},{8,9},{9,8},{10,11... | collective-permute-start | bytes 196616 | tf_op jit(solution)/shard_map/ppermute | solution.py:202
  30.5 25.1 %collective-permute-start.6 = (bf16[256,2048]{1,0:T(8,128)(2,1)}, bf16[256,2048]{1,0:T(8,128)(2,1)}, u32[]{:S(2)}, u32[]{:S(2)}) collective-permute-start(bf16[256,2048]{1,0:T(8,128)(2,1)} %collective-permute-done.2.refs_1_), channel_id=1, source_target_pairs={{0,1},{1,0},{2,3},{3,2},{4,5},{5,4},{6,7},{7,6},{8,9},{9,8},{10,11... | collective-permute-start | bytes 3145736 | tf_op jit(solution)/shard_map/ppermute | solution.py:202
  32.2 23.4 %collective-permute-start.5 = (bf16[256,2048]{1,0:T(8,128)(2,1)}, bf16[256,2048]{1,0:T(8,128)(2,1)}, u32[]{:S(2)}, u32[]{:S(2)}) collective-permute-start(bf16[256,2048]{1,0:T(8,128)(2,1)} %collective-permute-done.1.refs_2_.refs_3_), channel_id=1, source_target_pairs={{0,4},{1,2},{2,1},{3,7},{4,0},{5,6},{6,5},{7,3},{8,12},{9,10},{10,... | collective-permute-start | bytes 3145736 | tf_op jit(solution)/shard_map/ppermute | solution.py:211
  40.1 16.1 %copy-start = (bf16[4,64,128]{2,1,0:T(8,128)(2,1)S(1)}, bf16[4,64,128]{2,1,0:T(8,128)(2,1)}, u32[]{:S(2)}) copy-start(bf16[4,64,128]{2,1,0:T(8,128)(2,1)} %gram.1.refs_4_.refs_7_) | copy-start | bytes 196612
  55.7 4.5 %collective-permute-start.7 = (bf16[256,4096]{1,0:T(8,128)(2,1)}, bf16[256,4096]{1,0:T(8,128)(2,1)}, u32[]{:S(2)}, u32[]{:S(2)}) collective-permute-start(bf16[256,4096]{1,0:T(8,128)(2,1)} %collective-permute-done.refs_1_.refs_8_), channel_id=1, source_target_pairs={{0,4},{4,0},{8,12},{12,8},{1,5},{5,1},{9,13},{13,9},{2,6},{6,2},{1... | collective-permute-start | bytes 6291464 | tf_op jit(solution)/shard_map/ppermute | solution.py:215
  55.7 19.7 %collective-permute-start.9 = (bf16[256,4096]{1,0:T(8,128)(2,1)}, bf16[256,4096]{1,0:T(8,128)(2,1)}, u32[]{:S(2)}, u32[]{:S(2)}) collective-permute-start(bf16[256,4096]{1,0:T(8,128)(2,1)} %get-tuple-element.71), channel_id=1, source_target_pairs={{0,4},{4,0},{8,12},{12,8},{1,5},{5,1},{9,13},{13,9},{2,6},{6,2},{1... | collective-permute-start | bytes 6291464 | tf_op jit(solution)/shard_map/ppermute | solution.py:215
  56.2 19.1 %collective-permute-start.8 = (bf16[6,64,128]{2,1,0:T(8,128)(2,1)S(1)}, bf16[6,64,128]{2,1,0:T(8,128)(2,1)S(1)}, u32[]{:S(2)}, u32[]{:S(2)}) collective-permute-start(bf16[6,64,128]{2,1,0:T(8,128)(2,1)S(1)} %pad_maximum_fusion.1), channel_id=1, source_target_pairs={{0,2},{1,3},{2,0},{3,1},{4,6},{5,7},{6,4},{7,5},{8,10},{9,11},{10,... | collective-permute-start | bytes 294920 | tf_op jit(solution)/shard_map/ppermute | solution.py:202
  58.7 27.8 %collective-permute-start.11 = (bf16[256,2048]{1,0:T(8,128)(2,1)}, bf16[256,2048]{1,0:T(8,128)(2,1)}, u32[]{:S(2)}, u32[]{:S(2)}) collective-permute-start(bf16[256,2048]{1,0:T(8,128)(2,1)} %collective-permute-done.5.refs_3_), channel_id=1, source_target_pairs={{1,0},{2,3},{5,4},{6,7},{9,8},{10,11},{13,12},{14,15},{17,16},{18,... | collective-permute-start | bytes 3145736 | tf_op jit(solution)/shard_map/ppermute | solution.py:202
  75.4 28.9 %collective-permute-start.10 = (bf16[256,2048]{1,0:T(8,128)(2,1)}, bf16[256,2048]{1,0:T(8,128)(2,1)}, u32[]{:S(2)}, u32[]{:S(2)}) collective-permute-start(bf16[256,2048]{1,0:T(8,128)(2,1)} %get-tuple-element.72.refs_6_.refs_1_), channel_id=1, source_target_pairs={{0,1},{3,2},{4,5},{7,6},{8,9},{11,10},{12,13},{15,14},{16,17},{19,... | collective-permute-start | bytes 3145736 | tf_op jit(solution)/shard_map/ppermute | solution.py:202
  81.8 18.9 %copy-start.1 = (bf16[10,64,128]{2,1,0:T(8,128)(2,1)}, bf16[10,64,128]{2,1,0:T(8,128)(2,1)S(1)}, u32[]{:S(2)}) copy-start(bf16[10,64,128]{2,1,0:T(8,128)(2,1)S(1)} %pad_maximum_fusion.refs_1_) | copy-start | bytes 491524
  81.8 18.9 %collective-permute-start.14 = (bf16[10,64,128]{2,1,0:T(8,128)(2,1)S(1)}, bf16[10,64,128]{2,1,0:T(8,128)(2,1)S(1)}, u32[]{:S(2)}, u32[]{:S(2)}) collective-permute-start(bf16[10,64,128]{2,1,0:T(8,128)(2,1)S(1)} %pad_maximum_fusion.refs_1_), channel_id=1, source_target_pairs={{0,12},{4,8},{8,4},{12,0},{1,13},{5,9},{9,5},{13,1},{2,14},{6,10},... | collective-permute-start | bytes 491528 | tf_op jit(solution)/shard_map/ppermute | solution.py:215
  82.2 18.5 %collective-permute-start.13 = (bf16[10,64,128]{2,1,0:T(8,128)(2,1)S(1)}, bf16[10,64,128]{2,1,0:T(8,128)(2,1)S(1)}, u32[]{:S(2)}, u32[]{:S(2)}) collective-permute-start(bf16[10,64,128]{2,1,0:T(8,128)(2,1)S(1)} %pad_maximum_fusion.refs_1_), channel_id=1, source_target_pairs={{0,8},{4,12},{8,0},{12,4},{1,9},{5,13},{9,1},{13,5},{2,10},{6,14},... | collective-permute-start | bytes 491528 | tf_op jit(solution)/shard_map/ppermute | solution.py:215
  83.5 17.3 %collective-permute-start.12 = (bf16[10,64,128]{2,1,0:T(8,128)(2,1)S(1)}, bf16[10,64,128]{2,1,0:T(8,128)(2,1)S(1)}, u32[]{:S(2)}, u32[]{:S(2)}) collective-permute-start(bf16[10,64,128]{2,1,0:T(8,128)(2,1)S(1)} %pad_maximum_fusion.refs_1_), channel_id=1, source_target_pairs={{0,4},{4,0},{8,12},{12,8},{1,5},{5,1},{9,13},{13,9},{2,6},{6,2},{1... | collective-permute-start | bytes 491528 | tf_op jit(solution)/shard_map/ppermute | solution.py:215
  100.7 0.7 copy-start.2
  100.7 0.7 copy-start.3
  101.4 0.7 copy-start.4
  104.2 4.5 %collective-permute-start.15 = (bf16[256,4096]{1,0:T(8,128)(2,1)}, bf16[256,4096]{1,0:T(8,128)(2,1)}, u32[]{:S(2)}, u32[]{:S(2)}) collective-permute-start(bf16[256,4096]{1,0:T(8,128)(2,1)} %get-tuple-element.77), channel_id=1, source_target_pairs={{0,4},{4,0},{8,12},{12,8},{1,5},{5,1},{9,13},{13,9},{2,6},{6,2},{1... | collective-permute-start | bytes 6291464 | tf_op jit(solution)/shard_map/ppermute | solution.py:215
  104.2 30.9 %collective-permute-start.17 = (bf16[256,2048]{1,0:T(8,128)(2,1)}, bf16[256,2048]{1,0:T(8,128)(2,1)}, u32[]{:S(2)}, u32[]{:S(2)}) collective-permute-start(bf16[256,2048]{1,0:T(8,128)(2,1)} %get-tuple-element.80.refs_3_), channel_id=1, source_target_pairs={{0,1},{1,0},{2,3},{3,2},{4,5},{5,4},{6,7},{7,6},{8,9},{9,8},{10,11... | collective-permute-start | bytes 3145736 | tf_op jit(solution)/shard_map/ppermute | solution.py:202
  108.7 26.4 %collective-permute-start.16 = (bf16[256,2048]{1,0:T(8,128)(2,1)}, bf16[256,2048]{1,0:T(8,128)(2,1)}, u32[]{:S(2)}, u32[]{:S(2)}) collective-permute-start(bf16[256,2048]{1,0:T(8,128)(2,1)} %sums_now.1), channel_id=1, source_target_pairs={{0,4},{1,2},{2,1},{3,7},{4,0},{5,6},{6,5},{7,3},{8,12},{9,10},{10,... | collective-permute-start | bytes 3145736 | tf_op jit(solution)/shard_map/ppermute | solution.py:211
  113.9 48.1 %collective-permute-start.20 = (bf16[256,4096]{1,0:T(8,128)(2,1)}, bf16[256,4096]{1,0:T(8,128)(2,1)}, u32[]{:S(2)}, u32[]{:S(2)}) collective-permute-start(bf16[256,4096]{1,0:T(8,128)(2,1)} %sums_others.1.refs_11_), channel_id=1, source_target_pairs={{0,8},{4,12},{8,0},{12,4},{1,9},{5,13},{9,1},{13,5},{2,10},{6,14},... | collective-permute-start | bytes 6291464 | tf_op jit(solution)/shard_map/ppermute | solution.py:215
  139.1 28.6 %collective-permute-start.18 = (bf16[256,2048]{1,0:T(8,128)(2,1)}, bf16[256,2048]{1,0:T(8,128)(2,1)}, u32[]{:S(2)}, u32[]{:S(2)}) collective-permute-start(bf16[256,2048]{1,0:T(8,128)(2,1)} %get-tuple-element.88), channel_id=1, source_target_pairs={{0,1},{1,0},{2,3},{3,2},{4,5},{5,4},{6,7},{7,6},{8,9},{9,8},{10,11... | collective-permute-start | bytes 3145736 | tf_op jit(solution)/shard_map/ppermute | solution.py:202
  141.1 26.7 %collective-permute-start.19 = (bf16[256,2048]{1,0:T(8,128)(2,1)}, bf16[256,2048]{1,0:T(8,128)(2,1)}, u32[]{:S(2)}, u32[]{:S(2)}) collective-permute-start(bf16[256,2048]{1,0:T(8,128)(2,1)} %get-tuple-element.89), channel_id=1, source_target_pairs={{0,4},{1,2},{2,1},{3,7},{4,0},{5,6},{6,5},{7,3},{8,12},{9,10},{10,... | collective-permute-start | bytes 3145736 | tf_op jit(solution)/shard_map/ppermute | solution.py:211

commit v5 on v4

--- a/solution.py
+++ b/solution.py
@@ -262,7 +262,7 @@
                 square = jnp.sum(
                     jnp.where(lane // SEQ == side, sums, 0.0), axis=1, keepdims=True
                 )
-                factor = jnp.minimum(1.0, clip / jnp.sqrt(square + 1e-06))
+                factor = jnp.minimum(1.0, clip / jnp.sqrt(jnp.maximum(square, 0.0) + 1e-06))
                 start = pl.multiple_of(block * r + (2 * p + side) * SEQ, SEQ)
                 out[pl.ds(start, SEQ), :] = jnp.broadcast_to(factor, (SEQ, 1))
 
@@ -419,12 +419,10 @@
         outs[0][...] = (refs[0][...].astype(F32) + inner_only(at, refs[1])).astype(BF16)
         outs[1][...] = total(refs[2], refs[3]).astype(BF16)
 
-    def last_outputs(at, refs, outs):
-        mine = either(at[0] == at[1], refs[1:3], refs[3:])
+    def last(at, refs, outs):
+        mine = either(at[0] == at[1], refs[4:6], refs[6:])
         outs[0][...] = (mine + refs[0][...].astype(F32)).astype(BF16)
-
-    def last_in_grad(at, refs, outs):
-        outs[0][...] = (total(*refs[:2]) + inner_only(at, refs[2])).astype(BF16)
+        outs[1][...] = (total(*refs[1:3]) + inner_only(at, refs[3])).astype(BF16)
 
     def block_of(at, j):
         return at[3] ^ j
@@ -443,13 +441,11 @@
     r3 = along(r3, OUTER)
     r2b = middle(r2b)
     update = make_update(at, xs, gs, *facts, 1, 2, update)
-    theirs, update = hold((theirs, update))
-    (outputs,) = add_up(
-        at, last_outputs, [theirs],
-        [(if_same, pa0), (if_same, pa1), (if_other, pb0), (if_other, pb1)], [wide], 2, "sums_outputs",
-    )
-    r3, r2b, outputs = hold((r3, r2b, outputs))
-    (in_grad,) = add_up(at, last_in_grad, [own, r3, r2b], [], [narrow], 2, "sums_in_grad")
+    r3, r2b, theirs, update = hold((r3, r2b, theirs, update))
+    outputs, in_grad = add_up(
+        at, last, [theirs, own, r3, r2b],
+        [(if_same, pa0), (if_same, pa1), (if_other, pb0), (if_other, pb1)], [wide, narrow], 2, "sums_last",
+    )
     return outputs, in_grad, update
 
 
@@ -468,7 +464,8 @@
         tiled=True,
     )
     grams = lax.psum(gram(x), "mp") * lax.psum(gram(g), "hidden")
-    factor = jnp.minimum(1.0, clip / jnp.sqrt(jnp.sum(grams, axis=(1, 2)) + 1e-06))
+    squares = jnp.maximum(jnp.sum(grams, axis=(1, 2)), 0.0)
+    factor = jnp.minimum(1.0, clip / jnp.sqrt(squares + 1e-06))
     none = lambda at, j: 0
     update = make_update(
         jnp.zeros((1,), jnp.int32),

time: 172 us -> 172 us (level)
  waiting for transfers between devices: 7.49 us -> 9.81 us
  Pallas kernels: 135 us -> 133 us
    ppermute x8, waiting for transfers between devices: 6.04 us -> 9.58 us  [along(): return lax.ppermute(value, 'hidden', pairs)]
    pallas_call x5 -> x4, Pallas kernels: 21.3 us -> 18.9 us  [add_up(): pl.pallas_call(lambda *refs: add_kernel(sums, len(arrays) + len(chosen),...]
  transfers between devices with their start and end apart: 21 -> 21, of which waited for: 5 -> 5; matrix products, arithmetic and copies ran while one was open for 0% -> 0% of each run, Pallas kernels for 77% -> 74%
where the time goes in v5:
time: 172 us; the launch traced here: 171 us
  Pallas kernels  133 us (77%)
  starting transfers between devices  25.6 us (15%)
  waiting for transfers between devices  9.81 us (6%)
    pallas_call x5, Pallas kernels, pair_matmul(): pl.pallas_call(kernel, grid=(steps,), in_specs=[pl.BlockSpec(memory_space...  69 us
    pallas_call x2, Pallas kernels, make_update(): pl.pallas_call(kernel, grid=(depth // tile,), in_specs=[pl.BlockSpec(memo...  39.5 us
    ppermute x8, starting transfers between devices, along(): return lax.ppermute(value, 'hidden', pairs)  19.4 us
    pallas_call x4, Pallas kernels, add_up(): pl.pallas_call(lambda *refs: add_kernel(sums, len(arrays) + len(chosen),...  18.9 us
    ppermute x8, waiting for transfers between devices, along(): return lax.ppermute(value, 'hidden', pairs)  9.58 us
    ppermute x9, starting transfers between devices, swap(): return lax.ppermute(value, 'mp', [(i, i ^ bit) for i in range(4)])  5.93 us
    pallas_call x1, Pallas kernels, gram_pairs(): pl.pallas_call(gram_kernel, in_specs=[pl.BlockSpec(memory_space=pltpu.VME...  3.58 us
  transfers between devices with their start and end apart: 21, of which 5 were waited for; matrix products, arithmetic and copies ran while one was open for 0% of the time, Pallas kernels for 74%

profile of v5, /device:TPU:0, one launch (start us, length us, event | category | flops | bytes accessed | tf_op | source)
XLA Modules:
  0.0 171.4 jit_solution(1420119419746828568)
XLA Ops:
  0.6 0.5 collective-permute-start.4
  1.1 0.1 collective-permute-start.2
  1.2 4.1 %collective-permute-start.1 = (bf16[256,2048]{1,0:T(8,128)(2,1)}, bf16[256,2048]{1,0:T(8,128)(2,1)}, u32[]{:S(2)}, u32[]{:S(2)}) collective-permute-start(bf16[256,2048]{1,0:T(8,128)(2,1)} %refs_2_.3), channel_id=1, source_target_pairs={{0,1},{1,0},{2,3},{3,2},{4,5},{5,4},{6,7},{7,6},{8,9},{9,8},{10,11... | collective-permute-start | bytes 3145736 | tf_op jit(solution)/shard_map/ppermute | solution.py:202
  5.4 1.5 collective-permute-start
  6.9 3.6 %gram.1.refs_4_.refs_7_ = bf16[4,64,128]{2,1,0:T(8,128)(2,1)} custom-call(bf16[256,2048]{1,0:T(8,128)(2,1)} %refs_2_.3, bf16[256,4096]{1,0:T(8,128)(2,1)} %refs_6_.3), custom_call_target="tpu_custom_call" | custom-call | flops 1 | bytes 1 | tf_op jit(solution)/shard_map/gram/pallas_call | solution.py:238
  10.4 0.0 collective-permute-start.3
  10.5 0.7 pad_add_fusion.refs_0_
  11.1 0.0 collective-permute-done.4.refs_2_.refs_7_
  11.1 18.3 %in_grad_here.2 = (bf16[256,2048]{1,0:T(8,128)(2,1)}, bf16[256,2048]{1,0:T(8,128)(2,1)}, bf16[2048,4096]{1,0:T(8,128)(2,1)}) custom-call(s32[4]{0:T(128)} %pad_add_fusion.refs_0_, bf16[256,4096]{1,0:T(8,128)(2,1)} %refs_6_.3, bf16[256,4096]{1,0:T(8,128)(2,1)} %collective-permute-done.4.refs_2_.refs_7_, f32[2048,4096]{1,0:T(8,128)} %refs_3_.1, ...), custom_call_target="tpu_custom_call" | custom-call | flops 1 | bytes 1 | tf_op jit(solution)/shard_map/in_grad_here/pallas_call | solution.py:81
  29.4 1.1 collective-permute-done.3
  30.5 0.0 collective-permute-done.2.refs_1_
  30.5 0.0 collective-permute-done.1.refs_2_.refs_3_
  30.5 1.7 collective-permute-start.6
  32.2 0.0 collective-permute-start.5
  32.2 7.9 %in_grad_here.3 = (bf16[256,2048]{1,0:T(8,128)(2,1)}, bf16[256,2048]{1,0:T(8,128)(2,1)}, bf16[2048,4096]{1,0:T(8,128)(2,1)}) custom-call(s32[4]{0:T(128)} %pad_add_fusion.refs_0_, bf16[256,4096]{1,0:T(8,128)(2,1)} %refs_6_.3, bf16[256,4096]{1,0:T(8,128)(2,1)} %collective-permute-done.4.refs_2_.refs_7_, ...), custom_call_target="tpu_custom_call", output_to_operand_aliasing={{0}: (4, {}), {1}: (5, {}), {2}: (6, {})} | custom-call | flops 1 | bytes 1 | tf_op jit(solution)/shard_map/in_grad_here/pallas_call | solution.py:81
  40.1 13.5 %outputs_near.1 = (bf16[256,4096]{1,0:T(8,128)(2,1)}, bf16[256,4096]{1,0:T(8,128)(2,1)}) custom-call(s32[4]{0:T(128)} %pad_add_fusion.refs_0_, bf16[256,2048]{1,0:T(8,128)(2,1)} %refs_2_.3, bf16[256,2048]{1,0:T(8,128)(2,1)} %collective-permute-done.1.refs_2_.refs_3_, bf16[2048,4096]{1,0:T(8,128)(2,1)} %get-tuple-element.61.refs_3_.refs_5_), custom_call_target="tpu_custom_call" | custom-call | flops 1 | bytes 1 | tf_op jit(solution)/shard_map/outputs_near/pallas_call | solution.py:81
  53.6 0.0 collective-permute-done.refs_1_.refs_8_
  53.6 2.1 %collective-permute-done.6.refs_2_ = bf16[256,2048]{1,0:T(8,128)(2,1)} collective-permute-done((bf16[256,2048]{1,0:T(8,128)(2,1)}, bf16[256,2048]{1,0:T(8,128)(2,1)}, u32[]{:S(2)}, u32[]{:S(2)}) %collective-permute-start.6) | collective-permute-done | bytes 1048608 | tf_op jit(solution)/shard_map/ppermute | solution.py:202
  55.7 0.0 collective-permute-done.5.refs_3_
  55.7 0.0 collective-permute-start.7
  55.7 0.5 collective-permute-start.9
  56.2 0.0 copy-done
  56.2 2.4 %collective-permute-start.8 = (bf16[6,64,128]{2,1,0:T(8,128)(2,1)S(1)}, bf16[6,64,128]{2,1,0:T(8,128)(2,1)S(1)}, u32[]{:S(2)}, u32[]{:S(2)}) collective-permute-start(bf16[6,64,128]{2,1,0:T(8,128)(2,1)S(1)} %pad_maximum_fusion.1), channel_id=1, source_target_pairs={{0,2},{1,3},{2,0},{3,1},{4,6},{5,7},{6,4},{7,5},{8,10},{9,11},{10,... | collective-permute-start | bytes 294920 | tf_op jit(solution)/shard_map/ppermute | solution.py:202
  58.7 1.3 collective-permute-start.11
  60.0 0.2 collective-permute-done.7.refs_2_.refs_9_
  60.2 15.2 %in_grad_there.1 = (bf16[256,2048]{1,0:T(8,128)(2,1)}, bf16[256,2048]{1,0:T(8,128)(2,1)}, bf16[256,2048]{1,0:T(8,128)(2,1)}, bf16[256,2048]{1,0:T(8,128)(2,1)}) custom-call(s32[4]{0:T(128)} %pad_add_fusion.refs_0_, bf16[256,4096]{1,0:T(8,128)(2,1)} %collective-permute-done.refs_1_.refs_8_, bf16[256,4096]{1,0:T(8,128)(2,1)} %collective-permute-done.7.refs_2_.refs_9_, ...), custom_call_target="tpu_custom_call" | custom-call | flops 1 | bytes 1 | tf_op jit(solution)/shard_map/in_grad_there/pallas_call | solution.py:81
  75.4 0.0 collective-permute-done.8
  75.4 0.0 collective-permute-done.9.refs_2_.refs_6_
  75.4 6.4 %collective-permute-start.10 = (bf16[256,2048]{1,0:T(8,128)(2,1)}, bf16[256,2048]{1,0:T(8,128)(2,1)}, u32[]{:S(2)}, u32[]{:S(2)}) collective-permute-start(bf16[256,2048]{1,0:T(8,128)(2,1)} %get-tuple-element.73.refs_6_.refs_1_), channel_id=1, source_target_pairs={{0,1},{3,2},{4,5},{7,6},{8,9},{11,10},{12,13},{15,14},{16,17},{19,... | collective-permute-start | bytes 3145736 | tf_op jit(solution)/shard_map/ppermute | solution.py:202
  81.8 0.0 copy-start.1
  81.9 0.3 collective-permute-start.14
  82.2 1.3 collective-permute-start.13
  83.5 0.3 collective-permute-start.12
  83.8 2.7 %collective-permute-done.11.refs_4_ = bf16[256,2048]{1,0:T(8,128)(2,1)} collective-permute-done((bf16[256,2048]{1,0:T(8,128)(2,1)}, bf16[256,2048]{1,0:T(8,128)(2,1)}, u32[]{:S(2)}, u32[]{:S(2)}) %collective-permute-start.11) | collective-permute-done | bytes 1048608 | tf_op jit(solution)/shard_map/ppermute | solution.py:202
  86.5 14.2 %outputs_far.1 = (bf16[256,4096]{1,0:T(8,128)(2,1)}, bf16[256,4096]{1,0:T(8,128)(2,1)}, bf16[2,256,2048]{2,1,0:T(8,128)(2,1)}) custom-call(s32[4]{0:T(128)} %pad_add_fusion.refs_0_, bf16[256,2048]{1,0:T(8,128)(2,1)} %collective-permute-done.2.refs_1_, bf16[256,2048]{1,0:T(8,128)(2,1)} %collective-permute-done.6.refs_2_, ...), custom_call_target="tpu_custom_call" | custom-call | flops 1 | bytes 1 | tf_op jit(solution)/shard_map/outputs_far/pallas_call | solution.py:81
  100.7 0.0 copy-done.1
  100.7 0.0 collective-permute-done.14.refs_4_
  100.7 0.0 copy-start.2
  100.7 0.0 collective-permute-done.13.refs_3_
  100.7 0.0 copy-start.3
  100.7 0.0 collective-permute-done.12.refs_2_
  100.7 0.6 copy-done.2
  101.3 0.1 copy-done.3
  101.4 0.7 copy-done.4
  102.1 2.1 %clip_factor.1.refs_1_ = f32[1024,1]{1,0:T(8,128)} custom-call(s32[4]{0:T(128)} %pad_add_fusion.refs_0_, bf16[10,64,128]{2,1,0:T(8,128)(2,1)} %copy-done.1, bf16[10,64,128]{2,1,0:T(8,128)(2,1)} %copy-done.4, bf16[10,64,128]{2,1,0:T(8,128)(2,1)} %copy-done.3, bf16[10,64,128]{2,1,0:T(8,128)(2,1)} %copy-done.2), custom_call_target="tpu_custom_call" | custom-call | flops 1 | bytes 1 | tf_op jit(solution)/shard_map/clip_factor/pallas_call | solution.py:271
  104.2 0.0 collective-permute-done.10.refs_2_
  104.2 0.0 collective-permute-start.15
  104.2 1.4 collective-permute-start.17
  105.6 3.1 %sums_now.1 = bf16[256,2048]{1,0:T(8,128)(2,1)} custom-call(s32[4]{0:T(128)} %pad_add_fusion.refs_0_, bf16[256,2048]{1,0:T(8,128)(2,1)} %get-tuple-element.73.refs_6_.refs_1_, bf16[256,2048]{1,0:T(8,128)(2,1)} %collective-permute-done.10.refs_2_), custom_call_target="tpu_custom_call" | custom-call | flops 1 | bytes 1 | tf_op jit(solution)/shard_map/sums_now/pallas_call | solution.py:177
  108.7 0.0 collective-permute-done.15.refs_4_.refs_8_
  108.7 0.2 collective-permute-start.16
  109.0 5.0 %sums_others.1.refs_11_ = bf16[256,4096]{1,0:T(8,128)(2,1)} custom-call(s32[4]{0:T(128)} %pad_add_fusion.refs_0_, bf16[256,4096]{1,0:T(8,128)(2,1)} %get-tuple-element.68.refs_6_.refs_1_.refs_5_, bf16[256,4096]{1,0:T(8,128)(2,1)} %collective-permute-done.9.refs_2_.refs_6_, bf16[256,4096]{1,0:T(8,128)(2,1)} %get-tuple-element.85.refs_3_.refs_7_, ...), custom_call_target="tpu_custom_call" | custom-call | flops 1 | bytes 1 | tf_op jit(solution)/shard_map/sums_others/pallas_call | solution.py:177
  114.0 1.5 collective-permute-start.20
  115.4 19.8 %update.2.refs_11_ = f32[2048,4096]{1,0:T(8,128)} custom-call(s32[4]{0:T(128)} %pad_add_fusion.refs_0_, f32[1024,1]{1,0:T(8,128)} %clip_factor.1.refs_1_, bf16[256,2048]{1,0:T(8,128)(2,1)} %refs_2_.3, bf16[256,2048]{1,0:T(8,128)(2,1)} %collective-permute-done.1.refs_2_.refs_3_, bf16[2,256,2048]{2,1,0:T(8,128)(2,1)} %get-tuple-element.83.refs_4_.refs_5_, ...), custom_call_target="tpu_custom_call" | custom-call | flops 1 | bytes 1 | tf_op jit(solution)/shard_map/update/pallas_call | solution.py:147
  135.2 0.0 collective-permute-done.17.refs_4_
  135.2 0.0 collective-permute-done.16.refs_2_
  135.2 4.0 %sums_later.1 = (bf16[256,2048]{1,0:T(8,128)(2,1)}, bf16[256,2048]{1,0:T(8,128)(2,1)}) custom-call(s32[4]{0:T(128)} %pad_add_fusion.refs_0_, bf16[256,2048]{1,0:T(8,128)(2,1)} %get-tuple-element.69.refs_1_, bf16[256,2048]{1,0:T(8,128)(2,1)} %collective-permute-done.16.refs_2_, bf16[256,2048]{1,0:T(8,128)(2,1)} %get-tuple-element.81.refs_3_, ...), custom_call_target="tpu_custom_call" | custom-call | flops 1 | bytes 1 | tf_op jit(solution)/shard_map/sums_later/pallas_call | solution.py:177
  139.2 2.0 %collective-permute-start.18 = (bf16[256,2048]{1,0:T(8,128)(2,1)}, bf16[256,2048]{1,0:T(8,128)(2,1)}, u32[]{:S(2)}, u32[]{:S(2)}) collective-permute-start(bf16[256,2048]{1,0:T(8,128)(2,1)} %get-tuple-element.89), channel_id=1, source_target_pairs={{0,1},{1,0},{2,3},{3,2},{4,5},{5,4},{6,7},{7,6},{8,9},{9,8},{10,11... | collective-permute-start | bytes 3145736 | tf_op jit(solution)/shard_map/ppermute | solution.py:202
  141.2 0.0 collective-permute-start.19
  141.2 19.7 %update.3 = f32[2048,4096]{1,0:T(8,128)} custom-call(s32[4]{0:T(128)} %pad_add_fusion.refs_0_, f32[1024,1]{1,0:T(8,128)} %clip_factor.1.refs_1_, bf16[256,2048]{1,0:T(8,128)(2,1)} %refs_2_.3, bf16[256,2048]{1,0:T(8,128)(2,1)} %collective-permute-done.1.refs_2_.refs_3_, ...), custom_call_target="tpu_custom_call", output_to_operand_aliasing={{}: (11, {})} | custom-call | flops 1 | bytes 1 | tf_op jit(solution)/shard_map/update/pallas_call | solution.py:147
  161.0 3.7 %collective-permute-done.18.refs_3_ = bf16[256,2048]{1,0:T(8,128)(2,1)} collective-permute-done((bf16[256,2048]{1,0:T(8,128)(2,1)}, bf16[256,2048]{1,0:T(8,128)(2,1)}, u32[]{:S(2)}, u32[]{:S(2)}) %collective-permute-start.18) | collective-permute-done | bytes 1048608 | tf_op jit(solution)/shard_map/ppermute | solution.py:202
  164.6 0.0 collective-permute-done.19.refs_4_
  164.6 0.0 collective-permute-done.20.refs_1_
  164.6 6.8 %sums_last.1 = (bf16[256,4096]{1,0:T(8,128)(2,1)}, bf16[256,2048]{1,0:T(8,128)(2,1)}) custom-call(s32[4]{0:T(128)} %pad_add_fusion.refs_0_, bf16[256,4096]{1,0:T(8,128)(2,1)} %collective-permute-done.20.refs_1_, bf16[256,2048]{1,0:T(8,128)(2,1)} %get-tuple-element.93.refs_2_, bf16[256,2048]{1,0:T(8,128)(2,1)} %collective-permute-done.18.refs_3_, ...), custom_call_target="tpu_custom_call" | custom-call | flops 1 | bytes 1 | tf_op jit(solution)/shard_map/sums_last/pallas_call | solution.py:177
  (9 shorter events, 0.1 us)
Async XLA Ops:
  0.6 10.5 %collective-permute-start.4 = (bf16[256,4096]{1,0:T(8,128)(2,1)}, bf16[256,4096]{1,0:T(8,128)(2,1)}, u32[]{:S(2)}, u32[]{:S(2)}) collective-permute-start(bf16[256,4096]{1,0:T(8,128)(2,1)} %refs_6_.3), channel_id=1, source_target_pairs={{0,4},{4,0},{8,12},{12,8},{1,5},{5,1},{9,13},{13,9},{2,6},{6,2},{1... | collective-permute-start | bytes 6291464 | tf_op jit(solution)/shard_map/ppermute | solution.py:215
  1.1 29.4 %collective-permute-start.2 = (bf16[256,2048]{1,0:T(8,128)(2,1)}, bf16[256,2048]{1,0:T(8,128)(2,1)}, u32[]{:S(2)}, u32[]{:S(2)}) collective-permute-start(bf16[256,2048]{1,0:T(8,128)(2,1)} %refs_2_.3), channel_id=1, source_target_pairs={{0,4},{1,2},{2,1},{3,7},{4,0},{5,6},{6,5},{7,3},{8,12},{9,10},{10,... | collective-permute-start | bytes 3145736 | tf_op jit(solution)/shard_map/ppermute | solution.py:211
  1.2 29.3 %collective-permute-start.1 = (bf16[256,2048]{1,0:T(8,128)(2,1)}, bf16[256,2048]{1,0:T(8,128)(2,1)}, u32[]{:S(2)}, u32[]{:S(2)}) collective-permute-start(bf16[256,2048]{1,0:T(8,128)(2,1)} %refs_2_.3), channel_id=1, source_target_pairs={{0,1},{1,0},{2,3},{3,2},{4,5},{5,4},{6,7},{7,6},{8,9},{9,8},{10,11... | collective-permute-start | bytes 3145736 | tf_op jit(solution)/shard_map/ppermute | solution.py:202
  5.4 48.2 %collective-permute-start = (bf16[256,4096]{1,0:T(8,128)(2,1)}, bf16[256,4096]{1,0:T(8,128)(2,1)}, u32[]{:S(2)}, u32[]{:S(2)}) collective-permute-start(bf16[256,4096]{1,0:T(8,128)(2,1)} %refs_6_.3), channel_id=1, source_target_pairs={{0,8},{4,12},{8,0},{12,4},{1,9},{5,13},{9,1},{13,5},{2,10},{6,14},... | collective-permute-start | bytes 6291464 | tf_op jit(solution)/shard_map/ppermute | solution.py:215
  10.4 20.1 %collective-permute-start.3 = (bf16[4,64,128]{2,1,0:T(8,128)(2,1)}, bf16[4,64,128]{2,1,0:T(8,128)(2,1)S(1)}, u32[]{:S(2)}, u32[]{:S(2)}) collective-permute-start(bf16[4,64,128]{2,1,0:T(8,128)(2,1)} %gram.1.refs_4_.refs_7_), channel_id=1, source_target_pairs={{0,1},{1,0},{2,3},{3,2},{4,5},{5,4},{6,7},{7,6},{8,9},{9,8},{10,11... | collective-permute-start | bytes 196616 | tf_op jit(solution)/shard_map/ppermute | solution.py:202
  30.5 25.1 %collective-permute-start.6 = (bf16[256,2048]{1,0:T(8,128)(2,1)}, bf16[256,2048]{1,0:T(8,128)(2,1)}, u32[]{:S(2)}, u32[]{:S(2)}) collective-permute-start(bf16[256,2048]{1,0:T(8,128)(2,1)} %collective-permute-done.2.refs_1_), channel_id=1, source_target_pairs={{0,1},{1,0},{2,3},{3,2},{4,5},{5,4},{6,7},{7,6},{8,9},{9,8},{10,11... | collective-permute-start | bytes 3145736 | tf_op jit(solution)/shard_map/ppermute | solution.py:202
  32.2 23.4 %collective-permute-start.5 = (bf16[256,2048]{1,0:T(8,128)(2,1)}, bf16[256,2048]{1,0:T(8,128)(2,1)}, u32[]{:S(2)}, u32[]{:S(2)}) collective-permute-start(bf16[256,2048]{1,0:T(8,128)(2,1)} %collective-permute-done.1.refs_2_.refs_3_), channel_id=1, source_target_pairs={{0,4},{1,2},{2,1},{3,7},{4,0},{5,6},{6,5},{7,3},{8,12},{9,10},{10,... | collective-permute-start | bytes 3145736 | tf_op jit(solution)/shard_map/ppermute | solution.py:211
  40.1 16.1 %copy-start = (bf16[4,64,128]{2,1,0:T(8,128)(2,1)S(1)}, bf16[4,64,128]{2,1,0:T(8,128)(2,1)}, u32[]{:S(2)}) copy-start(bf16[4,64,128]{2,1,0:T(8,128)(2,1)} %gram.1.refs_4_.refs_7_) | copy-start | bytes 196612
  55.7 4.5 %collective-permute-start.7 = (bf16[256,4096]{1,0:T(8,128)(2,1)}, bf16[256,4096]{1,0:T(8,128)(2,1)}, u32[]{:S(2)}, u32[]{:S(2)}) collective-permute-start(bf16[256,4096]{1,0:T(8,128)(2,1)} %collective-permute-done.refs_1_.refs_8_), channel_id=1, source_target_pairs={{0,4},{4,0},{8,12},{12,8},{1,5},{5,1},{9,13},{13,9},{2,6},{6,2},{1... | collective-permute-start | bytes 6291464 | tf_op jit(solution)/shard_map/ppermute | solution.py:215
  55.7 19.7 %collective-permute-start.9 = (bf16[256,4096]{1,0:T(8,128)(2,1)}, bf16[256,4096]{1,0:T(8,128)(2,1)}, u32[]{:S(2)}, u32[]{:S(2)}) collective-permute-start(bf16[256,4096]{1,0:T(8,128)(2,1)} %get-tuple-element.72), channel_id=1, source_target_pairs={{0,4},{4,0},{8,12},{12,8},{1,5},{5,1},{9,13},{13,9},{2,6},{6,2},{1... | collective-permute-start | bytes 6291464 | tf_op jit(solution)/shard_map/ppermute | solution.py:215
  56.2 19.1 %collective-permute-start.8 = (bf16[6,64,128]{2,1,0:T(8,128)(2,1)S(1)}, bf16[6,64,128]{2,1,0:T(8,128)(2,1)S(1)}, u32[]{:S(2)}, u32[]{:S(2)}) collective-permute-start(bf16[6,64,128]{2,1,0:T(8,128)(2,1)S(1)} %pad_maximum_fusion.1), channel_id=1, source_target_pairs={{0,2},{1,3},{2,0},{3,1},{4,6},{5,7},{6,4},{7,5},{8,10},{9,11},{10,... | collective-permute-start | bytes 294920 | tf_op jit(solution)/shard_map/ppermute | solution.py:202
  58.7 27.8 %collective-permute-start.11 = (bf16[256,2048]{1,0:T(8,128)(2,1)}, bf16[256,2048]{1,0:T(8,128)(2,1)}, u32[]{:S(2)}, u32[]{:S(2)}) collective-permute-start(bf16[256,2048]{1,0:T(8,128)(2,1)} %collective-permute-done.5.refs_3_), channel_id=1, source_target_pairs={{1,0},{2,3},{5,4},{6,7},{9,8},{10,11},{13,12},{14,15},{17,16},{18,... | collective-permute-start | bytes 3145736 | tf_op jit(solution)/shard_map/ppermute | solution.py:202
  75.4 28.9 %collective-permute-start.10 = (bf16[256,2048]{1,0:T(8,128)(2,1)}, bf16[256,2048]{1,0:T(8,128)(2,1)}, u32[]{:S(2)}, u32[]{:S(2)}) collective-permute-start(bf16[256,2048]{1,0:T(8,128)(2,1)} %get-tuple-element.73.refs_6_.refs_1_), channel_id=1, source_target_pairs={{0,1},{3,2},{4,5},{7,6},{8,9},{11,10},{12,13},{15,14},{16,17},{19,... | collective-permute-start | bytes 3145736 | tf_op jit(solution)/shard_map/ppermute | solution.py:202
  81.8 18.8 %copy-start.1 = (bf16[10,64,128]{2,1,0:T(8,128)(2,1)}, bf16[10,64,128]{2,1,0:T(8,128)(2,1)S(1)}, u32[]{:S(2)}) copy-start(bf16[10,64,128]{2,1,0:T(8,128)(2,1)S(1)} %pad_maximum_fusion.refs_1_) | copy-start | bytes 491524
  81.9 18.8 %collective-permute-start.14 = (bf16[10,64,128]{2,1,0:T(8,128)(2,1)S(1)}, bf16[10,64,128]{2,1,0:T(8,128)(2,1)S(1)}, u32[]{:S(2)}, u32[]{:S(2)}) collective-permute-start(bf16[10,64,128]{2,1,0:T(8,128)(2,1)S(1)} %pad_maximum_fusion.refs_1_), channel_id=1, source_target_pairs={{0,12},{4,8},{8,4},{12,0},{1,13},{5,9},{9,5},{13,1},{2,14},{6,10},... | collective-permute-start | bytes 491528 | tf_op jit(solution)/shard_map/ppermute | solution.py:215
  82.2 18.5 %collective-permute-start.13 = (bf16[10,64,128]{2,1,0:T(8,128)(2,1)S(1)}, bf16[10,64,128]{2,1,0:T(8,128)(2,1)S(1)}, u32[]{:S(2)}, u32[]{:S(2)}) collective-permute-start(bf16[10,64,128]{2,1,0:T(8,128)(2,1)S(1)} %pad_maximum_fusion.refs_1_), channel_id=1, source_target_pairs={{0,8},{4,12},{8,0},{12,4},{1,9},{5,13},{9,1},{13,5},{2,10},{6,14},... | collective-permute-start | bytes 491528 | tf_op jit(solution)/shard_map/ppermute | solution.py:215
  83.5 17.2 %collective-permute-start.12 = (bf16[10,64,128]{2,1,0:T(8,128)(2,1)S(1)}, bf16[10,64,128]{2,1,0:T(8,128)(2,1)S(1)}, u32[]{:S(2)}, u32[]{:S(2)}) collective-permute-start(bf16[10,64,128]{2,1,0:T(8,128)(2,1)S(1)} %pad_maximum_fusion.refs_1_), channel_id=1, source_target_pairs={{0,4},{4,0},{8,12},{12,8},{1,5},{5,1},{9,13},{13,9},{2,6},{6,2},{1... | collective-permute-start | bytes 491528 | tf_op jit(solution)/shard_map/ppermute | solution.py:215
  100.7 0.7 copy-start.2
  100.7 0.7 copy-start.3
  101.4 0.7 copy-start.4
  104.2 4.5 %collective-permute-start.15 = (bf16[256,4096]{1,0:T(8,128)(2,1)}, bf16[256,4096]{1,0:T(8,128)(2,1)}, u32[]{:S(2)}, u32[]{:S(2)}) collective-permute-start(bf16[256,4096]{1,0:T(8,128)(2,1)} %get-tuple-element.78), channel_id=1, source_target_pairs={{0,4},{4,0},{8,12},{12,8},{1,5},{5,1},{9,13},{13,9},{2,6},{6,2},{1... | collective-permute-start | bytes 6291464 | tf_op jit(solution)/shard_map/ppermute | solution.py:215
  104.2 31.0 %collective-permute-start.17 = (bf16[256,2048]{1,0:T(8,128)(2,1)}, bf16[256,2048]{1,0:T(8,128)(2,1)}, u32[]{:S(2)}, u32[]{:S(2)}) collective-permute-start(bf16[256,2048]{1,0:T(8,128)(2,1)} %get-tuple-element.81.refs_3_), channel_id=1, source_target_pairs={{0,1},{1,0},{2,3},{3,2},{4,5},{5,4},{6,7},{7,6},{8,9},{9,8},{10,11... | collective-permute-start | bytes 3145736 | tf_op jit(solution)/shard_map/ppermute | solution.py:202
  108.7 26.5 %collective-permute-start.16 = (bf16[256,2048]{1,0:T(8,128)(2,1)}, bf16[256,2048]{1,0:T(8,128)(2,1)}, u32[]{:S(2)}, u32[]{:S(2)}) collective-permute-start(bf16[256,2048]{1,0:T(8,128)(2,1)} %sums_now.1), channel_id=1, source_target_pairs={{0,4},{1,2},{2,1},{3,7},{4,0},{5,6},{6,5},{7,3},{8,12},{9,10},{10,... | collective-permute-start | bytes 3145736 | tf_op jit(solution)/shard_map/ppermute | solution.py:211
  114.0 50.7 %collective-permute-start.20 = (bf16[256,4096]{1,0:T(8,128)(2,1)}, bf16[256,4096]{1,0:T(8,128)(2,1)}, u32[]{:S(2)}, u32[]{:S(2)}) collective-permute-start(bf16[256,4096]{1,0:T(8,128)(2,1)} %sums_others.1.refs_11_), channel_id=1, source_target_pairs={{0,8},{4,12},{8,0},{12,4},{1,9},{5,13},{9,1},{13,5},{2,10},{6,14},... | collective-permute-start | bytes 6291464 | tf_op jit(solution)/shard_map/ppermute | solution.py:215
  139.2 25.4 %collective-permute-start.18 = (bf16[256,2048]{1,0:T(8,128)(2,1)}, bf16[256,2048]{1,0:T(8,128)(2,1)}, u32[]{:S(2)}, u32[]{:S(2)}) collective-permute-start(bf16[256,2048]{1,0:T(8,128)(2,1)} %get-tuple-element.89), channel_id=1, source_target_pairs={{0,1},{1,0},{2,3},{3,2},{4,5},{5,4},{6,7},{7,6},{8,9},{9,8},{10,11... | collective-permute-start | bytes 3145736 | tf_op jit(solution)/shard_map/ppermute | solution.py:202
  141.2 23.4 %collective-permute-start.19 = (bf16[256,2048]{1,0:T(8,128)(2,1)}, bf16[256,2048]{1,0:T(8,128)(2,1)}, u32[]{:S(2)}, u32[]{:S(2)}) collective-permute-start(bf16[256,2048]{1,0:T(8,128)(2,1)} %get-tuple-element.90), channel_id=1, source_target_pairs={{0,4},{1,2},{2,1},{3,7},{4,0},{5,6},{6,5},{7,3},{8,12},{9,10},{10,... | collective-permute-start | bytes 3145736 | tf_op jit(solution)/shard_map/ppermute | solution.py:211

commit v6 on v4

--- a/solution.py
+++ b/solution.py
@@ -262,7 +262,7 @@
                 square = jnp.sum(
                     jnp.where(lane // SEQ == side, sums, 0.0), axis=1, keepdims=True
                 )
-                factor = jnp.minimum(1.0, clip / jnp.sqrt(square + 1e-06))
+                factor = jnp.minimum(1.0, clip / jnp.sqrt(jnp.maximum(square, 0.0) + 1e-06))
                 start = pl.multiple_of(block * r + (2 * p + side) * SEQ, SEQ)
                 out[pl.ds(start, SEQ), :] = jnp.broadcast_to(factor, (SEQ, 1))
 
@@ -468,7 +468,8 @@
         tiled=True,
     )
     grams = lax.psum(gram(x), "mp") * lax.psum(gram(g), "hidden")
-    factor = jnp.minimum(1.0, clip / jnp.sqrt(jnp.sum(grams, axis=(1, 2)) + 1e-06))
+    squares = jnp.maximum(jnp.sum(grams, axis=(1, 2)), 0.0)
+    factor = jnp.minimum(1.0, clip / jnp.sqrt(squares + 1e-06))
     none = lambda at, j: 0
     update = make_update(
         jnp.zeros((1,), jnp.int32),

time: 172 us -> 172 us (level)
  no operation moved by 1% of the time
where the time goes in v6:
time: 172 us; the launch traced here: 171 us
  Pallas kernels  135 us (78%)
  starting transfers between devices  25.6 us (15%)
  waiting for transfers between devices  7.49 us (4%)
    pallas_call x5, Pallas kernels, pair_matmul(): pl.pallas_call(kernel, grid=(steps,), in_specs=[pl.BlockSpec(memory_space...  69 us
    pallas_call x2, Pallas kernels, make_update(): pl.pallas_call(kernel, grid=(depth // tile,), in_specs=[pl.BlockSpec(memo...  39.4 us
    pallas_call x5, Pallas kernels, add_up(): pl.pallas_call(lambda *refs: add_kernel(sums, len(arrays) + len(chosen),...  21.3 us
    ppermute x8, starting transfers between devices, along(): return lax.ppermute(value, 'hidden', pairs)  19.4 us
    ppermute x8, waiting for transfers between devices, along(): return lax.ppermute(value, 'hidden', pairs)  6.04 us
    ppermute x9, starting transfers between devices, swap(): return lax.ppermute(value, 'mp', [(i, i ^ bit) for i in range(4)])  5.94 us
    pallas_call x1, Pallas kernels, gram_pairs(): pl.pallas_call(gram_kernel, in_specs=[pl.BlockSpec(memory_space=pltpu.VME...  3.57 us
  transfers between devices with their start and end apart: 21, of which 5 were waited for; matrix products, arithmetic and copies ran while one was open for 0% of the time, Pallas kernels for 77%

profile of v6, /device:TPU:0, one launch (start us, length us, event | category | flops | bytes accessed | tf_op | source)
XLA Modules:
  0.0 171.3 jit_solution(11823092145101290265)
XLA Ops:
  0.6 0.5 collective-permute-start.4
  1.1 0.1 collective-permute-start.2
  1.2 4.1 %collective-permute-start.1 = (bf16[256,2048]{1,0:T(8,128)(2,1)}, bf16[256,2048]{1,0:T(8,128)(2,1)}, u32[]{:S(2)}, u32[]{:S(2)}) collective-permute-start(bf16[256,2048]{1,0:T(8,128)(2,1)} %refs_2_.3), channel_id=1, source_target_pairs={{0,1},{1,0},{2,3},{3,2},{4,5},{5,4},{6,7},{7,6},{8,9},{9,8},{10,11... | collective-permute-start | bytes 3145736 | tf_op jit(solution)/shard_map/ppermute | solution.py:202
  5.4 1.5 collective-permute-start
  6.9 3.6 %gram.1.refs_4_.refs_7_ = bf16[4,64,128]{2,1,0:T(8,128)(2,1)} custom-call(bf16[256,2048]{1,0:T(8,128)(2,1)} %refs_2_.3, bf16[256,4096]{1,0:T(8,128)(2,1)} %refs_6_.3), custom_call_target="tpu_custom_call" | custom-call | flops 1 | bytes 1 | tf_op jit(solution)/shard_map/gram/pallas_call | solution.py:238
  10.4 0.0 collective-permute-start.3
  10.4 0.6 pad_add_fusion.refs_0_
  11.0 0.0 collective-permute-done.4.refs_2_.refs_7_
  11.0 18.3 %in_grad_here.2 = (bf16[256,2048]{1,0:T(8,128)(2,1)}, bf16[256,2048]{1,0:T(8,128)(2,1)}, bf16[2048,4096]{1,0:T(8,128)(2,1)}) custom-call(s32[4]{0:T(128)} %pad_add_fusion.refs_0_, bf16[256,4096]{1,0:T(8,128)(2,1)} %refs_6_.3, bf16[256,4096]{1,0:T(8,128)(2,1)} %collective-permute-done.4.refs_2_.refs_7_, f32[2048,4096]{1,0:T(8,128)} %refs_3_.1, ...), custom_call_target="tpu_custom_call" | custom-call | flops 1 | bytes 1 | tf_op jit(solution)/shard_map/in_grad_here/pallas_call | solution.py:81
  29.3 1.2 collective-permute-done.3
  30.5 0.0 collective-permute-done.2.refs_1_
  30.5 0.0 collective-permute-done.1.refs_2_.refs_3_
  30.5 1.7 collective-permute-start.6
  32.2 0.0 collective-permute-start.5
  32.2 7.9 %in_grad_here.3 = (bf16[256,2048]{1,0:T(8,128)(2,1)}, bf16[256,2048]{1,0:T(8,128)(2,1)}, bf16[2048,4096]{1,0:T(8,128)(2,1)}) custom-call(s32[4]{0:T(128)} %pad_add_fusion.refs_0_, bf16[256,4096]{1,0:T(8,128)(2,1)} %refs_6_.3, bf16[256,4096]{1,0:T(8,128)(2,1)} %collective-permute-done.4.refs_2_.refs_7_, ...), custom_call_target="tpu_custom_call", output_to_operand_aliasing={{0}: (4, {}), {1}: (5, {}), {2}: (6, {})} | custom-call | flops 1 | bytes 1 | tf_op jit(solution)/shard_map/in_grad_here/pallas_call | solution.py:81
  40.1 13.5 %outputs_near.1 = (bf16[256,4096]{1,0:T(8,128)(2,1)}, bf16[256,4096]{1,0:T(8,128)(2,1)}) custom-call(s32[4]{0:T(128)} %pad_add_fusion.refs_0_, bf16[256,2048]{1,0:T(8,128)(2,1)} %refs_2_.3, bf16[256,2048]{1,0:T(8,128)(2,1)} %collective-permute-done.1.refs_2_.refs_3_, bf16[2048,4096]{1,0:T(8,128)(2,1)} %get-tuple-element.60.refs_3_.refs_5_), custom_call_target="tpu_custom_call" | custom-call | flops 1 | bytes 1 | tf_op jit(solution)/shard_map/outputs_near/pallas_call | solution.py:81
  53.6 0.0 collective-permute-done.refs_1_.refs_8_
  53.6 2.1 %collective-permute-done.6.refs_2_ = bf16[256,2048]{1,0:T(8,128)(2,1)} collective-permute-done((bf16[256,2048]{1,0:T(8,128)(2,1)}, bf16[256,2048]{1,0:T(8,128)(2,1)}, u32[]{:S(2)}, u32[]{:S(2)}) %collective-permute-start.6) | collective-permute-done | bytes 1048608 | tf_op jit(solution)/shard_map/ppermute | solution.py:202
  55.7 0.0 collective-permute-done.5.refs_3_
  55.7 0.0 collective-permute-start.7
  55.7 0.5 collective-permute-start.9
  56.2 0.0 copy-done
  56.2 2.4 %collective-permute-start.8 = (bf16[6,64,128]{2,1,0:T(8,128)(2,1)S(1)}, bf16[6,64,128]{2,1,0:T(8,128)(2,1)S(1)}, u32[]{:S(2)}, u32[]{:S(2)}) collective-permute-start(bf16[6,64,128]{2,1,0:T(8,128)(2,1)S(1)} %pad_maximum_fusion.1), channel_id=1, source_target_pairs={{0,2},{1,3},{2,0},{3,1},{4,6},{5,7},{6,4},{7,5},{8,10},{9,11},{10,... | collective-permute-start | bytes 294920 | tf_op jit(solution)/shard_map/ppermute | solution.py:202
  58.7 1.3 collective-permute-start.11
  60.0 0.2 collective-permute-done.7.refs_2_.refs_9_
  60.2 15.2 %in_grad_there.1 = (bf16[256,2048]{1,0:T(8,128)(2,1)}, bf16[256,2048]{1,0:T(8,128)(2,1)}, bf16[256,2048]{1,0:T(8,128)(2,1)}, bf16[256,2048]{1,0:T(8,128)(2,1)}) custom-call(s32[4]{0:T(128)} %pad_add_fusion.refs_0_, bf16[256,4096]{1,0:T(8,128)(2,1)} %collective-permute-done.refs_1_.refs_8_, bf16[256,4096]{1,0:T(8,128)(2,1)} %collective-permute-done.7.refs_2_.refs_9_, ...), custom_call_target="tpu_custom_call" | custom-call | flops 1 | bytes 1 | tf_op jit(solution)/shard_map/in_grad_there/pallas_call | solution.py:81
  75.3 0.0 collective-permute-done.8
  75.4 0.0 collective-permute-done.9.refs_2_.refs_3_
  75.4 6.4 %collective-permute-start.10 = (bf16[256,2048]{1,0:T(8,128)(2,1)}, bf16[256,2048]{1,0:T(8,128)(2,1)}, u32[]{:S(2)}, u32[]{:S(2)}) collective-permute-start(bf16[256,2048]{1,0:T(8,128)(2,1)} %get-tuple-element.72.refs_6_.refs_1_), channel_id=1, source_target_pairs={{0,1},{3,2},{4,5},{7,6},{8,9},{11,10},{12,13},{15,14},{16,17},{19,... | collective-permute-start | bytes 3145736 | tf_op jit(solution)/shard_map/ppermute | solution.py:202
  81.8 0.0 copy-start.1
  81.8 0.3 collective-permute-start.14
  82.2 1.3 collective-permute-start.13
  83.5 0.3 collective-permute-start.12
  83.8 2.7 %collective-permute-done.11.refs_4_ = bf16[256,2048]{1,0:T(8,128)(2,1)} collective-permute-done((bf16[256,2048]{1,0:T(8,128)(2,1)}, bf16[256,2048]{1,0:T(8,128)(2,1)}, u32[]{:S(2)}, u32[]{:S(2)}) %collective-permute-start.11) | collective-permute-done | bytes 1048608 | tf_op jit(solution)/shard_map/ppermute | solution.py:202
  86.5 14.2 %outputs_far.1 = (bf16[256,4096]{1,0:T(8,128)(2,1)}, bf16[256,4096]{1,0:T(8,128)(2,1)}, bf16[2,256,2048]{2,1,0:T(8,128)(2,1)}) custom-call(s32[4]{0:T(128)} %pad_add_fusion.refs_0_, bf16[256,2048]{1,0:T(8,128)(2,1)} %collective-permute-done.2.refs_1_, bf16[256,2048]{1,0:T(8,128)(2,1)} %collective-permute-done.6.refs_2_, ...), custom_call_target="tpu_custom_call" | custom-call | flops 1 | bytes 1 | tf_op jit(solution)/shard_map/outputs_far/pallas_call | solution.py:81
  100.7 0.0 copy-done.1
  100.7 0.0 collective-permute-done.14.refs_4_
  100.7 0.0 copy-start.2
  100.7 0.0 collective-permute-done.13.refs_3_
  100.7 0.0 collective-permute-done.12.refs_2_
  100.7 0.6 copy-done.2
  101.4 0.1 copy-done.3
  101.4 0.7 copy-done.4
  102.1 2.1 %clip_factor.1.refs_1_ = f32[1024,1]{1,0:T(8,128)} custom-call(s32[4]{0:T(128)} %pad_add_fusion.refs_0_, bf16[10,64,128]{2,1,0:T(8,128)(2,1)} %copy-done.1, bf16[10,64,128]{2,1,0:T(8,128)(2,1)} %copy-done.4, bf16[10,64,128]{2,1,0:T(8,128)(2,1)} %copy-done.3, bf16[10,64,128]{2,1,0:T(8,128)(2,1)} %copy-done.2), custom_call_target="tpu_custom_call" | custom-call | flops 1 | bytes 1 | tf_op jit(solution)/shard_map/clip_factor/pallas_call | solution.py:271
  104.2 0.0 collective-permute-done.10.refs_2_
  104.2 0.0 collective-permute-start.15
  104.2 1.4 collective-permute-start.17
  105.6 3.1 %sums_now.1 = bf16[256,2048]{1,0:T(8,128)(2,1)} custom-call(s32[4]{0:T(128)} %pad_add_fusion.refs_0_, bf16[256,2048]{1,0:T(8,128)(2,1)} %get-tuple-element.72.refs_6_.refs_1_, bf16[256,2048]{1,0:T(8,128)(2,1)} %collective-permute-done.10.refs_2_), custom_call_target="tpu_custom_call" | custom-call | flops 1 | bytes 1 | tf_op jit(solution)/shard_map/sums_now/pallas_call | solution.py:177
  108.7 0.0 collective-permute-done.15.refs_4_.refs_5_
  108.7 0.2 collective-permute-start.16
  109.0 5.0 %sums_others.1.refs_11_ = bf16[256,4096]{1,0:T(8,128)(2,1)} custom-call(s32[4]{0:T(128)} %pad_add_fusion.refs_0_, bf16[256,4096]{1,0:T(8,128)(2,1)} %get-tuple-element.67.refs_6_.refs_1_.refs_2_, bf16[256,4096]{1,0:T(8,128)(2,1)} %collective-permute-done.9.refs_2_.refs_3_, bf16[256,4096]{1,0:T(8,128)(2,1)} %get-tuple-element.84.refs_3_.refs_4_, ...), custom_call_target="tpu_custom_call" | custom-call | flops 1 | bytes 1 | tf_op jit(solution)/shard_map/sums_others/pallas_call | solution.py:177
  113.9 1.5 collective-permute-start.20
  115.4 19.7 %update.2.refs_11_ = f32[2048,4096]{1,0:T(8,128)} custom-call(s32[4]{0:T(128)} %pad_add_fusion.refs_0_, f32[1024,1]{1,0:T(8,128)} %clip_factor.1.refs_1_, bf16[256,2048]{1,0:T(8,128)(2,1)} %refs_2_.3, bf16[256,2048]{1,0:T(8,128)(2,1)} %collective-permute-done.1.refs_2_.refs_3_, bf16[2,256,2048]{2,1,0:T(8,128)(2,1)} %get-tuple-element.82.refs_4_.refs_5_, ...), custom_call_target="tpu_custom_call" | custom-call | flops 1 | bytes 1 | tf_op jit(solution)/shard_map/update/pallas_call | solution.py:147
  135.1 0.0 collective-permute-done.17.refs_4_
  135.1 0.0 collective-permute-done.16.refs_2_
  135.2 4.0 %sums_later.1 = (bf16[256,2048]{1,0:T(8,128)(2,1)}, bf16[256,2048]{1,0:T(8,128)(2,1)}) custom-call(s32[4]{0:T(128)} %pad_add_fusion.refs_0_, bf16[256,2048]{1,0:T(8,128)(2,1)} %get-tuple-element.68.refs_1_, bf16[256,2048]{1,0:T(8,128)(2,1)} %collective-permute-done.16.refs_2_, bf16[256,2048]{1,0:T(8,128)(2,1)} %get-tuple-element.80.refs_3_, ...), custom_call_target="tpu_custom_call" | custom-call | flops 1 | bytes 1 | tf_op jit(solution)/shard_map/sums_later/pallas_call | solution.py:177
  139.1 2.0 %collective-permute-start.18 = (bf16[256,2048]{1,0:T(8,128)(2,1)}, bf16[256,2048]{1,0:T(8,128)(2,1)}, u32[]{:S(2)}, u32[]{:S(2)}) collective-permute-start(bf16[256,2048]{1,0:T(8,128)(2,1)} %get-tuple-element.88), channel_id=1, source_target_pairs={{0,1},{1,0},{2,3},{3,2},{4,5},{5,4},{6,7},{7,6},{8,9},{9,8},{10,11... | collective-permute-start | bytes 3145736 | tf_op jit(solution)/shard_map/ppermute | solution.py:202
  141.1 0.0 collective-permute-start.19
  141.1 19.7 %update.3 = f32[2048,4096]{1,0:T(8,128)} custom-call(s32[4]{0:T(128)} %pad_add_fusion.refs_0_, f32[1024,1]{1,0:T(8,128)} %clip_factor.1.refs_1_, bf16[256,2048]{1,0:T(8,128)(2,1)} %refs_2_.3, bf16[256,2048]{1,0:T(8,128)(2,1)} %collective-permute-done.1.refs_2_.refs_3_, ...), custom_call_target="tpu_custom_call", output_to_operand_aliasing={{}: (11, {})} | custom-call | flops 1 | bytes 1 | tf_op jit(solution)/shard_map/update/pallas_call | solution.py:147
  160.9 1.2 collective-permute-done.20.refs_1_
  162.1 5.7 %sums_outputs.1 = bf16[256,4096]{1,0:T(8,128)(2,1)} custom-call(s32[4]{0:T(128)} %pad_add_fusion.refs_0_, bf16[256,4096]{1,0:T(8,128)(2,1)} %collective-permute-done.20.refs_1_, bf16[256,4096]{1,0:T(8,128)(2,1)} %get-tuple-element.67.refs_6_.refs_1_.refs_2_, bf16[256,4096]{1,0:T(8,128)(2,1)} %collective-permute-done.9.refs_2_.refs_3_, ...), custom_call_target="tpu_custom_call" | custom-call | flops 1 | bytes 1 | tf_op jit(solution)/shard_map/sums_outputs/pallas_call | solution.py:177
  167.8 0.0 collective-permute-done.18.refs_2_
  167.8 0.0 collective-permute-done.19.refs_3_
  167.8 3.5 %sums_in_grad.1 = bf16[256,2048]{1,0:T(8,128)(2,1)} custom-call(s32[4]{0:T(128)} %pad_add_fusion.refs_0_, bf16[256,2048]{1,0:T(8,128)(2,1)} %get-tuple-element.93.refs_1_, bf16[256,2048]{1,0:T(8,128)(2,1)} %collective-permute-done.18.refs_2_, bf16[256,2048]{1,0:T(8,128)(2,1)} %collective-permute-done.19.refs_3_), custom_call_target="tpu_custom_call" | custom-call | flops 1 | bytes 1 | tf_op jit(solution)/shard_map/sums_in_grad/pallas_call | solution.py:177
  (10 shorter events, 0.1 us)
Async XLA Ops:
  0.6 10.4 %collective-permute-start.4 = (bf16[256,4096]{1,0:T(8,128)(2,1)}, bf16[256,4096]{1,0:T(8,128)(2,1)}, u32[]{:S(2)}, u32[]{:S(2)}) collective-permute-start(bf16[256,4096]{1,0:T(8,128)(2,1)} %refs_6_.3), channel_id=1, source_target_pairs={{0,4},{4,0},{8,12},{12,8},{1,5},{5,1},{9,13},{13,9},{2,6},{6,2},{1... | collective-permute-start | bytes 6291464 | tf_op jit(solution)/shard_map/ppermute | solution.py:215
  1.1 29.4 %collective-permute-start.2 = (bf16[256,2048]{1,0:T(8,128)(2,1)}, bf16[256,2048]{1,0:T(8,128)(2,1)}, u32[]{:S(2)}, u32[]{:S(2)}) collective-permute-start(bf16[256,2048]{1,0:T(8,128)(2,1)} %refs_2_.3), channel_id=1, source_target_pairs={{0,4},{1,2},{2,1},{3,7},{4,0},{5,6},{6,5},{7,3},{8,12},{9,10},{10,... | collective-permute-start | bytes 3145736 | tf_op jit(solution)/shard_map/ppermute | solution.py:211
  1.2 29.3 %collective-permute-start.1 = (bf16[256,2048]{1,0:T(8,128)(2,1)}, bf16[256,2048]{1,0:T(8,128)(2,1)}, u32[]{:S(2)}, u32[]{:S(2)}) collective-permute-start(bf16[256,2048]{1,0:T(8,128)(2,1)} %refs_2_.3), channel_id=1, source_target_pairs={{0,1},{1,0},{2,3},{3,2},{4,5},{5,4},{6,7},{7,6},{8,9},{9,8},{10,11... | collective-permute-start | bytes 3145736 | tf_op jit(solution)/shard_map/ppermute | solution.py:202
  5.4 48.2 %collective-permute-start = (bf16[256,4096]{1,0:T(8,128)(2,1)}, bf16[256,4096]{1,0:T(8,128)(2,1)}, u32[]{:S(2)}, u32[]{:S(2)}) collective-permute-start(bf16[256,4096]{1,0:T(8,128)(2,1)} %refs_6_.3), channel_id=1, source_target_pairs={{0,8},{4,12},{8,0},{12,4},{1,9},{5,13},{9,1},{13,5},{2,10},{6,14},... | collective-permute-start | bytes 6291464 | tf_op jit(solution)/shard_map/ppermute | solution.py:215
  10.4 20.1 %collective-permute-start.3 = (bf16[4,64,128]{2,1,0:T(8,128)(2,1)}, bf16[4,64,128]{2,1,0:T(8,128)(2,1)S(1)}, u32[]{:S(2)}, u32[]{:S(2)}) collective-permute-start(bf16[4,64,128]{2,1,0:T(8,128)(2,1)} %gram.1.refs_4_.refs_7_), channel_id=1, source_target_pairs={{0,1},{1,0},{2,3},{3,2},{4,5},{5,4},{6,7},{7,6},{8,9},{9,8},{10,11... | collective-permute-start | bytes 196616 | tf_op jit(solution)/shard_map/ppermute | solution.py:202
  30.5 25.1 %collective-permute-start.6 = (bf16[256,2048]{1,0:T(8,128)(2,1)}, bf16[256,2048]{1,0:T(8,128)(2,1)}, u32[]{:S(2)}, u32[]{:S(2)}) collective-permute-start(bf16[256,2048]{1,0:T(8,128)(2,1)} %collective-permute-done.2.refs_1_), channel_id=1, source_target_pairs={{0,1},{1,0},{2,3},{3,2},{4,5},{5,4},{6,7},{7,6},{8,9},{9,8},{10,11... | collective-permute-start | bytes 3145736 | tf_op jit(solution)/shard_map/ppermute | solution.py:202
  32.2 23.4 %collective-permute-start.5 = (bf16[256,2048]{1,0:T(8,128)(2,1)}, bf16[256,2048]{1,0:T(8,128)(2,1)}, u32[]{:S(2)}, u32[]{:S(2)}) collective-permute-start(bf16[256,2048]{1,0:T(8,128)(2,1)} %collective-permute-done.1.refs_2_.refs_3_), channel_id=1, source_target_pairs={{0,4},{1,2},{2,1},{3,7},{4,0},{5,6},{6,5},{7,3},{8,12},{9,10},{10,... | collective-permute-start | bytes 3145736 | tf_op jit(solution)/shard_map/ppermute | solution.py:211
  40.1 16.1 %copy-start = (bf16[4,64,128]{2,1,0:T(8,128)(2,1)S(1)}, bf16[4,64,128]{2,1,0:T(8,128)(2,1)}, u32[]{:S(2)}) copy-start(bf16[4,64,128]{2,1,0:T(8,128)(2,1)} %gram.1.refs_4_.refs_7_) | copy-start | bytes 196612
  55.7 4.5 %collective-permute-start.7 = (bf16[256,4096]{1,0:T(8,128)(2,1)}, bf16[256,4096]{1,0:T(8,128)(2,1)}, u32[]{:S(2)}, u32[]{:S(2)}) collective-permute-start(bf16[256,4096]{1,0:T(8,128)(2,1)} %collective-permute-done.refs_1_.refs_8_), channel_id=1, source_target_pairs={{0,4},{4,0},{8,12},{12,8},{1,5},{5,1},{9,13},{13,9},{2,6},{6,2},{1... | collective-permute-start | bytes 6291464 | tf_op jit(solution)/shard_map/ppermute | solution.py:215
  55.7 19.7 %collective-permute-start.9 = (bf16[256,4096]{1,0:T(8,128)(2,1)}, bf16[256,4096]{1,0:T(8,128)(2,1)}, u32[]{:S(2)}, u32[]{:S(2)}) collective-permute-start(bf16[256,4096]{1,0:T(8,128)(2,1)} %get-tuple-element.71), channel_id=1, source_target_pairs={{0,4},{4,0},{8,12},{12,8},{1,5},{5,1},{9,13},{13,9},{2,6},{6,2},{1... | collective-permute-start | bytes 6291464 | tf_op jit(solution)/shard_map/ppermute | solution.py:215
  56.2 19.1 %collective-permute-start.8 = (bf16[6,64,128]{2,1,0:T(8,128)(2,1)S(1)}, bf16[6,64,128]{2,1,0:T(8,128)(2,1)S(1)}, u32[]{:S(2)}, u32[]{:S(2)}) collective-permute-start(bf16[6,64,128]{2,1,0:T(8,128)(2,1)S(1)} %pad_maximum_fusion.1), channel_id=1, source_target_pairs={{0,2},{1,3},{2,0},{3,1},{4,6},{5,7},{6,4},{7,5},{8,10},{9,11},{10,... | collective-permute-start | bytes 294920 | tf_op jit(solution)/shard_map/ppermute | solution.py:202
  58.7 27.8 %collective-permute-start.11 = (bf16[256,2048]{1,0:T(8,128)(2,1)}, bf16[256,2048]{1,0:T(8,128)(2,1)}, u32[]{:S(2)}, u32[]{:S(2)}) collective-permute-start(bf16[256,2048]{1,0:T(8,128)(2,1)} %collective-permute-done.5.refs_3_), channel_id=1, source_target_pairs={{1,0},{2,3},{5,4},{6,7},{9,8},{10,11},{13,12},{14,15},{17,16},{18,... | collective-permute-start | bytes 3145736 | tf_op jit(solution)/shard_map/ppermute | solution.py:202
  75.4 28.9 %collective-permute-start.10 = (bf16[256,2048]{1,0:T(8,128)(2,1)}, bf16[256,2048]{1,0:T(8,128)(2,1)}, u32[]{:S(2)}, u32[]{:S(2)}) collective-permute-start(bf16[256,2048]{1,0:T(8,128)(2,1)} %get-tuple-element.72.refs_6_.refs_1_), channel_id=1, source_target_pairs={{0,1},{3,2},{4,5},{7,6},{8,9},{11,10},{12,13},{15,14},{16,17},{19,... | collective-permute-start | bytes 3145736 | tf_op jit(solution)/shard_map/ppermute | solution.py:202
  81.8 18.9 %copy-start.1 = (bf16[10,64,128]{2,1,0:T(8,128)(2,1)}, bf16[10,64,128]{2,1,0:T(8,128)(2,1)S(1)}, u32[]{:S(2)}) copy-start(bf16[10,64,128]{2,1,0:T(8,128)(2,1)S(1)} %pad_maximum_fusion.refs_1_) | copy-start | bytes 491524
  81.8 18.9 %collective-permute-start.14 = (bf16[10,64,128]{2,1,0:T(8,128)(2,1)S(1)}, bf16[10,64,128]{2,1,0:T(8,128)(2,1)S(1)}, u32[]{:S(2)}, u32[]{:S(2)}) collective-permute-start(bf16[10,64,128]{2,1,0:T(8,128)(2,1)S(1)} %pad_maximum_fusion.refs_1_), channel_id=1, source_target_pairs={{0,12},{4,8},{8,4},{12,0},{1,13},{5,9},{9,5},{13,1},{2,14},{6,10},... | collective-permute-start | bytes 491528 | tf_op jit(solution)/shard_map/ppermute | solution.py:215
  82.2 18.5 %collective-permute-start.13 = (bf16[10,64,128]{2,1,0:T(8,128)(2,1)S(1)}, bf16[10,64,128]{2,1,0:T(8,128)(2,1)S(1)}, u32[]{:S(2)}, u32[]{:S(2)}) collective-permute-start(bf16[10,64,128]{2,1,0:T(8,128)(2,1)S(1)} %pad_maximum_fusion.refs_1_), channel_id=1, source_target_pairs={{0,8},{4,12},{8,0},{12,4},{1,9},{5,13},{9,1},{13,5},{2,10},{6,14},... | collective-permute-start | bytes 491528 | tf_op jit(solution)/shard_map/ppermute | solution.py:215
  83.5 17.3 %collective-permute-start.12 = (bf16[10,64,128]{2,1,0:T(8,128)(2,1)S(1)}, bf16[10,64,128]{2,1,0:T(8,128)(2,1)S(1)}, u32[]{:S(2)}, u32[]{:S(2)}) collective-permute-start(bf16[10,64,128]{2,1,0:T(8,128)(2,1)S(1)} %pad_maximum_fusion.refs_1_), channel_id=1, source_target_pairs={{0,4},{4,0},{8,12},{12,8},{1,5},{5,1},{9,13},{13,9},{2,6},{6,2},{1... | collective-permute-start | bytes 491528 | tf_op jit(solution)/shard_map/ppermute | solution.py:215
  100.7 0.7 copy-start.2
  100.7 0.7 copy-start.3
  101.4 0.7 copy-start.4
  104.2 4.5 %collective-permute-start.15 = (bf16[256,4096]{1,0:T(8,128)(2,1)}, bf16[256,4096]{1,0:T(8,128)(2,1)}, u32[]{:S(2)}, u32[]{:S(2)}) collective-permute-start(bf16[256,4096]{1,0:T(8,128)(2,1)} %get-tuple-element.77), channel_id=1, source_target_pairs={{0,4},{4,0},{8,12},{12,8},{1,5},{5,1},{9,13},{13,9},{2,6},{6,2},{1... | collective-permute-start | bytes 6291464 | tf_op jit(solution)/shard_map/ppermute | solution.py:215
  104.2 30.9 %collective-permute-start.17 = (bf16[256,2048]{1,0:T(8,128)(2,1)}, bf16[256,2048]{1,0:T(8,128)(2,1)}, u32[]{:S(2)}, u32[]{:S(2)}) collective-permute-start(bf16[256,2048]{1,0:T(8,128)(2,1)} %get-tuple-element.80.refs_3_), channel_id=1, source_target_pairs={{0,1},{1,0},{2,3},{3,2},{4,5},{5,4},{6,7},{7,6},{8,9},{9,8},{10,11... | collective-permute-start | bytes 3145736 | tf_op jit(solution)/shard_map/ppermute | solution.py:202
  108.7 26.4 %collective-permute-start.16 = (bf16[256,2048]{1,0:T(8,128)(2,1)}, bf16[256,2048]{1,0:T(8,128)(2,1)}, u32[]{:S(2)}, u32[]{:S(2)}) collective-permute-start(bf16[256,2048]{1,0:T(8,128)(2,1)} %sums_now.1), channel_id=1, source_target_pairs={{0,4},{1,2},{2,1},{3,7},{4,0},{5,6},{6,5},{7,3},{8,12},{9,10},{10,... | collective-permute-start | bytes 3145736 | tf_op jit(solution)/shard_map/ppermute | solution.py:211
  113.9 48.1 %collective-permute-start.20 = (bf16[256,4096]{1,0:T(8,128)(2,1)}, bf16[256,4096]{1,0:T(8,128)(2,1)}, u32[]{:S(2)}, u32[]{:S(2)}) collective-permute-start(bf16[256,4096]{1,0:T(8,128)(2,1)} %sums_others.1.refs_11_), channel_id=1, source_target_pairs={{0,8},{4,12},{8,0},{12,4},{1,9},{5,13},{9,1},{13,5},{2,10},{6,14},... | collective-permute-start | bytes 6291464 | tf_op jit(solution)/shard_map/ppermute | solution.py:215
  139.1 28.6 %collective-permute-start.18 = (bf16[256,2048]{1,0:T(8,128)(2,1)}, bf16[256,2048]{1,0:T(8,128)(2,1)}, u32[]{:S(2)}, u32[]{:S(2)}) collective-permute-start(bf16[256,2048]{1,0:T(8,128)(2,1)} %get-tuple-element.88), channel_id=1, source_target_pairs={{0,1},{1,0},{2,3},{3,2},{4,5},{5,4},{6,7},{7,6},{8,9},{9,8},{10,11... | collective-permute-start | bytes 3145736 | tf_op jit(solution)/shard_map/ppermute | solution.py:202
  141.1 26.7 %collective-permute-start.19 = (bf16[256,2048]{1,0:T(8,128)(2,1)}, bf16[256,2048]{1,0:T(8,128)(2,1)}, u32[]{:S(2)}, u32[]{:S(2)}) collective-permute-start(bf16[256,2048]{1,0:T(8,128)(2,1)} %get-tuple-element.89), channel_id=1, source_target_pairs={{0,4},{1,2},{2,1},{3,7},{4,0},{5,6},{6,5},{7,3},{8,12},{9,10},{10,... | collective-permute-start | bytes 3145736 | tf_op jit(solution)/shard_map/ppermute | solution.py:211
